TPU v7x, 32 devices: a whole 2x2x4 slice. The times are simulated.
32 devices in a mesh: dp: 8 (over z, y), heads: 4 (over x, core).
Axes of the slice: x: 2, y: 2, z: 4, core: 2. Of those that a mesh axis runs over, the one named last changes fastest.
Arguments:
- content_in: bfloat16 [12288, 768], P(('dp', 'heads')), may hold values from -6 to 6
- query_in: bfloat16 [12288, 768], P(('dp', 'heads')), may hold values from -6 to 6
- content_grad: bfloat16 [12288, 768], P(('dp', 'heads')), may hold values from -6 to 6
- query_grad: bfloat16 [12288, 768], P(('dp', 'heads')), may hold values from -6 to 6
- segment_ids: int32 [24, 512], P('dp'), may hold values from 0 to 1
- doc_lengths: int32 [24, 8], P('dp'), may hold values from 1 to 256, 512 in all within a row
- factor_order: int32 [24, 512], P('dp'), may hold values from 0 to 511, each once within a row
- attn_proj: float32 [4, 768, 768], P(None, 'dp', 'heads'), may hold values from -0.21875 to 0.21875
- attn_proj_first: float32 [4, 768, 768], P(None, 'dp', 'heads'), may hold values from -0.00061035156 to 0.00061035156
- attn_proj_second: float32 [4, 768, 768], P(None, 'dp', 'heads'), may hold values from 6.511719e-11 to 1.041875e-09
- out_proj: float32 [768, 768], P('heads', 'dp'), may hold values from -0.875 to 0.875
- out_proj_first: float32 [768, 768], P('heads', 'dp'), may hold values from -0.00061035156 to 0.00061035156
- out_proj_second: float32 [768, 768], P('heads', 'dp'), may hold values from 6.511719e-11 to 1.041875e-09
- up_proj: float32 [768, 3072], P('dp', 'heads'), may hold values from -0.21875 to 0.21875
- up_proj_first: float32 [768, 3072], P('dp', 'heads'), may hold values from -0.00061035156 to 0.00061035156
- up_proj_second: float32 [768, 3072], P('dp', 'heads'), may hold values from 6.511719e-11 to 1.041875e-09
- down_proj: float32 [3072, 768], P('heads', 'dp'), may hold values from -0.109375 to 0.109375
- down_proj_first: float32 [3072, 768], P('heads', 'dp'), may hold values from -0.00061035156 to 0.00061035156
- down_proj_second: float32 [3072, 768], P('heads', 'dp'), may hold values from 6.511719e-11 to 1.041875e-09
- head_bias: float32 [5, 12, 64], P(None, 'heads'), may hold values from -3 to 3
- head_bias_first: float32 [5, 12, 64], P(None, 'heads'), may hold values from -0.00061035156 to 0.00061035156
- head_bias_second: float32 [5, 12, 64], P(None, 'heads'), may hold values from 1.3023438e-10 to 5.209375e-10
- up_bias: float32 [3072], P('heads'), may hold values from -3 to 3
- up_bias_first: float32 [3072], P('heads'), may hold values from -0.00036621094 to 0.00036621094
- up_bias_second: float32 [3072], P('heads'), may hold values from 5.2093753e-11 to 2.0837501e-10
- norm_param: float32 [5, 768], replicated, may hold values from -2 to 2
- norm_param_first: float32 [5, 768], replicated, may hold values from -0.0017089844 to 0.0017089844
- norm_param_second: float32 [5, 768], replicated, may hold values from 6.511719e-10 to 1.041875e-08
Outputs:
- content_out: bfloat16 [12288, 768], P(('dp', 'heads'))
- query_out: bfloat16 [12288, 768], P(('dp', 'heads'))
- content_in_grad: float32 [12288, 768], P(('dp', 'heads'))
- query_in_grad: float32 [12288, 768], P(('dp', 'heads'))
- grad_norm: float32 [], replicated
- attn_proj_grad: float32 [4, 768, 768], P(None, 'dp', 'heads')
- attn_proj_first_new: float32 [4, 768, 768], P(None, 'dp', 'heads')
- attn_proj_second_new: float32 [4, 768, 768], P(None, 'dp', 'heads')
- attn_proj_new: float32 [4, 768, 768], P(None, 'dp', 'heads')
- out_proj_grad: float32 [768, 768], P('heads', 'dp')
- out_proj_first_new: float32 [768, 768], P('heads', 'dp')
- out_proj_second_new: float32 [768, 768], P('heads', 'dp')
- out_proj_new: float32 [768, 768], P('heads', 'dp')
- up_proj_grad: float32 [768, 3072], P('dp', 'heads')
- up_proj_first_new: float32 [768, 3072], P('dp', 'heads')
- up_proj_second_new: float32 [768, 3072], P('dp', 'heads')
- up_proj_new: float32 [768, 3072], P('dp', 'heads')
- down_proj_grad: float32 [3072, 768], P('heads', 'dp')
- down_proj_first_new: float32 [3072, 768], P('heads', 'dp')
- down_proj_second_new: float32 [3072, 768], P('heads', 'dp')
- down_proj_new: float32 [3072, 768], P('heads', 'dp')
- head_bias_grad: float32 [5, 12, 64], P(None, 'heads')
- head_bias_first_new: float32 [5, 12, 64], P(None, 'heads')
- head_bias_second_new: float32 [5, 12, 64], P(None, 'heads')
- head_bias_new: float32 [5, 12, 64], P(None, 'heads')
- up_bias_grad: float32 [3072], P('heads')
- up_bias_first_new: float32 [3072], P('heads')
- up_bias_second_new: float32 [3072], P('heads')
- up_bias_new: float32 [3072], P('heads')
- norm_param_grad: float32 [5, 768], replicated
- norm_param_first_new: float32 [5, 768], replicated
- norm_param_second_new: float32 [5, 768], replicated
- norm_param_new: float32 [5, 768], replicated
Inputs may be any that keep to these rules, and one draw needn't show every extreme that they name: `doc_lengths`: each row's 8 lengths sum to 512, and the largest is exactly 256. `factor_order`: each row holds every position of 0 to 511 once.
All inputs are finite; a program needn't handle non-finite values.
Results may differ from a plain program's by a relative error of at most 0.018.
Values may be sent and summed in bfloat16 or wider, within the bound.
A program may use at most 192 MiB of HBM per device.

v0:
```python
import jax
import jax.numpy as jnp
from jax import lax
from jax.sharding import PartitionSpec as P

STEP = 10


HIGH_PRECISION = lax.Precision.HIGHEST
NORM_EPSILON = 1e-05
CLIP_NORM = 1.0
MATRIX_RATE = 0.08
VECTOR_RATE = 0.5
BETA_ONE = 0.9
BETA_TWO = 0.999
ADAM_EPSILON = 1e-08
WEIGHT_DECAY = 0.01
MASKED_SCORE = -1e30


def position_table(length, width):
    distance = (length - jnp.arange(2 * length)).astype(jnp.float32)
    frequency = 1.0 / 10000.0 ** (jnp.arange(0, width, 2).astype(jnp.float32) / width)
    angles = distance[:, None] * frequency[None, :]
    return jnp.concatenate([jnp.sin(angles), jnp.cos(angles)], -1)


def pair_masks(segment, lengths, order):
    length = segment.shape[-1]
    places = jnp.arange(length, dtype=jnp.int32)
    doc_ends = jnp.cumsum(lengths, -1)
    document = jnp.sum((places[:, None] >= doc_ends[None, :]).astype(jnp.int32), -1)
    ranking = jnp.sum(jnp.where(order[:, None] == places[None, :], places[:, None], 0), 0)
    same_doc = document[:, None] == document[None, :]
    allow_content = same_doc & (ranking[None, :] <= ranking[:, None])
    allow_query = same_doc & (ranking[None, :] < ranking[:, None])
    differ = (segment[:, None] != segment[None, :]).astype(jnp.float32)
    return (allow_content, allow_query, differ)


def rel_shift(wide_scores):
    length = wide_scores.shape[-2]
    amount = length - jnp.arange(length, dtype=jnp.int32)
    shifted = wide_scores
    for bit in range(length.bit_length()):
        step = 1 << bit
        filler = jnp.zeros(shifted.shape[:-1] + (step,), shifted.dtype)
        moved = jnp.concatenate([shifted[..., step:], filler], -1)
        chosen = amount >> bit & 1 == 1
        shifted = jnp.where(chosen[:, None], moved, shifted)
    return shifted[..., :length]


def rel_unshift(narrow):
    length = narrow.shape[-1]
    amount = length - jnp.arange(length, dtype=jnp.int32)
    shifted = jnp.concatenate([narrow, jnp.zeros(narrow.shape, narrow.dtype)], -1)
    for bit in range(length.bit_length()):
        step = 1 << bit
        filler = jnp.zeros(shifted.shape[:-1] + (step,), shifted.dtype)
        moved = jnp.concatenate([filler, shifted[..., :-step]], -1)
        chosen = amount >> bit & 1 == 1
        shifted = jnp.where(chosen[:, None], moved, shifted)
    return shifted


def seq_scores(query_now, keys_now, relative, head_bias, differ):
    scale = query_now.shape[-1] ** (-0.5)
    content = jnp.einsum("ihd,jhd->hij", query_now, keys_now, preferred_element_type=jnp.float32)
    content = (
        content
        + jnp.einsum(
            "jhd,hd->hj", keys_now.astype(jnp.float32), head_bias[0], precision=HIGH_PRECISION
        )[:, None, :]
    )
    position = jnp.einsum("ihd,phd->hip", query_now, relative, preferred_element_type=jnp.float32)
    position = (
        position
        + jnp.einsum(
            "phd,hd->hp", relative.astype(jnp.float32), head_bias[1], precision=HIGH_PRECISION
        )[:, None, :]
    )
    segment = jnp.einsum(
        "ihd,shd->hsi",
        query_now.astype(jnp.float32) + head_bias[2],
        head_bias[3:5],
        precision=HIGH_PRECISION,
    )
    seg_term = segment[:, 0, :, None] + differ[None] * (
        segment[:, 1, :, None] - segment[:, 0, :, None]
    )
    return (content + rel_shift(position) + seg_term) * scale


def seq_mix(scores, allowed, values):
    highest = jnp.maximum(jnp.max(jnp.where(allowed, scores, MASKED_SCORE), -1), 0.0)
    weights_exp = jnp.exp(jnp.where(allowed, scores - highest[..., None], MASKED_SCORE))
    totals = jnp.exp(-highest) + jnp.sum(weights_exp, -1)
    chances = (weights_exp / totals[..., None]).astype(jnp.bfloat16)
    mixed = jnp.einsum("hij,jhd->ihd", chances, values, preferred_element_type=jnp.float32)
    return (mixed.astype(jnp.bfloat16), highest + jnp.log(totals))


def seq_mix_back(scores, allowed, logsum, values, upper):
    chances = jnp.exp(jnp.where(allowed, scores - logsum[..., None], MASKED_SCORE))
    dchance = jnp.einsum("ihd,jhd->hij", upper, values, preferred_element_type=jnp.float32)
    dvalues = jnp.einsum(
        "hij,ihd->jhd", chances.astype(jnp.bfloat16), upper, preferred_element_type=jnp.float32
    )
    centre = jnp.sum(chances * dchance, -1, keepdims=True)
    return ((chances * (dchance - centre)).astype(jnp.bfloat16), dvalues)


def seq_scores_back(dscore, query_now, keys_now, relative, head_bias, differ):
    scale = query_now.shape[-1] ** (-0.5)
    dwide = rel_unshift(dscore)
    dscore_wide = dscore.astype(jnp.float32)
    dwide_wide = dwide.astype(jnp.float32)
    key_col = jnp.sum(dscore_wide, 1)
    rel_col = jnp.sum(dwide_wide, 1)
    seg_zero = jnp.sum(dscore_wide * (1.0 - differ)[None], -1)
    seg_one = jnp.sum(dscore_wide * differ[None], -1)
    dquery = (
        jnp.einsum("hij,jhd->ihd", dscore, keys_now, preferred_element_type=jnp.float32)
        + jnp.einsum("hip,phd->ihd", dwide, relative, preferred_element_type=jnp.float32)
        + jnp.einsum("hi,hd->ihd", seg_zero, head_bias[3], precision=HIGH_PRECISION)
        + jnp.einsum("hi,hd->ihd", seg_one, head_bias[4], precision=HIGH_PRECISION)
    )
    dkeys = jnp.einsum(
        "hij,ihd->jhd", dscore, query_now, preferred_element_type=jnp.float32
    ) + jnp.einsum("hj,hd->jhd", key_col, head_bias[0], precision=HIGH_PRECISION)
    drelative = jnp.einsum(
        "hip,ihd->phd", dwide, query_now, preferred_element_type=jnp.float32
    ) + jnp.einsum("hp,hd->phd", rel_col, head_bias[1], precision=HIGH_PRECISION)
    shifted = query_now.astype(jnp.float32) + head_bias[2]
    dheads = jnp.stack(
        [
            jnp.einsum(
                "hj,jhd->hd", key_col, keys_now.astype(jnp.float32), precision=HIGH_PRECISION
            ),
            jnp.einsum(
                "hp,phd->hd", rel_col, relative.astype(jnp.float32), precision=HIGH_PRECISION
            ),
            jnp.sum(seg_zero, 1)[:, None] * head_bias[3]
            + jnp.sum(seg_one, 1)[:, None] * head_bias[4],
            jnp.einsum("hi,ihd->hd", seg_zero, shifted, precision=HIGH_PRECISION),
            jnp.einsum("hi,ihd->hd", seg_one, shifted, precision=HIGH_PRECISION),
        ]
    )
    return (dquery * scale, dkeys * scale, drelative * scale, dheads * scale)


def layer_norm_parts(values, gain_row, bias_row):
    row_mean = jnp.mean(values, -1, keepdims=True)
    centred = values - row_mean
    row_var = jnp.mean(centred * centred, -1, keepdims=True)
    inverse = lax.rsqrt(row_var + NORM_EPSILON)
    normed = centred * inverse
    return (normed * gain_row + bias_row, normed, inverse)


def layer_norm_back(upstream, normed, inverse, gain_row):
    scaled = upstream * gain_row
    first_mean = jnp.mean(scaled, -1, keepdims=True)
    second_mean = jnp.mean(scaled * normed, -1, keepdims=True)
    return inverse * (scaled - first_mean - normed * second_mean)


def gelu_back(before, upstream):
    return jax.vjp(lambda inner: jax.nn.gelu(inner, approximate=True), before)[1](upstream)[0]


def adam_step(master, first, second, gradient, factor, decayed):
    clipped = gradient * factor
    new_first = BETA_ONE * first + (1.0 - BETA_ONE) * clipped
    new_second = BETA_TWO * second + (1.0 - BETA_TWO) * clipped * clipped
    first_hat = new_first / (1.0 - BETA_ONE**STEP)
    second_hat = new_second / (1.0 - BETA_TWO**STEP)
    update = first_hat / (jnp.sqrt(second_hat) + ADAM_EPSILON)
    if decayed:
        update = update + WEIGHT_DECAY * master
        return (new_first, new_second, master - MATRIX_RATE * update)
    return (new_first, new_second, master - VECTOR_RATE * update)


def local(
    content_in,
    query_in,
    content_grad,
    query_grad,
    segment_ids,
    doc_lengths,
    factor_order,
    attn_proj,
    attn_proj_first,
    attn_proj_second,
    out_proj,
    out_proj_first,
    out_proj_second,
    up_proj,
    up_proj_first,
    up_proj_second,
    down_proj,
    down_proj_first,
    down_proj_second,
    head_bias,
    head_bias_first,
    head_bias_second,
    up_bias,
    up_bias_first,
    up_bias_second,
    norm_param,
    norm_param_first,
    norm_param_second,
):
    local_rows, width = content_in.shape
    sequences, length = segment_ids.shape
    local_heads, head_size = (head_bias.shape[1], head_bias.shape[2])
    head_cols = local_heads * head_size
    hidden_cols = up_bias.shape[0]
    group_tokens = sequences * length
    seq_shape = (sequences, length, local_heads, head_size)
    projection, out_weight, up_weight, down_weight = (
        lax.all_gather(attn_proj.astype(jnp.bfloat16), "dp", axis=1, tiled=True),
        lax.all_gather(out_proj.astype(jnp.bfloat16), "dp", axis=1, tiled=True),
        lax.all_gather(up_proj.astype(jnp.bfloat16), "dp", axis=0, tiled=True),
        lax.all_gather(down_proj.astype(jnp.bfloat16), "dp", axis=1, tiled=True),
    )
    content_rows, query_rows = (
        lax.all_gather(content_in, "heads", axis=0, tiled=True),
        lax.all_gather(query_in, "heads", axis=0, tiled=True),
    )
    projected = jnp.einsum(
        "td,kde->kte", content_rows, projection[:3], preferred_element_type=jnp.float32
    ).astype(jnp.bfloat16)
    query_g = jnp.dot(query_rows, projection[0], preferred_element_type=jnp.float32).astype(
        jnp.bfloat16
    )
    table = position_table(length, width).astype(jnp.bfloat16)
    relative = jnp.dot(table, projection[3], preferred_element_type=jnp.float32).astype(
        jnp.bfloat16
    )
    relative = relative.reshape(2 * length, local_heads, head_size)
    allow_content, allow_query, differ = jax.vmap(pair_masks)(
        segment_ids, doc_lengths, factor_order
    )
    sequence_items = (
        projected[0].reshape(seq_shape),
        projected[1].reshape(seq_shape),
        projected[2].reshape(seq_shape),
        query_g.reshape(seq_shape),
        allow_content,
        allow_query,
        differ,
    )

    def forward_sequence(items):
        query_c, key_s, value_s, query_q, allow_c, allow_q, differ_s = items
        mixed_c, logsum_c = seq_mix(
            seq_scores(query_c, key_s, relative, head_bias, differ_s), allow_c, value_s
        )
        mixed_q, logsum_q = seq_mix(
            seq_scores(query_q, key_s, relative, head_bias, differ_s), allow_q, value_s
        )
        return (mixed_c, mixed_q, logsum_c, logsum_q)

    mixed_c, mixed_q, logsum_c, logsum_q = lax.map(forward_sequence, sequence_items)
    attended_c = mixed_c.reshape(group_tokens, head_cols)
    attended_q = mixed_q.reshape(group_tokens, head_cols)
    rows_c = attended_c
    rows_q = attended_q
    attention_sum = lax.psum_scatter(
        jnp.concatenate(
            [
                jnp.dot(rows_c, out_weight, preferred_element_type=jnp.float32),
                jnp.dot(rows_q, out_weight, preferred_element_type=jnp.float32),
            ],
            1,
        ),
        "heads",
        scatter_dimension=0,
        tiled=True,
    )
    middle_c, normed1_c, inverse1_c = layer_norm_parts(
        content_in.astype(jnp.float32) + attention_sum[:, :width], norm_param[0], norm_param[1]
    )
    middle_q, normed1_q, inverse1_q = layer_norm_parts(
        query_in.astype(jnp.float32) + attention_sum[:, width:], norm_param[0], norm_param[1]
    )
    middle_rows_c, middle_rows_q = (
        lax.all_gather(middle_c.astype(jnp.bfloat16), "heads", axis=0, tiled=True),
        lax.all_gather(middle_q.astype(jnp.bfloat16), "heads", axis=0, tiled=True),
    )
    before_c = jnp.dot(middle_rows_c, up_weight, preferred_element_type=jnp.float32) + up_bias
    before_q = jnp.dot(middle_rows_q, up_weight, preferred_element_type=jnp.float32) + up_bias
    hidden_c = jax.nn.gelu(before_c, approximate=True).astype(jnp.bfloat16)
    hidden_q = jax.nn.gelu(before_q, approximate=True).astype(jnp.bfloat16)
    rows_c = hidden_c
    rows_q = hidden_q
    feed_sum = lax.psum_scatter(
        jnp.concatenate(
            [
                jnp.dot(rows_c, down_weight, preferred_element_type=jnp.float32),
                jnp.dot(rows_q, down_weight, preferred_element_type=jnp.float32),
            ],
            1,
        ).astype(jnp.bfloat16),
        "heads",
        scatter_dimension=0,
        tiled=True,
    ).astype(jnp.float32)
    final_c, normed2_c, inverse2_c = layer_norm_parts(
        middle_c + feed_sum[:, :width] + norm_param[2], norm_param[3], norm_param[4]
    )
    final_q, normed2_q, inverse2_q = layer_norm_parts(
        middle_q + feed_sum[:, width:] + norm_param[2], norm_param[3], norm_param[4]
    )
    upstream_c = content_grad.astype(jnp.float32)
    upstream_q = query_grad.astype(jnp.float32)
    dfinal_c = layer_norm_back(upstream_c, normed2_c, inverse2_c, norm_param[3])
    dfinal_q = layer_norm_back(upstream_q, normed2_q, inverse2_q, norm_param[3])
    gain2_grad = jnp.sum(upstream_c * normed2_c, 0) + jnp.sum(upstream_q * normed2_q, 0)
    bias2_grad = jnp.sum(upstream_c, 0) + jnp.sum(upstream_q, 0)
    outbias_grad = jnp.sum(dfinal_c, 0) + jnp.sum(dfinal_q, 0)
    back_c, back_q = (
        lax.all_gather(dfinal_c.astype(jnp.bfloat16), "heads", axis=0, tiled=True),
        lax.all_gather(dfinal_q.astype(jnp.bfloat16), "heads", axis=0, tiled=True),
    )
    down_grad = jnp.einsum(
        "tf,td->fd", hidden_c, back_c, preferred_element_type=jnp.float32
    ) + jnp.einsum("tf,td->fd", hidden_q, back_q, preferred_element_type=jnp.float32)
    dbefore_c = gelu_back(
        before_c, jnp.einsum("td,fd->tf", back_c, down_weight, preferred_element_type=jnp.float32)
    ).astype(jnp.bfloat16)
    dbefore_q = gelu_back(
        before_q, jnp.einsum("td,fd->tf", back_q, down_weight, preferred_element_type=jnp.float32)
    ).astype(jnp.bfloat16)
    upbias_local = jnp.sum(dbefore_c.astype(jnp.float32), 0) + jnp.sum(
        dbefore_q.astype(jnp.float32), 0
    )
    up_grad = jnp.einsum(
        "td,tf->df", middle_rows_c, dbefore_c, preferred_element_type=jnp.float32
    ) + jnp.einsum("td,tf->df", middle_rows_q, dbefore_q, preferred_element_type=jnp.float32)
    rows_c = dbefore_c
    rows_q = dbefore_q
    feed_back = lax.psum_scatter(
        jnp.concatenate(
            [
                jnp.einsum("tf,df->td", rows_c, up_weight, preferred_element_type=jnp.float32),
                jnp.einsum("tf,df->td", rows_q, up_weight, preferred_element_type=jnp.float32),
            ],
            1,
        ).astype(jnp.bfloat16),
        "heads",
        scatter_dimension=0,
        tiled=True,
    ).astype(jnp.float32)
    dmiddle_c = dfinal_c + feed_back[:, :width]
    dmiddle_q = dfinal_q + feed_back[:, width:]
    dresid_c = layer_norm_back(dmiddle_c, normed1_c, inverse1_c, norm_param[0])
    dresid_q = layer_norm_back(dmiddle_q, normed1_q, inverse1_q, norm_param[0])
    gain1_grad = jnp.sum(dmiddle_c * normed1_c, 0) + jnp.sum(dmiddle_q * normed1_q, 0)
    bias1_grad = jnp.sum(dmiddle_c, 0) + jnp.sum(dmiddle_q, 0)
    dattn_c, dattn_q = (
        lax.all_gather(dresid_c.astype(jnp.bfloat16), "heads", axis=0, tiled=True),
        lax.all_gather(dresid_q.astype(jnp.bfloat16), "heads", axis=0, tiled=True),
    )
    out_grad = jnp.einsum(
        "te,td->ed", attended_c, dattn_c, preferred_element_type=jnp.float32
    ) + jnp.einsum("te,td->ed", attended_q, dattn_q, preferred_element_type=jnp.float32)
    dmixed_c = jnp.einsum(
        "td,ed->te", dattn_c, out_weight, preferred_element_type=jnp.float32
    ).astype(jnp.bfloat16)
    dmixed_q = jnp.einsum(
        "td,ed->te", dattn_q, out_weight, preferred_element_type=jnp.float32
    ).astype(jnp.bfloat16)

    def backward_sequence(items):
        (
            query_c,
            key_s,
            value_s,
            query_q,
            allow_c,
            allow_q,
            differ_s,
            logsum_cs,
            logsum_qs,
            upper_c,
            upper_q,
        ) = items
        dscore_c, dvalue_c = seq_mix_back(
            seq_scores(query_c, key_s, relative, head_bias, differ_s),
            allow_c,
            logsum_cs,
            value_s,
            upper_c,
        )
        dscore_q, dvalue_q = seq_mix_back(
            seq_scores(query_q, key_s, relative, head_bias, differ_s),
            allow_q,
            logsum_qs,
            value_s,
            upper_q,
        )
        dquery_c, dkey_c, drel_c, dhead_c = seq_scores_back(
            dscore_c, query_c, key_s, relative, head_bias, differ_s
        )
        dquery_q, dkey_q, drel_q, dhead_q = seq_scores_back(
            dscore_q, query_q, key_s, relative, head_bias, differ_s
        )
        return (
            dquery_c.astype(jnp.bfloat16),
            (dkey_c + dkey_q).astype(jnp.bfloat16),
            (dvalue_c + dvalue_q).astype(jnp.bfloat16),
            dquery_q.astype(jnp.bfloat16),
            (drel_c + drel_q).astype(jnp.bfloat16),
            dhead_c + dhead_q,
        )

    dquery_all, dkey_all, dvalue_all, dquery_g, drel_all, dhead_all = lax.map(
        backward_sequence,
        sequence_items
        + (logsum_c, logsum_q, dmixed_c.reshape(seq_shape), dmixed_q.reshape(seq_shape)),
    )
    dstack = jnp.stack(
        [
            dquery_all.reshape(group_tokens, head_cols),
            dkey_all.reshape(group_tokens, head_cols),
            dvalue_all.reshape(group_tokens, head_cols),
        ]
    )
    dquery_g = dquery_g.reshape(group_tokens, head_cols)
    drel_sum = jnp.sum(drel_all.astype(jnp.float32), 0).reshape(2 * length, head_cols)
    head_local = jnp.sum(dhead_all, 0)
    proj_three = jnp.einsum("td,kte->kde", content_rows, dstack, preferred_element_type=jnp.float32)
    query_term = jnp.einsum("td,te->de", query_rows, dquery_g, preferred_element_type=jnp.float32)
    rel_term = jnp.dot(table.astype(jnp.float32).T, drel_sum, precision=HIGH_PRECISION)
    proj_grad = jnp.stack([proj_three[0] + query_term, proj_three[1], proj_three[2], rel_term])
    content_part = jnp.einsum(
        "kte,kde->td", dstack, projection[:3], preferred_element_type=jnp.float32
    )
    query_part = jnp.einsum(
        "te,de->td", dquery_g, projection[0], preferred_element_type=jnp.float32
    )
    input_back = lax.psum_scatter(
        jnp.concatenate([content_part, query_part], 1).astype(jnp.bfloat16),
        "heads",
        scatter_dimension=0,
        tiled=True,
    ).astype(jnp.float32)
    content_in_grad = dresid_c + input_back[:, :width]
    query_in_grad = dresid_q + input_back[:, width:]
    proj_share, out_share, up_share, down_share = (
        lax.psum_scatter(proj_grad, "dp", scatter_dimension=1, tiled=True),
        lax.psum_scatter(out_grad, "dp", scatter_dimension=1, tiled=True),
        lax.psum_scatter(up_grad, "dp", scatter_dimension=0, tiled=True),
        lax.psum_scatter(down_grad, "dp", scatter_dimension=1, tiled=True),
    )
    heads_count = lax.axis_size("heads")
    head_index = lax.axis_index("heads")
    head_full = jnp.zeros((5, local_heads * heads_count, head_size), jnp.float32)
    head_full = lax.dynamic_update_slice_in_dim(head_full, head_local, head_index * local_heads, 1)
    bias_full = jnp.zeros((hidden_cols * heads_count,), jnp.float32)
    bias_full = lax.dynamic_update_slice_in_dim(
        bias_full, upbias_local, head_index * hidden_cols, 0
    )
    norm_local = jnp.stack([gain1_grad, bias1_grad, outbias_grad, gain2_grad, bias2_grad])
    head_sum, bias_sum, norm_sum = lax.psum((head_full, bias_full, norm_local), ("dp", "heads"))
    head_grad = lax.dynamic_slice_in_dim(head_sum, head_index * local_heads, local_heads, 1)
    bias_grad = lax.dynamic_slice_in_dim(bias_sum, head_index * hidden_cols, hidden_cols, 0)
    devices = lax.axis_size("dp") * heads_count
    shared_squares = (
        jnp.sum(head_sum * head_sum) + jnp.sum(bias_sum * bias_sum) + jnp.sum(norm_sum * norm_sum)
    )
    local_squares = (
        jnp.sum(proj_share * proj_share)
        + jnp.sum(out_share * out_share)
        + jnp.sum(up_share * up_share)
        + jnp.sum(down_share * down_share)
        + shared_squares / devices
    )
    grad_norm = jnp.sqrt(lax.psum(local_squares, ("dp", "heads")))
    factor = CLIP_NORM / jnp.maximum(grad_norm, CLIP_NORM)
    attn_first, attn_second, attn_new = adam_step(
        attn_proj, attn_proj_first, attn_proj_second, proj_share, factor, True
    )
    out_first, out_second, out_new = adam_step(
        out_proj, out_proj_first, out_proj_second, out_share, factor, True
    )
    up_first, up_second, up_new = adam_step(
        up_proj, up_proj_first, up_proj_second, up_share, factor, True
    )
    down_first, down_second, down_new = adam_step(
        down_proj, down_proj_first, down_proj_second, down_share, factor, True
    )
    head_first, head_second, head_new = adam_step(
        head_bias, head_bias_first, head_bias_second, head_grad, factor, False
    )
    bias_first, bias_second, bias_new = adam_step(
        up_bias, up_bias_first, up_bias_second, bias_grad, factor, False
    )
    norm_first, norm_second, norm_new = adam_step(
        norm_param, norm_param_first, norm_param_second, norm_sum, factor, False
    )
    return (
        final_c.astype(jnp.bfloat16),
        final_q.astype(jnp.bfloat16),
        content_in_grad,
        query_in_grad,
        grad_norm,
        proj_share,
        attn_first,
        attn_second,
        attn_new,
        out_share,
        out_first,
        out_second,
        out_new,
        up_share,
        up_first,
        up_second,
        up_new,
        down_share,
        down_first,
        down_second,
        down_new,
        head_grad,
        head_first,
        head_second,
        head_new,
        bias_grad,
        bias_first,
        bias_second,
        bias_new,
        norm_sum,
        norm_first,
        norm_second,
        norm_new,
    )


def solution(mesh):
    return jax.shard_map(
        local,
        mesh=mesh,
        in_specs=(
            P(("dp", "heads"), None),
            P(("dp", "heads"), None),
            P(("dp", "heads"), None),
            P(("dp", "heads"), None),
            P("dp", None),
            P("dp", None),
            P("dp", None),
            P(None, "dp", "heads"),
            P(None, "dp", "heads"),
            P(None, "dp", "heads"),
            P("heads", "dp"),
            P("heads", "dp"),
            P("heads", "dp"),
            P("dp", "heads"),
            P("dp", "heads"),
            P("dp", "heads"),
            P("heads", "dp"),
            P("heads", "dp"),
            P("heads", "dp"),
            P(None, "heads", None),
            P(None, "heads", None),
            P(None, "heads", None),
            P("heads"),
            P("heads"),
            P("heads"),
            P(),
            P(),
            P(),
        ),
        out_specs=(
            P(("dp", "heads"), None),
            P(("dp", "heads"), None),
            P(("dp", "heads"), None),
            P(("dp", "heads"), None),
            P(),
            P(None, "dp", "heads"),
            P(None, "dp", "heads"),
            P(None, "dp", "heads"),
            P(None, "dp", "heads"),
            P("heads", "dp"),
            P("heads", "dp"),
            P("heads", "dp"),
            P("heads", "dp"),
            P("dp", "heads"),
            P("dp", "heads"),
            P("dp", "heads"),
            P("dp", "heads"),
            P("heads", "dp"),
            P("heads", "dp"),
            P("heads", "dp"),
            P("heads", "dp"),
            P(None, "heads", None),
            P(None, "heads", None),
            P(None, "heads", None),
            P(None, "heads", None),
            P("heads"),
            P("heads"),
            P("heads"),
            P("heads"),
            P(),
            P(),
            P(),
            P(),
        ),
        check_vma=False,
    )
```

profile of v0, /device:TPU:0, one launch (start us, length us, event | category | flops | bytes accessed | tf_op | source)
XLA Modules:
  0.0 2122.7 jit_solution(9810665744599799521)
XLA Ops:
  13.4 35.7 %all_gather.39 = bf16[192,768]{0,1:T(8,128)(2,1)} all-gather(bf16[192,96]{0,1:T(8,128)(2,1)S(1)} %copy.315), channel_id=1, replica_groups=mesh['dp'=8,'heads'=4] {'dp'}, dimensions={1}, use_global_device_ids=true | all-gather | bytes 331776 | tf_op jit(solution)/shard_map/all_gather | solution.py:225
  70.5 13.2 all-gather.16.cloned.1.call-done
  87.7 21.7 %all-gather.14.cloned.1.call-done = bf16[1536,768]{1,0:T(8,128)(2,1)} async-done(((bf16[384,768]{1,0:T(8,128)(2,1)}), bf16[1536,768]{1,0:T(8,128)(2,1)}) %all-gather.14.cloned.1.call-update) | async-done | bytes 2359312 | tf_op jit(solution)/shard_map/all_gather | solution.py:230
  118.6 550.2 %while.38 = (s32[]{:T(128)}, bf16[3,512,3,64]{1,3,2,0:T(8,128)(2,1)}, bf16[3,512,3,64]{1,3,2,0:T(8,128)(2,1)}, f32[3,3,512]{2,1,0:T(4,128)}, f32[3,3,512]{2,1,0:...) while((s32[]{:T(128)}, ...), condition=%wide.region_8.9_spmd, body=%wide.region_3.8_spmd.sunk | while | flops 868459520 | bytes 825601664 | solution.py:267
  164.5 8.1 pad_select_fusion.91
  179.6 7.9 pad_select_fusion.92
  196.0 7.9 pad_select_fusion.93
  228.7 7.8 pad_select_fusion.95
  244.9 7.8 pad_select_fusion.96
  338.9 8.1 pad_select_fusion.91
  353.9 7.9 pad_select_fusion.92
  370.4 7.9 pad_select_fusion.93
  403.1 7.8 pad_select_fusion.95
  419.3 7.8 pad_select_fusion.96
  513.2 8.1 pad_select_fusion.91
  528.3 7.9 pad_select_fusion.92
  544.8 7.9 pad_select_fusion.93
  577.5 7.8 pad_select_fusion.95
  593.7 7.8 pad_select_fusion.96
  685.1 75.5 %reduce-scatter.19.cloned.1.call-done = f32[384,1536]{0,1:T(8,128)} async-done(((f32[1536,1536]{0,1:T(8,128)}), f32[384,1536]{0,1:T(8,128)}) %reduce-scatter.19.cloned.1.call-update) | async-done | bytes 2359312 | tf_op jit(solution)/shard_map/reduce_scatter | solution.py:272
  766.2 38.1 %all-gather.20.cloned.1.call-done = bf16[768,768]{1,0:T(8,128)(2,1)} async-done(((bf16[96,768]{1,0:T(8,128)(2,1)}), bf16[768,768]{1,0:T(8,128)(2,1)}) %all-gather.20.cloned.1.call-update) | async-done | bytes 1179664 | tf_op jit(solution)/shard_map/all_gather | solution.py:226
  804.3 24.8 %all-gather.24.cloned.1.call-done = bf16[1536,768]{0,1:T(8,128)(2,1)} async-done(((bf16[384,768]{0,1:T(8,128)(2,1)}), bf16[1536,768]{0,1:T(8,128)(2,1)}) %all-gather.24.cloned.1.call-update) | async-done | bytes 2359312 | tf_op jit(solution)/shard_map/all_gather | solution.py:292
  835.4 20.0 all-gather.18.cloned.1.call-done
  861.5 37.7 %all-gather.22.cloned.1.call-done = bf16[768,768]{0,1:T(8,128)(2,1)} async-done(((bf16[768,96]{0,1:T(8,128)(2,1)}), bf16[768,768]{0,1:T(8,128)(2,1)}) %all-gather.22.cloned.1.call-update) | async-done | bytes 1179664 | tf_op jit(solution)/shard_map/all_gather | solution.py:227
  918.9 43.3 %reduce-scatter.25.cloned.1.call-done = bf16[384,1536]{1,0:T(8,128)(2,1)} async-done(((bf16[1536,1536]{1,0:T(8,128)(2,1)}), bf16[384,1536]{1,0:T(8,128)(2,1)}) %reduce-scatter.25.cloned.1.call-update) | async-done | bytes 1179664
  972.3 23.4 %all-gather.28.cloned.1.call-done = bf16[1536,768]{0,1:T(8,128)(2,1)} async-done(((bf16[384,768]{0,1:T(8,128)(2,1)}), bf16[1536,768]{0,1:T(8,128)(2,1)}) %all-gather.28.cloned.1.call-update) | async-done | bytes 2359312 | tf_op jit(solution)/shard_map/all_gather | solution.py:327
  1002.0 20.0 all-gather.26.cloned.1.call-done
  1022.1 13.6 convert_reduce_fusion.5
  1049.1 47.8 %reduce-scatter.27.cloned.1.call-done = bf16[384,1536]{1,0:T(8,128)(2,1)} async-done(((bf16[1536,1536]{1,0:T(8,128)(2,1)}), bf16[384,1536]{1,0:T(8,128)(2,1)}) %reduce-scatter.27.cloned.1.call-update) | async-done | bytes 1179664
  1134.0 22.3 %all-gather.32.cloned.1.call-done = bf16[1536,768]{0,1:T(8,128)(2,1)} async-done(((bf16[384,768]{0,1:T(8,128)(2,1)}), bf16[1536,768]{0,1:T(8,128)(2,1)}) %all-gather.32.cloned.1.call-update) | async-done | bytes 2359312 | tf_op jit(solution)/shard_map/all_gather | solution.py:366
  1163.6 734.7 %while.39 = (s32[]{:T(128)}, bf16[3,512,3,64]{1,3,2,0:T(8,128)(2,1)}, bf16[3,512,3,64]{1,3,2,0:T(8,128)(2,1)}, bf16[3,512,3,64]{1,3,2,0:T(8,128)(2,1)}, bf16[3,5...) while((s32[]{:T(128)}, ...), condition=%wide.region_43.44_spmd, body=%wide.region_28.43_spmd.sunk | while | flops 2349047808 | bytes 1216818048 | solution.py:421
  1197.4 8.5 pad_select_fusion.104
  1212.8 8.0 pad_select_fusion.105
  1229.5 7.8 pad_select_fusion.106
  1245.8 7.8 pad_select_fusion.107
  1262.0 8.1 pad_select_fusion.108
  1278.5 7.7 pad_select_fusion.109
  1440.5 8.2 pad_select_fusion.104
  1455.6 7.8 pad_select_fusion.105
  1472.0 7.8 pad_select_fusion.106
  1504.3 8.2 pad_select_fusion.108
  1682.8 8.1 pad_select_fusion.104
  1697.9 7.8 pad_select_fusion.105
  1714.3 7.8 pad_select_fusion.106
  1746.7 8.0 pad_select_fusion.108
  1946.1 40.8 %all-reduce.62 = (f32[5,12,64]{2,1,0:T(8,128)S(1)}, f32[3072]{0:T(1024)S(1)}, f32[5,768]{1,0:T(8,128)S(1)}) all-reduce(f32[5,12,64]{2,1,0:T(8,128)S(1)} %dynamic_update_slice.50, f32[3072]{0:T(1024)S(1)} %add_dynamic-update-slice_fusion, f32[5,768]{1,0:T(8,128)S(1)} %stack.61), channel_id=1, replica_groups=mesh['dp'=8,'heads'=4] {'dp','heads'}, use_global_device_ids=true, to_apply=%region_55.56 | all-reduce | flops 10752 | bytes 86016 | tf_op jit(solution)/shard_map/psum | solution.py:469
  1992.4 51.5 %reduce-scatter.31.cloned.1.call-done = f32[96,768]{1,0:T(8,128)} async-done(((f32[768,768]{1,0:T(8,128)}), f32[96,768]{1,0:T(8,128)}) %reduce-scatter.31.cloned.1.call-update) | async-done | bytes 294928
  2049.8 39.7 %psum.31 = f32[]{:T(128)} all-reduce(f32[]{:T(128)S(6)} %add.882), channel_id=1, replica_groups=mesh['dp'=8,'heads'=4] {'dp','heads'}, use_global_device_ids=true, to_apply=%region_73.74 | all-reduce | flops 1 | bytes 8 | tf_op jit(solution)/shard_map/psum | solution.py:483
  (1453 shorter events, 1262.7 us)
Async XLA Ops:
  7.2 50.8 %copy-start.126 = (s32[3,512]{1,0:T(4,128)S(1)}, s32[3,512]{1,0:T(4,128)}, u32[]{:S(2)}) copy-start(s32[3,512]{1,0:T(4,128)} %param.36) | copy-start | bytes 18436
  7.2 55.4 %all-gather.12.cloned.1.call-start = ((), (), s32[]{:S(2)}) async-start(), calls=%async_computation.8 | async-start | bytes 1769472 | tf_op jit(solution)/shard_map/all_gather | solution.py:224
  9.2 74.5 %all-gather.16.cloned.1.call-start = ((), (), s32[]{:S(2)}) async-start(), calls=%async_computation.10 | async-start | bytes 2949120 | tf_op jit(solution)/shard_map/all_gather | solution.py:231
  10.0 99.4 %all-gather.14.cloned.1.call-start = ((), (), s32[]{:S(2)}) async-start(), calls=%async_computation.9 | async-start | bytes 2949120 | tf_op jit(solution)/shard_map/all_gather | solution.py:230
  10.7 749.9 %reduce-scatter.19.cloned.1.call-start = ((), (), s32[]{:S(2)}) async-start(), calls=%async_computation.11 | async-start | bytes 11796480 | tf_op jit(solution)/shard_map/reduce_scatter | solution.py:272
  67.7 16.0 copy-start.78
  70.5 38.9 %copy-start.81 = (bf16[3,768,192]{1,2,0:T(8,128)(2,1)S(1)}, bf16[3,768,192]{1,2,0:T(8,128)(2,1)}, u32[]{:S(2)}) copy-start(bf16[3,768,192]{1,2,0:T(8,128)(2,1)} %copy.406) | copy-start | bytes 2654212
  141.2 13.1 copy-start.16
  141.2 13.1 copy-start.44
  682.0 122.3 %all-gather.20.cloned.1.call-start = ((), (), s32[]{:S(2)}) async-start(), calls=%async_computation.13 | async-start | bytes 1327104 | tf_op jit(solution)/shard_map/all_gather | solution.py:226
  683.6 145.5 %all-gather.24.cloned.1.call-start = ((), (), s32[]{:S(2)}) async-start(), calls=%async_computation.15 | async-start | bytes 2949120 | tf_op jit(solution)/shard_map/all_gather | solution.py:292
  685.1 421.1 %copy-start.104 = (f32[768]{0:T(1024)}, f32[768]{0:T(1024)S(1)}, u32[]{:S(2)}) copy-start(f32[768]{0:T(1024)S(1)} %get-tuple-element.760) | copy-start | bytes 9220
  762.6 340.1 %copy-start.29 = (f32[384,768]{0,1:T(8,128)}, f32[384,768]{0,1:T(8,128)S(1)}, u32[]{:S(2)}) copy-start(f32[384,768]{0,1:T(8,128)S(1)} %get-tuple-element.875) | copy-start | bytes 3538948
  762.6 343.6 %copy-start.27 = (f32[384,768]{0,1:T(8,128)}, f32[384,768]{0,1:T(8,128)S(1)}, u32[]{:S(2)}) copy-start(f32[384,768]{0,1:T(8,128)S(1)} %get-tuple-element.976) | copy-start | bytes 3538948
  762.6 340.1 %copy-start.108 = (f32[384]{0:T(512)}, f32[384]{0:T(512)S(1)}, u32[]{:S(2)}) copy-start(f32[384]{0:T(512)S(1)} %broadcast_multiply_fusion.11) | copy-start | bytes 4612
  762.7 343.5 %copy-start.110 = (f32[384]{0:T(512)}, f32[384]{0:T(512)S(1)}, u32[]{:S(2)}) copy-start(f32[384]{0:T(512)S(1)} %broadcast_multiply_fusion.10) | copy-start | bytes 4612
  763.0 343.2 %copy-start.115 = (f32[384]{0:T(512)}, f32[384]{0:T(512)S(1)}, u32[]{:S(2)}) copy-start(f32[384]{0:T(512)S(1)} %add_rsqrt_fusion.2) | copy-start | bytes 4612
  763.0 339.7 %copy-start.113 = (f32[384]{0:T(512)}, f32[384]{0:T(512)S(1)}, u32[]{:S(2)}) copy-start(f32[384]{0:T(512)S(1)} %add_rsqrt_fusion.3) | copy-start | bytes 4612
  764.4 90.9 %all-gather.18.cloned.1.call-start = ((), (), s32[]{:S(2)}) async-start(), calls=%async_computation.12 | async-start | bytes 2949120 | tf_op jit(solution)/shard_map/all_gather | solution.py:291
  765.2 134.0 %all-gather.22.cloned.1.call-start = ((), (), s32[]{:S(2)}) async-start(), calls=%async_computation.14 | async-start | bytes 1327104 | tf_op jit(solution)/shard_map/all_gather | solution.py:227
  766.0 196.3 %reduce-scatter.25.cloned.1.call-start = ((), (), s32[]{:S(2)}) async-start(), calls=%async_computation.22 | async-start | bytes 5898240
  835.4 63.8 %copy-start.143 = (f32[768]{0:T(1024)S(1)}, f32[768]{0:T(1024)}, u32[]{:S(2)}) copy-start(f32[768]{0:T(1024)} %param.54) | copy-start | bytes 9220
  915.5 80.3 %all-gather.28.cloned.1.call-start = ((), (), s32[]{:S(2)}) async-start(), calls=%async_computation.17 | async-start | bytes 2949120 | tf_op jit(solution)/shard_map/all_gather | solution.py:327
  971.6 50.5 %all-gather.26.cloned.1.call-start = ((), (), s32[]{:S(2)}) async-start(), calls=%async_computation.16 | async-start | bytes 2949120 | tf_op jit(solution)/shard_map/all_gather | solution.py:326
  972.3 124.6 %reduce-scatter.27.cloned.1.call-start = ((), (), s32[]{:S(2)}) async-start(), calls=%async_computation.23 | async-start | bytes 5898240
  1022.1 13.6 copy-start.149
  1048.9 81.4 %all-gather.30.cloned.1.call-start = ((), (), s32[]{:S(2)}) async-start(), calls=%async_computation.18 | async-start | bytes 2949120 | tf_op jit(solution)/shard_map/all_gather | solution.py:365
  1106.1 50.3 %all-gather.32.cloned.1.call-start = ((), (), s32[]{:S(2)}) async-start(), calls=%async_computation.19 | async-start | bytes 2949120 | tf_op jit(solution)/shard_map/all_gather | solution.py:366
  1108.7 833.7 %reduce-scatter.23.cloned.1.call-start = ((), (), s32[]{:S(2)}) async-start(), calls=%async_computation.21 | async-start | bytes 2654208 | tf_op jit(solution)/shard_map/reduce_scatter | solution.py:458
  1120.2 823.8 %reduce-scatter.21.cloned.1.call-start = ((), (), s32[]{:S(2)}) async-start(), calls=%async_computation.20 | async-start | bytes 2654208 | tf_op jit(solution)/shard_map/reduce_scatter | solution.py:457
  1128.4 862.4 %reduce-scatter.33.cloned.1.call-start = ((), (), s32[]{:S(2)}) async-start(), calls=%async_computation.26 | async-start | bytes 884736
  1163.8 18.1 copy-start.56
  1163.8 23.4 %copy-start.18 = (bf16[1024,3,64]{0,2,1:T(8,128)(2,1)}, bf16[1024,3,64]{0,2,1:T(8,128)(2,1)S(1)}, u32[]{:S(2)}) copy-start(bf16[1024,3,64]{0,2,1:T(8,128)(2,1)S(1)} %get-tuple-element.1538) | copy-start | bytes 1179652 | tf_op jit(solution)/shard_map/while
  1163.8 23.4 %copy-start.46 = (f32[3,1024]{1,0:T(4,128)}, f32[3,1024]{1,0:T(4,128)S(1)}, u32[]{:S(2)}) copy-start(f32[3,1024]{1,0:T(4,128)S(1)} %get-tuple-element.1539) | copy-start | bytes 36868 | tf_op jit(solution)/shard_map/while
  1165.1 32.3 %copy-start.119 = (pred[512]{0:T(512)(128)(4,1)}, pred[512]{0:T(512)(128)(4,1)S(1)}, u32[]{:S(2)}) copy-start(pred[512]{0:T(512)(128)(4,1)S(1)} %and_compare_fusion.50) | copy-start | bytes 1540 | tf_op jit(solution)/shard_map/while
  1407.0 18.1 copy-start.56
  1407.0 23.4 %copy-start.18 = (bf16[1024,3,64]{0,2,1:T(8,128)(2,1)}, bf16[1024,3,64]{0,2,1:T(8,128)(2,1)S(1)}, u32[]{:S(2)}) copy-start(bf16[1024,3,64]{0,2,1:T(8,128)(2,1)S(1)} %get-tuple-element.1538) | copy-start | bytes 1179652 | tf_op jit(solution)/shard_map/while
  1407.0 23.4 %copy-start.46 = (f32[3,1024]{1,0:T(4,128)}, f32[3,1024]{1,0:T(4,128)S(1)}, u32[]{:S(2)}) copy-start(f32[3,1024]{1,0:T(4,128)S(1)} %get-tuple-element.1539) | copy-start | bytes 36868 | tf_op jit(solution)/shard_map/while
  1408.3 32.2 %copy-start.119 = (pred[512]{0:T(512)(128)(4,1)}, pred[512]{0:T(512)(128)(4,1)S(1)}, u32[]{:S(2)}) copy-start(pred[512]{0:T(512)(128)(4,1)S(1)} %and_compare_fusion.50) | copy-start | bytes 1540 | tf_op jit(solution)/shard_map/while
  1649.4 18.1 copy-start.56
  1649.4 23.4 %copy-start.18 = (bf16[1024,3,64]{0,2,1:T(8,128)(2,1)}, bf16[1024,3,64]{0,2,1:T(8,128)(2,1)S(1)}, u32[]{:S(2)}) copy-start(bf16[1024,3,64]{0,2,1:T(8,128)(2,1)S(1)} %get-tuple-element.1538) | copy-start | bytes 1179652 | tf_op jit(solution)/shard_map/while
  1649.4 23.4 %copy-start.46 = (f32[3,1024]{1,0:T(4,128)}, f32[3,1024]{1,0:T(4,128)S(1)}, u32[]{:S(2)}) copy-start(f32[3,1024]{1,0:T(4,128)S(1)} %get-tuple-element.1539) | copy-start | bytes 36868 | tf_op jit(solution)/shard_map/while
  1650.6 32.2 %copy-start.119 = (pred[512]{0:T(512)(128)(4,1)}, pred[512]{0:T(512)(128)(4,1)S(1)}, u32[]{:S(2)}) copy-start(pred[512]{0:T(512)(128)(4,1)S(1)} %and_compare_fusion.50) | copy-start | bytes 1540 | tf_op jit(solution)/shard_map/while
  1909.1 134.8 %reduce-scatter.31.cloned.1.call-start = ((), (), s32[]{:S(2)}) async-start(), calls=%async_computation.25 | async-start | bytes 2654208
  1926.0 177.7 %reduce-scatter.29.cloned.1.call-start = ((), (), s32[]{:S(2)}) async-start(), calls=%async_computation.24 | async-start | bytes 5898240
  1940.7 108.0 %copy-start.58 = (bf16[384,768]{0,1:T(8,128)(2,1)S(1)}, bf16[384,768]{0,1:T(8,128)(2,1)}, u32[]{:S(2)}) copy-start(bf16[384,768]{0,1:T(8,128)(2,1)} %get-tuple-element.989) | copy-start | bytes 1769476
  2049.8 44.5 %copy-start.144 = (f32[768]{0:T(1024)S(1)}, f32[768]{0:T(1024)}, u32[]{:S(2)}) copy-start(f32[768]{0:T(1024)} %param.54) | copy-start | bytes 9220
  2049.8 45.9 %copy-start.125 = (f32[5,3,64]{2,1,0:T(4,128)S(1)}, f32[5,3,64]{2,1,0:T(4,128)}, u32[]{:S(2)}) copy-start(f32[5,3,64]{2,1,0:T(4,128)} %param.51) | copy-start | bytes 11524
  (300 other events, 1274.1 us)
Sparse Core Ops, SparseCore 0:
  10.8 48.0 all-gather.11
  60.4 23.2 all-gather.15
  85.3 24.0 all-gather.13
  682.1 78.4 reduce-scatter.18
  763.2 41.0 all-gather.19
  806.3 22.7 all-gather.23
  831.3 24.0 all-gather.17
  858.1 41.0 all-gather.21
  915.6 46.5 reduce-scatter.24
  971.7 24.0 all-gather.27
  998.0 24.0 all-gather.25
  1049.0 47.8 reduce-scatter.26
  1106.2 24.0 all-gather.29
  1132.3 24.0 all-gather.31
  1160.3 68.9 reduce-scatter.22
  1233.1 68.0 reduce-scatter.20
  1909.3 62.5 reduce-scatter.32
  1975.6 68.2 reduce-scatter.30
  2046.6 47.5 reduce-scatter.28
where the time goes:
time: 2130 us; the launch traced here: 2120 us
  local copies, waits for them, and re-layouts  605 us (28%)
  other arithmetic  593 us (28%)
  waiting for transfers between devices  444 us (21%)
  matrix products  302 us (14%)
  blocking collectives  116 us (5%)
  loops' own time  38.4 us (2%)
  between operations  22.4 us (1%)
    select_n x54, other arithmetic, rel_shift(): shifted = jnp.where(chosen[:, None], moved, shifted)  415 us
    slice x120, local copies, waits for them, and re-layouts, rel_shift(): moved = jnp.concatenate([shifted[..., step:], filler], -1)  390 us
    unnamed x24, waiting for transfers between devices  146 us
    while x504, local copies, waits for them, and re-layouts  86.5 us
    reduce_scatter x1, waiting for transfers between devices, local(): lax.psum_scatter(jnp.concatenate([jnp.dot(rows_c, out_weight, preferred_e...  75.5 us
    unnamed x227, local copies, waits for them, and re-layouts  65.5 us
    select_n x27, other arithmetic, rel_unshift(): shifted = jnp.where(chosen[:, None], moved, shifted)  58.2 us
  transfers between devices with their start and end apart: 19, of which 14 were waited for; matrix products, arithmetic and copies ran while one was open for 39% of the time, Pallas kernels for 0%

commit v1 on v0

--- a/solution.py
+++ b/solution.py
@@ -1,6 +1,12 @@
+import functools
+
 import jax
 import jax.numpy as jnp
+import ml_dtypes
+import numpy as np
 from jax import lax
+from jax.experimental import pallas as pl
+from jax.experimental.pallas import tpu as pltpu
 from jax.sharding import PartitionSpec as P
 
 STEP = 10
@@ -16,138 +22,350 @@
 ADAM_EPSILON = 1e-08
 WEIGHT_DECAY = 0.01
 MASKED_SCORE = -1e30
+LOG2E = 1.4426950408889634
+VMEM_LIMIT = 56 << 20
 
 
 def position_table(length, width):
-    distance = (length - jnp.arange(2 * length)).astype(jnp.float32)
-    frequency = 1.0 / 10000.0 ** (jnp.arange(0, width, 2).astype(jnp.float32) / width)
+    distance = length // 2 - np.arange(length)
+    frequency = 10000.0 ** (-np.arange(0, width, 2) / width)
     angles = distance[:, None] * frequency[None, :]
-    return jnp.concatenate([jnp.sin(angles), jnp.cos(angles)], -1)
-
-
-def pair_masks(segment, lengths, order):
-    length = segment.shape[-1]
+    return np.concatenate([np.sin(angles), np.cos(angles)], -1).astype(np.float32).astype(ml_dtypes.bfloat16)
+
+
+def dot(left, right):
+    return lax.dot_general(left, right, (((1,), (0,)), ((), ())), preferred_element_type=jnp.float32)
+
+
+def dot_nt(left, right):
+    return lax.dot_general(left, right, (((1,), (1,)), ((), ())), preferred_element_type=jnp.float32)
+
+
+def split_pair(values):
+    high = values.astype(jnp.bfloat16)
+    low = (values - high.astype(jnp.float32)).astype(jnp.bfloat16)
+    return jnp.concatenate([high, low], -1)
+
+
+def row_facts(segment_ids, doc_lengths, factor_order):
+    rows, length = segment_ids.shape
     places = jnp.arange(length, dtype=jnp.int32)
-    doc_ends = jnp.cumsum(lengths, -1)
-    document = jnp.sum((places[:, None] >= doc_ends[None, :]).astype(jnp.int32), -1)
-    ranking = jnp.sum(jnp.where(order[:, None] == places[None, :], places[:, None], 0), 0)
-    same_doc = document[:, None] == document[None, :]
-    allow_content = same_doc & (ranking[None, :] <= ranking[:, None])
-    allow_query = same_doc & (ranking[None, :] < ranking[:, None])
-    differ = (segment[:, None] != segment[None, :]).astype(jnp.float32)
-    return (allow_content, allow_query, differ)
-
-
-def rel_shift(wide_scores):
-    length = wide_scores.shape[-2]
-    amount = length - jnp.arange(length, dtype=jnp.int32)
-    shifted = wide_scores
-    for bit in range(length.bit_length()):
-        step = 1 << bit
-        filler = jnp.zeros(shifted.shape[:-1] + (step,), shifted.dtype)
-        moved = jnp.concatenate([shifted[..., step:], filler], -1)
-        chosen = amount >> bit & 1 == 1
-        shifted = jnp.where(chosen[:, None], moved, shifted)
-    return shifted[..., :length]
-
-
-def rel_unshift(narrow):
-    length = narrow.shape[-1]
-    amount = length - jnp.arange(length, dtype=jnp.int32)
-    shifted = jnp.concatenate([narrow, jnp.zeros(narrow.shape, narrow.dtype)], -1)
-    for bit in range(length.bit_length()):
-        step = 1 << bit
-        filler = jnp.zeros(shifted.shape[:-1] + (step,), shifted.dtype)
-        moved = jnp.concatenate([filler, shifted[..., :-step]], -1)
-        chosen = amount >> bit & 1 == 1
-        shifted = jnp.where(chosen[:, None], moved, shifted)
-    return shifted
-
-
-def seq_scores(query_now, keys_now, relative, head_bias, differ):
-    scale = query_now.shape[-1] ** (-0.5)
-    content = jnp.einsum("ihd,jhd->hij", query_now, keys_now, preferred_element_type=jnp.float32)
-    content = (
-        content
-        + jnp.einsum(
-            "jhd,hd->hj", keys_now.astype(jnp.float32), head_bias[0], precision=HIGH_PRECISION
-        )[:, None, :]
-    )
-    position = jnp.einsum("ihd,phd->hip", query_now, relative, preferred_element_type=jnp.float32)
-    position = (
-        position
-        + jnp.einsum(
-            "phd,hd->hp", relative.astype(jnp.float32), head_bias[1], precision=HIGH_PRECISION
-        )[:, None, :]
-    )
-    segment = jnp.einsum(
-        "ihd,shd->hsi",
-        query_now.astype(jnp.float32) + head_bias[2],
-        head_bias[3:5],
-        precision=HIGH_PRECISION,
-    )
-    seg_term = segment[:, 0, :, None] + differ[None] * (
-        segment[:, 1, :, None] - segment[:, 0, :, None]
-    )
-    return (content + rel_shift(position) + seg_term) * scale
-
-
-def seq_mix(scores, allowed, values):
-    highest = jnp.maximum(jnp.max(jnp.where(allowed, scores, MASKED_SCORE), -1), 0.0)
-    weights_exp = jnp.exp(jnp.where(allowed, scores - highest[..., None], MASKED_SCORE))
-    totals = jnp.exp(-highest) + jnp.sum(weights_exp, -1)
-    chances = (weights_exp / totals[..., None]).astype(jnp.bfloat16)
-    mixed = jnp.einsum("hij,jhd->ihd", chances, values, preferred_element_type=jnp.float32)
-    return (mixed.astype(jnp.bfloat16), highest + jnp.log(totals))
-
-
-def seq_mix_back(scores, allowed, logsum, values, upper):
-    chances = jnp.exp(jnp.where(allowed, scores - logsum[..., None], MASKED_SCORE))
-    dchance = jnp.einsum("ihd,jhd->hij", upper, values, preferred_element_type=jnp.float32)
-    dvalues = jnp.einsum(
-        "hij,ihd->jhd", chances.astype(jnp.bfloat16), upper, preferred_element_type=jnp.float32
-    )
-    centre = jnp.sum(chances * dchance, -1, keepdims=True)
-    return ((chances * (dchance - centre)).astype(jnp.bfloat16), dvalues)
-
-
-def seq_scores_back(dscore, query_now, keys_now, relative, head_bias, differ):
-    scale = query_now.shape[-1] ** (-0.5)
-    dwide = rel_unshift(dscore)
-    dscore_wide = dscore.astype(jnp.float32)
-    dwide_wide = dwide.astype(jnp.float32)
-    key_col = jnp.sum(dscore_wide, 1)
-    rel_col = jnp.sum(dwide_wide, 1)
-    seg_zero = jnp.sum(dscore_wide * (1.0 - differ)[None], -1)
-    seg_one = jnp.sum(dscore_wide * differ[None], -1)
-    dquery = (
-        jnp.einsum("hij,jhd->ihd", dscore, keys_now, preferred_element_type=jnp.float32)
-        + jnp.einsum("hip,phd->ihd", dwide, relative, preferred_element_type=jnp.float32)
-        + jnp.einsum("hi,hd->ihd", seg_zero, head_bias[3], precision=HIGH_PRECISION)
-        + jnp.einsum("hi,hd->ihd", seg_one, head_bias[4], precision=HIGH_PRECISION)
-    )
-    dkeys = jnp.einsum(
-        "hij,ihd->jhd", dscore, query_now, preferred_element_type=jnp.float32
-    ) + jnp.einsum("hj,hd->jhd", key_col, head_bias[0], precision=HIGH_PRECISION)
-    drelative = jnp.einsum(
-        "hip,ihd->phd", dwide, query_now, preferred_element_type=jnp.float32
-    ) + jnp.einsum("hp,hd->phd", rel_col, head_bias[1], precision=HIGH_PRECISION)
-    shifted = query_now.astype(jnp.float32) + head_bias[2]
-    dheads = jnp.stack(
+    counts = doc_lengths.shape[1]
+    earlier = jnp.arange(counts)[:, None] <= jnp.arange(counts)[None, :]
+    ends = jnp.sum(jnp.where(earlier[None], doc_lengths[:, :, None], 0), 1)
+    start = jnp.sum(jnp.where(doc_lengths == length // 2, ends - doc_lengths, 0), -1)
+    token = (places[None] + start[:, None]) % length
+    document = jnp.sum((token[:, :, None] >= ends[:, None, :]).astype(jnp.int32), -1)
+    ranking = jnp.sum(
+        jnp.where(factor_order[:, :, None] == token[:, None, :], places[None, :, None], 0), 1
+    )
+    segment = jnp.sum(
+        jnp.where(places[None, :, None] == token[:, None, :], segment_ids[:, :, None], 0), 1
+    )
+    base = document * length
+    zero = jnp.zeros_like(base)
+    facts = jnp.stack([base + ranking, base, segment, token, zero, zero, zero, zero], 1)
+    facts = facts.astype(jnp.float32)
+    return facts, jnp.swapaxes(facts, 1, 2)
+
+
+def roll_matrix(token_col, length):
+    lanes = lax.broadcasted_iota(jnp.int32, (length, length), 1).astype(jnp.float32)
+    return jnp.where(token_col == lanes, 1.0, 0.0).astype(jnp.bfloat16)
+
+
+def unroll_matrix(token_row, length):
+    places = lax.broadcasted_iota(jnp.int32, (length, length), 0).astype(jnp.float32)
+    return jnp.where(token_row == places, 1.0, 0.0).astype(jnp.bfloat16)
+
+
+def write_masks(mask_ref, facts_row, facts_col, half):
+    for block in range(2):
+        part = slice(block * half, (block + 1) * half)
+        code_i, base_i = facts_col[part, 0:1], facts_col[part, 1:2]
+        code_j = facts_row[0:1, part]
+        same = code_j >= base_i
+        mask_ref[0, block] = jnp.where(same & (code_j <= code_i), 0.0, MASKED_SCORE)
+        mask_ref[1, block] = jnp.where(same & (code_j < code_i), 0.0, MASKED_SCORE)
+
+
+def query_sides(query, bias, segment_col, factor):
+    wide = query.astype(jnp.float32)
+    with_u = split_pair((wide + bias[0]) * factor)
+    with_w = split_pair((wide + bias[1]) * factor)
+    with_c = wide + bias[2]
+    same = jnp.sum(with_c * bias[3], -1, keepdims=True) * factor
+    change = jnp.sum(with_c * (bias[4] - bias[3]), -1, keepdims=True) * factor
+    return with_u, with_w, with_c, same + change * segment_col, change * (1.0 - 2.0 * segment_col)
+
+
+def block_scores(with_u, with_w, keys_twice, relative_twice, half):
+    content = dot_nt(with_u, keys_twice)
+    position = dot_nt(with_w, relative_twice)
+    return content + pltpu.roll(position, half, 1, stride=1, stride_axis=0)[:, :half]
+
+
+def attention_forward_kernel(
+    head_size, content_ref, query_ref, weight_ref, table_ref, bias_ref, row_ref, col_ref,
+    proj_ref, mixed_ref, logsum_ref, relative_ref, mask_ref,
+):
+    length = content_ref.shape[0]
+    half = length // 2
+    width = weight_ref.shape[-1]
+    heads = width // head_size
+    factor = head_size ** (-0.5) * LOG2E
+
+    @pl.when(pl.program_id(0) == 0)
+    def _():
+        relative_ref[...] = dot(table_ref[...], weight_ref[3]).astype(jnp.bfloat16)
+
+    facts_row, facts_col = row_ref[0], col_ref[0]
+    write_masks(mask_ref, facts_row, facts_col, half)
+    roll = roll_matrix(facts_col[:, 3:4], length)
+    unroll = unroll_matrix(facts_row[3:4, :], length)
+    content, query = content_ref[...], query_ref[...]
+    joined = jnp.concatenate(
         [
-            jnp.einsum(
-                "hj,jhd->hd", key_col, keys_now.astype(jnp.float32), precision=HIGH_PRECISION
-            ),
-            jnp.einsum(
-                "hp,phd->hd", rel_col, relative.astype(jnp.float32), precision=HIGH_PRECISION
-            ),
-            jnp.sum(seg_zero, 1)[:, None] * head_bias[3]
-            + jnp.sum(seg_one, 1)[:, None] * head_bias[4],
-            jnp.einsum("hi,ihd->hd", seg_zero, shifted, precision=HIGH_PRECISION),
-            jnp.einsum("hi,ihd->hd", seg_one, shifted, precision=HIGH_PRECISION),
-        ]
-    )
-    return (dquery * scale, dkeys * scale, drelative * scale, dheads * scale)
+            dot(content, weight_ref[0]).astype(jnp.bfloat16),
+            dot(content, weight_ref[1]).astype(jnp.bfloat16),
+            dot(content, weight_ref[2]).astype(jnp.bfloat16),
+            dot(query, weight_ref[0]).astype(jnp.bfloat16),
+        ],
+        -1,
+    )
+    proj_ref[0] = dot(roll, joined).astype(jnp.bfloat16)
+    segment_col, segment_row = facts_col[:, 2:3], facts_row[2:3, :]
+    mixed = [[None] * heads, [None] * heads]
+    for head in range(heads):
+        cols = lambda kind: slice(kind * width + head * head_size, kind * width + (head + 1) * head_size)
+        bias = [bias_ref[kind : kind + 1, head * head_size : (head + 1) * head_size] for kind in range(5)]
+        keys, values = proj_ref[0, :, cols(1)], proj_ref[0, :, cols(2)]
+        keys_twice = jnp.concatenate([keys, keys], -1)
+        relative = relative_ref[:, head * head_size : (head + 1) * head_size]
+        relative_twice = jnp.concatenate([relative, relative], -1)
+        for stream in range(2):
+            with_u, with_w, _, own, slope = query_sides(
+                proj_ref[0, :, cols(3 * stream)], bias, segment_col, factor
+            )
+            pieces = []
+            for block in range(2):
+                part = slice(block * half, (block + 1) * half)
+                scores = block_scores(
+                    with_u[part], with_w[part], keys_twice[part], relative_twice, half
+                )
+                scores = scores + own[part] + slope[part] * segment_row[:, part] + mask_ref[stream, block]
+                highest = jnp.maximum(jnp.max(scores, -1, keepdims=True), 0.0)
+                weights = jnp.exp2(scores - highest)
+                totals = jnp.exp2(-highest) + jnp.sum(weights, -1, keepdims=True)
+                pieces.append(dot(weights.astype(jnp.bfloat16), values[part]) / totals)
+                index = stream * heads + head
+                logsum_ref[0, part, index : index + 1] = highest + jnp.log2(totals)
+            mixed[stream][head] = jnp.concatenate(pieces, 0).astype(jnp.bfloat16)
+    both = jnp.concatenate(mixed[0] + mixed[1], -1)
+    both = dot(unroll, both).astype(jnp.bfloat16)
+    mixed_ref[0] = both[:, :width]
+    mixed_ref[1] = both[:, width:]
+
+
+def attention_forward(content_rows, query_rows, projection, table, head_bias, facts):
+    rows, length = facts[0].shape[0], facts[0].shape[2]
+    tokens, depth = content_rows.shape
+    width = projection.shape[-1]
+    head_size = head_bias.shape[-1]
+    half = length // 2
+    full = lambda *shape: pl.BlockSpec(shape, lambda r: (0,) * len(shape))
+    return pl.pallas_call(
+        functools.partial(attention_forward_kernel, head_size),
+        grid=(rows,),
+        in_specs=[
+            pl.BlockSpec((length, depth), lambda r: (r, 0)),
+            pl.BlockSpec((length, depth), lambda r: (r, 0)),
+            full(4, depth, width),
+            full(length, depth),
+            full(5, width),
+            pl.BlockSpec((1, 8, length), lambda r: (r, 0, 0)),
+            pl.BlockSpec((1, length, 8), lambda r: (r, 0, 0)),
+        ],
+        out_specs=[
+            pl.BlockSpec((1, length, 4 * width), lambda r: (r, 0, 0)),
+            pl.BlockSpec((2, length, width), lambda r: (0, r, 0)),
+            pl.BlockSpec((1, length, 8), lambda r: (r, 0, 0)),
+        ],
+        out_shape=[
+            jax.ShapeDtypeStruct((rows, length, 4 * width), jnp.bfloat16),
+            jax.ShapeDtypeStruct((2, tokens, width), jnp.bfloat16),
+            jax.ShapeDtypeStruct((rows, length, 8), jnp.float32),
+        ],
+        scratch_shapes=[
+            pltpu.VMEM((length, width), jnp.bfloat16),
+            pltpu.VMEM((2, 2, half, half), jnp.float32),
+        ],
+        compiler_params=pltpu.CompilerParams(vmem_limit_bytes=VMEM_LIMIT),
+    )(content_rows, query_rows, projection, table, head_bias.reshape(5, width), *facts)
+
+
+def attention_backward_kernel(
+    head_size, content_ref, query_ref, weight_ref, table_ref, turned_ref, bias_ref, row_ref, col_ref,
+    proj_ref, logsum_ref, upper_ref,
+    dinput_ref, dweight_ref, dhead_ref,
+    relative_ref, backward_ref, mask_ref, drel_ref, dcols_ref, dkeys_ref, dvalues_ref,
+):
+    length = content_ref.shape[0]
+    half = length // 2
+    width = weight_ref.shape[-1]
+    heads = width // head_size
+    scale = head_size ** (-0.5)
+    factor = scale * LOG2E
+    row = pl.program_id(0)
+
+    @pl.when(row == 0)
+    def _():
+        relative_ref[...] = dot(table_ref[...], weight_ref[3]).astype(jnp.bfloat16)
+        backward_ref[...] = dot(turned_ref[...], weight_ref[3]).astype(jnp.bfloat16)
+        drel_ref[...] = jnp.zeros_like(drel_ref)
+        dweight_ref[...] = jnp.zeros_like(dweight_ref)
+        dhead_ref[...] = jnp.zeros_like(dhead_ref)
+
+    facts_row, facts_col = row_ref[0], col_ref[0]
+    write_masks(mask_ref, facts_row, facts_col, half)
+    roll = roll_matrix(facts_col[:, 3:4], length)
+    upper = dot(roll, jnp.concatenate([upper_ref[0], upper_ref[1]], -1)).astype(jnp.bfloat16)
+    segment_col, segment_row = facts_col[:, 2:3], facts_row[2:3, :]
+    down = lax.broadcasted_iota(jnp.int32, (half, half), 0)
+    along = lax.broadcasted_iota(jnp.int32, (half, half), 1)
+    mirror = jnp.where(down + along == half - 1, 1.0, 0.0).astype(jnp.bfloat16)
+    lane = lax.broadcasted_iota(jnp.int32, (length, head_size), 1)
+    extra = jnp.where(lane == 0, segment_col, jnp.where(lane == 1, 1.0, 0.0)).astype(jnp.bfloat16)
+    for head in range(heads):
+        own_cols = slice(head * head_size, (head + 1) * head_size)
+        cols = lambda kind: slice(kind * width + head * head_size, kind * width + (head + 1) * head_size)
+        bias = [bias_ref[kind : kind + 1, own_cols] for kind in range(5)]
+        keys, values = proj_ref[0, :, cols(1)], proj_ref[0, :, cols(2)]
+        keys_twice = jnp.concatenate([keys, keys], -1)
+        keys_extra = jnp.concatenate([keys, extra], -1)
+        relative = relative_ref[:, own_cols]
+        relative_twice = jnp.concatenate([relative, relative], -1)
+        backward = backward_ref[:, own_cols]
+        heads_sums = [jnp.zeros((1, head_size), jnp.float32) for _ in range(5)]
+        for stream in range(2):
+            with_u, with_w, with_c, own, slope = query_sides(
+                proj_ref[0, :, cols(3 * stream)], bias, segment_col, factor
+            )
+            index = stream * heads + head
+            own = own - logsum_ref[0, :, index : index + 1]
+            upper_now = upper[:, index * head_size : (index + 1) * head_size]
+            with_u_t, with_w_t, upper_t = with_u.T, with_w.T, upper_now.T
+            dquery = []
+            for block in range(2):
+                part = slice(block * half, (block + 1) * half)
+                scores = block_scores(
+                    with_u[part], with_w[part], keys_twice[part], relative_twice, half
+                )
+                scores = scores + own[part] + slope[part] * segment_row[:, part] + mask_ref[stream, block]
+                chances = jnp.exp2(scores)
+                dchance = dot_nt(upper_now[part], values[part])
+                centre = jnp.sum(chances * dchance, -1, keepdims=True)
+                dscore = (chances * (dchance - centre)).astype(jnp.bfloat16)
+                dvalue_part = dot(upper_t[:, part], chances.astype(jnp.bfloat16))
+                by_key = dot(dscore, keys_extra[part])
+                turned = dot(dscore, mirror)
+                wide = pltpu.roll(
+                    jnp.concatenate([turned, jnp.zeros((half, half), jnp.float32)], -1),
+                    0, 1, stride=1, stride_axis=0,
+                ).astype(jnp.bfloat16)
+                by_place = dot(wide, backward)
+                dkey_part = dot(with_u_t[:, part], dscore)
+                dkey_part = dkey_part[:head_size] + dkey_part[head_size:]
+                drel_part = dot(with_w_t[:, part], wide)
+                drel_ref[own_cols] += drel_part[:head_size] + drel_part[head_size:]
+                if stream == 0:
+                    dkeys_ref[own_cols, part] = dkey_part
+                    dvalues_ref[own_cols, part] = dvalue_part
+                else:
+                    dkeys_ref[own_cols, part] += dkey_part
+                    dvalues_ref[own_cols, part] += dvalue_part
+                with_seg, total = by_key[:, head_size : head_size + 1], by_key[:, head_size + 1 : head_size + 2]
+                seg_i = segment_col[part]
+                seg_one = with_seg + seg_i * (total - 2.0 * with_seg)
+                seg_zero = total - seg_one
+                by_key = by_key[:, :head_size]
+                by_segment = seg_zero * bias[3] + seg_one * bias[4]
+                dquery.append((by_key + by_place + by_segment) * scale)
+                for kind, term in enumerate(
+                    (by_key, by_place, by_segment, seg_zero * with_c[part], seg_one * with_c[part])
+                ):
+                    heads_sums[kind] = heads_sums[kind] + jnp.sum(term, 0, keepdims=True)
+            dcols_ref[:, cols(stream)] = jnp.concatenate(dquery, 0).astype(jnp.bfloat16)
+        for kind in range(5):
+            dhead_ref[kind : kind + 1, own_cols] += heads_sums[kind] * scale
+    dcols_ref[:, 2 * width : 3 * width] = (dkeys_ref[...] * (1.0 / LOG2E)).astype(jnp.bfloat16).T
+    dcols_ref[:, 3 * width :] = dvalues_ref[...].astype(jnp.bfloat16).T
+    unroll = unroll_matrix(facts_row[3:4, :], length)
+    joined = dot(unroll, dcols_ref[...]).astype(jnp.bfloat16)
+    joined_t = joined.T
+    content, query = content_ref[...], query_ref[...]
+    dweight_ref[0] += dot(joined_t[:width], content) + dot(joined_t[width : 2 * width], query)
+    dweight_ref[1] += dot(joined_t[2 * width : 3 * width], content)
+    dweight_ref[2] += dot(joined_t[3 * width :], content)
+    dinput_ref[0] = (
+        dot_nt(joined[:, :width], weight_ref[0])
+        + dot_nt(joined[:, 2 * width : 3 * width], weight_ref[1])
+        + dot_nt(joined[:, 3 * width :], weight_ref[2])
+    ).astype(jnp.bfloat16)
+    dinput_ref[1] = dot_nt(joined[:, width : 2 * width], weight_ref[0]).astype(jnp.bfloat16)
+
+    @pl.when(row == pl.num_programs(0) - 1)
+    def _():
+        drel = drel_ref[...] * (1.0 / LOG2E)
+        high = drel.astype(jnp.bfloat16)
+        low = (drel - high.astype(jnp.float32)).astype(jnp.bfloat16)
+        dweight_ref[3] = dot(high, turned_ref[...]) + dot(low, turned_ref[...])
+
+
+def attention_backward(content_rows, query_rows, projection, tables, head_bias, facts, proj, logsum, upper):
+    rows, length = facts[0].shape[0], facts[0].shape[2]
+    tokens, depth = content_rows.shape
+    width = projection.shape[-1]
+    head_size = head_bias.shape[-1]
+    half = length // 2
+    full = lambda *shape: pl.BlockSpec(shape, lambda r: (0,) * len(shape))
+    return pl.pallas_call(
+        functools.partial(attention_backward_kernel, head_size),
+        grid=(rows,),
+        in_specs=[
+            pl.BlockSpec((length, depth), lambda r: (r, 0)),
+            pl.BlockSpec((length, depth), lambda r: (r, 0)),
+            full(4, depth, width),
+            full(length, depth),
+            full(length, depth),
+            full(5, width),
+            pl.BlockSpec((1, 8, length), lambda r: (r, 0, 0)),
+            pl.BlockSpec((1, length, 8), lambda r: (r, 0, 0)),
+            pl.BlockSpec((1, length, 4 * width), lambda r: (r, 0, 0)),
+            pl.BlockSpec((1, length, 8), lambda r: (r, 0, 0)),
+            pl.BlockSpec((2, length, width), lambda r: (0, r, 0)),
+        ],
+        out_specs=[
+            pl.BlockSpec((2, length, depth), lambda r: (0, r, 0)),
+            full(4, width, depth),
+            full(5, width),
+        ],
+        out_shape=[
+            jax.ShapeDtypeStruct((2, tokens, depth), jnp.bfloat16),
+            jax.ShapeDtypeStruct((4, width, depth), jnp.float32),
+            jax.ShapeDtypeStruct((5, width), jnp.float32),
+        ],
+        scratch_shapes=[
+            pltpu.VMEM((length, width), jnp.bfloat16),
+            pltpu.VMEM((length, width), jnp.bfloat16),
+            pltpu.VMEM((2, 2, half, half), jnp.float32),
+            pltpu.VMEM((width, length), jnp.float32),
+            pltpu.VMEM((length, 4 * width), jnp.bfloat16),
+            pltpu.VMEM((width, length), jnp.float32),
+            pltpu.VMEM((width, length), jnp.float32),
+        ],
+        compiler_params=pltpu.CompilerParams(vmem_limit_bytes=VMEM_LIMIT),
+    )(content_rows, query_rows, projection, *tables, head_bias.reshape(5, width), *facts, proj, logsum, upper)
 
 
 def layer_norm_parts(values, gain_row, bias_row):
@@ -216,10 +434,7 @@
     local_rows, width = content_in.shape
     sequences, length = segment_ids.shape
     local_heads, head_size = (head_bias.shape[1], head_bias.shape[2])
-    head_cols = local_heads * head_size
     hidden_cols = up_bias.shape[0]
-    group_tokens = sequences * length
-    seq_shape = (sequences, length, local_heads, head_size)
     projection, out_weight, up_weight, down_weight = (
         lax.all_gather(attn_proj.astype(jnp.bfloat16), "dp", axis=1, tiled=True),
         lax.all_gather(out_proj.astype(jnp.bfloat16), "dp", axis=1, tiled=True),
@@ -230,43 +445,13 @@
         lax.all_gather(content_in, "heads", axis=0, tiled=True),
         lax.all_gather(query_in, "heads", axis=0, tiled=True),
     )
-    projected = jnp.einsum(
-        "td,kde->kte", content_rows, projection[:3], preferred_element_type=jnp.float32
-    ).astype(jnp.bfloat16)
-    query_g = jnp.dot(query_rows, projection[0], preferred_element_type=jnp.float32).astype(
-        jnp.bfloat16
-    )
-    table = position_table(length, width).astype(jnp.bfloat16)
-    relative = jnp.dot(table, projection[3], preferred_element_type=jnp.float32).astype(
-        jnp.bfloat16
-    )
-    relative = relative.reshape(2 * length, local_heads, head_size)
-    allow_content, allow_query, differ = jax.vmap(pair_masks)(
-        segment_ids, doc_lengths, factor_order
-    )
-    sequence_items = (
-        projected[0].reshape(seq_shape),
-        projected[1].reshape(seq_shape),
-        projected[2].reshape(seq_shape),
-        query_g.reshape(seq_shape),
-        allow_content,
-        allow_query,
-        differ,
-    )
-
-    def forward_sequence(items):
-        query_c, key_s, value_s, query_q, allow_c, allow_q, differ_s = items
-        mixed_c, logsum_c = seq_mix(
-            seq_scores(query_c, key_s, relative, head_bias, differ_s), allow_c, value_s
-        )
-        mixed_q, logsum_q = seq_mix(
-            seq_scores(query_q, key_s, relative, head_bias, differ_s), allow_q, value_s
-        )
-        return (mixed_c, mixed_q, logsum_c, logsum_q)
-
-    mixed_c, mixed_q, logsum_c, logsum_q = lax.map(forward_sequence, sequence_items)
-    attended_c = mixed_c.reshape(group_tokens, head_cols)
-    attended_q = mixed_q.reshape(group_tokens, head_cols)
+    table = position_table(length, width)
+    tables = (jnp.asarray(table), jnp.asarray(table[::-1].copy()))
+    facts = row_facts(segment_ids, doc_lengths, factor_order)
+    proj, mixed, logsum = attention_forward(
+        content_rows, query_rows, projection, tables[0], head_bias, facts
+    )
+    attended_c, attended_q = mixed[0], mixed[1]
     rows_c = attended_c
     rows_q = attended_q
     attention_sum = lax.psum_scatter(
@@ -375,76 +560,14 @@
         "td,ed->te", dattn_q, out_weight, preferred_element_type=jnp.float32
     ).astype(jnp.bfloat16)
 
-    def backward_sequence(items):
-        (
-            query_c,
-            key_s,
-            value_s,
-            query_q,
-            allow_c,
-            allow_q,
-            differ_s,
-            logsum_cs,
-            logsum_qs,
-            upper_c,
-            upper_q,
-        ) = items
-        dscore_c, dvalue_c = seq_mix_back(
-            seq_scores(query_c, key_s, relative, head_bias, differ_s),
-            allow_c,
-            logsum_cs,
-            value_s,
-            upper_c,
-        )
-        dscore_q, dvalue_q = seq_mix_back(
-            seq_scores(query_q, key_s, relative, head_bias, differ_s),
-            allow_q,
-            logsum_qs,
-            value_s,
-            upper_q,
-        )
-        dquery_c, dkey_c, drel_c, dhead_c = seq_scores_back(
-            dscore_c, query_c, key_s, relative, head_bias, differ_s
-        )
-        dquery_q, dkey_q, drel_q, dhead_q = seq_scores_back(
-            dscore_q, query_q, key_s, relative, head_bias, differ_s
-        )
-        return (
-            dquery_c.astype(jnp.bfloat16),
-            (dkey_c + dkey_q).astype(jnp.bfloat16),
-            (dvalue_c + dvalue_q).astype(jnp.bfloat16),
-            dquery_q.astype(jnp.bfloat16),
-            (drel_c + drel_q).astype(jnp.bfloat16),
-            dhead_c + dhead_q,
-        )
-
-    dquery_all, dkey_all, dvalue_all, dquery_g, drel_all, dhead_all = lax.map(
-        backward_sequence,
-        sequence_items
-        + (logsum_c, logsum_q, dmixed_c.reshape(seq_shape), dmixed_q.reshape(seq_shape)),
-    )
-    dstack = jnp.stack(
-        [
-            dquery_all.reshape(group_tokens, head_cols),
-            dkey_all.reshape(group_tokens, head_cols),
-            dvalue_all.reshape(group_tokens, head_cols),
-        ]
-    )
-    dquery_g = dquery_g.reshape(group_tokens, head_cols)
-    drel_sum = jnp.sum(drel_all.astype(jnp.float32), 0).reshape(2 * length, head_cols)
-    head_local = jnp.sum(dhead_all, 0)
-    proj_three = jnp.einsum("td,kte->kde", content_rows, dstack, preferred_element_type=jnp.float32)
-    query_term = jnp.einsum("td,te->de", query_rows, dquery_g, preferred_element_type=jnp.float32)
-    rel_term = jnp.dot(table.astype(jnp.float32).T, drel_sum, precision=HIGH_PRECISION)
-    proj_grad = jnp.stack([proj_three[0] + query_term, proj_three[1], proj_three[2], rel_term])
-    content_part = jnp.einsum(
-        "kte,kde->td", dstack, projection[:3], preferred_element_type=jnp.float32
-    )
-    query_part = jnp.einsum(
-        "te,de->td", dquery_g, projection[0], preferred_element_type=jnp.float32
-    )
+    dinput, dweight, head_local = attention_backward(
+        content_rows, query_rows, projection, tables, head_bias, facts, proj, logsum,
+        jnp.stack([dmixed_c, dmixed_q]),
+    )
+    head_local = head_local.reshape(head_bias.shape)
+    proj_grad = jnp.swapaxes(dweight, 1, 2)
     input_back = lax.psum_scatter(
-        jnp.concatenate([content_part, query_part], 1).astype(jnp.bfloat16),
+        jnp.concatenate([dinput[0], dinput[1]], 1),
         "heads",
         scatter_dimension=0,
         tiled=True,

time: 2130 us -> 988 us (0.46)
  local copies, waits for them, and re-layouts: 605 us -> 26.2 us
  other arithmetic: 593 us -> 57.7 us
  matrix products: 302 us -> 75.8 us
  Pallas kernels: 0 us -> 113 us
  waiting for transfers between devices: 444 us -> 557 us
  loops' own time: 38.4 us -> 0 us
    select_n x81 -> x1, other arithmetic: 473 us -> 0.08 us  [row_facts(): token = (places[None] + start[:, None]) % length]
    slice x189 -> x0, local copies, waits for them, and re-layouts: 401 us -> none  [the longest x120 390 us: rel_shift(): moved = jnp.concatenate([shifted[..., step:], filler], -1)]
    dot_general x117 -> x0, matrix products: 227 us -> none  [the longest x12 38 us: seq_scores(): jnp.einsum('ihd,jhd->hij', query_now, keys_now, preferred_element_type=jn...]
    pallas_call x0 -> x2, Pallas kernels: none -> 113 us  [the longest x1 63.6 us: attention_backward(): pl.pallas_call(functools.partial(attention_backward_kernel, head_size), g...]
    while x517 -> x0, local copies, waits for them, and re-layouts: 97.1 us -> none
    reduce_scatter x0 -> x3, waiting for transfers between devices: none -> 84.1 us  [the longest x1 47.9 us: local(): lax.psum_scatter(jnp.concatenate([jnp.einsum('tf,df->td', rows_c, up_weig...]
    reduce_scatter x1, waiting for transfers between devices: 0.01 us -> 58.1 us  [local(): lax.psum_scatter(up_grad, 'dp', scatter_dimension=0, tiled=True)]
    unnamed x24 -> x21, waiting for transfers between devices: 146 us -> 91.2 us
  transfers between devices with their start and end apart: 19 -> 19, of which waited for: 14 -> 17; matrix products, arithmetic and copies ran while one was open for 39% -> 10% of each run, Pallas kernels for 0% -> 7%
where the time goes in v1:
time: 988 us; the launch traced here: 978 us
  waiting for transfers between devices  557 us (56%)
  blocking collectives  114 us (12%)
  Pallas kernels  113 us (11%)
  matrix products  75.8 us (8%)
  other arithmetic  57.7 us (6%)
  local copies, waits for them, and re-layouts  26.2 us (3%)
  between operations  22 us (2%)
  starting transfers between devices  11.7 us (1%)
    unnamed x21, waiting for transfers between devices  91.2 us
    reduce_scatter x1, waiting for transfers between devices, local(): lax.psum_scatter(jnp.concatenate([jnp.dot(rows_c, out_weight, preferred_e...  76.2 us
    pallas_call x1, Pallas kernels, attention_backward(): pl.pallas_call(functools.partial(attention_backward_kernel, head_size), g...  63.6 us
    reduce_scatter x1, waiting for transfers between devices, local(): lax.psum_scatter(up_grad, 'dp', scatter_dimension=0, tiled=True)  58.1 us
    pallas_call x1, Pallas kernels, attention_forward(): pl.pallas_call(functools.partial(attention_forward_kernel, head_size), gr...  49.6 us
    reduce_scatter x1, waiting for transfers between devices, local(): lax.psum_scatter(jnp.concatenate([jnp.einsum('tf,df->td', rows_c, up_weig...  47.9 us
    psum x1, blocking collectives, local(): lax.psum((head_full, bias_full, norm_local), ('dp', 'heads'))  40.8 us
    psum x1, blocking collectives, local(): grad_norm = jnp.sqrt(lax.psum(local_squares, ('dp', 'heads')))  39.8 us
  transfers between devices with their start and end apart: 19, of which 17 were waited for; matrix products, arithmetic and copies ran while one was open for 10% of the time, Pallas kernels for 7%

profile of v1, /device:TPU:0, one launch (start us, length us, event | category | flops | bytes accessed | tf_op | source)
XLA Modules:
  0.0 977.5 jit_solution(2032128644326416147)
XLA Ops:
  16.9 33.6 %all_gather.39 = bf16[192,768]{0,1:T(8,128)(2,1)S(1)} all-gather(bf16[192,96]{0,1:T(8,128)(2,1)S(1)} %copy.154), channel_id=1, replica_groups=mesh['dp'=8,'heads'=4] {'dp'}, dimensions={1}, use_global_device_ids=true | all-gather | bytes 331776 | tf_op jit(solution)/shard_map/all_gather | solution.py:440
  50.5 8.8 all-gather.16.cloned.1.call-done.weight_ref
  59.3 25.0 %all-gather.12.cloned.1.call-done.content_ref = bf16[1536,768]{1,0:T(8,128)(2,1)} async-done(((bf16[384,768]{1,0:T(8,128)(2,1)}), bf16[1536,768]{1,0:T(8,128)(2,1)}) %all-gather.12.cloned.1.call-update) | async-done | bytes 2359312 | tf_op jit(solution)/shard_map/all_gather | solution.py:445
  84.3 25.7 %all-gather.14.cloned.1.call-done.query_ref = bf16[1536,768]{1,0:T(8,128)(2,1)} async-done(((bf16[384,768]{1,0:T(8,128)(2,1)}), bf16[1536,768]{1,0:T(8,128)(2,1)}) %all-gather.14.cloned.1.call-update) | async-done | bytes 2359312 | tf_op jit(solution)/shard_map/all_gather | solution.py:446
  110.0 49.6 %shard_map.541 = (bf16[3,512,768]{2,1,0:T(8,128)(2,1)}, bf16[2,1536,192]{2,1,0:T(8,128)(2,1)}, f32[3,512,8]{2,1,0:T(8,128)}) custom-call(bf16[1536,768]{1,0:T(8,128)(2,1)} %all-gather.12.cloned.1.call-done.content_ref, bf16[1536,768]{1,0:T(8,128)(2,1)} %all-gather.14.cloned.1.call-done.query_ref, ...), custom_call_target="tpu_custom_call" | custom-call | tf_op jit(solution)/shard_map/pallas_call | solution.py:177
  159.6 2.1 fusion.35
  162.5 4.8 pad_maximum_fusion
  169.7 76.2 %reduce-scatter.13.cloned.1.call-done = f32[384,1536]{1,0:T(8,128)} async-done(((f32[1536,1536]{1,0:T(8,128)}), f32[384,1536]{1,0:T(8,128)}) %reduce-scatter.13.cloned.1.call-update) | async-done | bytes 2359312 | tf_op jit(solution)/shard_map/reduce_scatter | solution.py:457
  251.5 38.1 %all-gather.20.cloned.1.call-done = bf16[768,768]{1,0:T(8,128)(2,1)} async-done(((bf16[96,768]{1,0:T(8,128)(2,1)}), bf16[768,768]{1,0:T(8,128)(2,1)}) %all-gather.20.cloned.1.call-update) | async-done | bytes 1179664 | tf_op jit(solution)/shard_map/all_gather | solution.py:441
  289.6 24.9 %all-gather.24.cloned.1.call-done = bf16[1536,768]{1,0:T(8,128)(2,1)} async-done(((bf16[384,768]{1,0:T(8,128)(2,1)}), bf16[1536,768]{1,0:T(8,128)(2,1)}) %all-gather.24.cloned.1.call-update) | async-done | bytes 2359312 | tf_op jit(solution)/shard_map/all_gather | solution.py:477
  314.5 6.1 fusion.77
  320.6 20.1 %all-gather.18.cloned.1.call-done = bf16[1536,768]{1,0:T(8,128)(2,1)} async-done(((bf16[384,768]{1,0:T(8,128)(2,1)}), bf16[1536,768]{1,0:T(8,128)(2,1)}) %all-gather.18.cloned.1.call-update) | async-done | bytes 2359312 | tf_op jit(solution)/shard_map/all_gather | solution.py:476
  340.7 6.2 fusion.76
  346.9 37.7 %all-gather.22.cloned.1.call-done = bf16[768,768]{0,1:T(8,128)(2,1)} async-done(((bf16[768,96]{0,1:T(8,128)(2,1)}), bf16[768,768]{0,1:T(8,128)(2,1)}) %all-gather.22.cloned.1.call-update) | async-done | bytes 1179664 | tf_op jit(solution)/shard_map/all_gather | solution.py:442
  384.6 5.9 convolution_convert_fusion.2
  390.5 3.1 convolution_convert_fusion.3
  393.6 2.6 pad_maximum_fusion.1
  396.2 10.5 %all-gather.28.cloned.1.call-start = ((), (), s32[]{:S(2)}) async-start(), calls=%async_computation.18 | async-start | bytes 2949120 | tf_op jit(solution)/shard_map/all_gather | solution.py:512
  406.8 36.2 %reduce-scatter.15.cloned.1.call-done = bf16[384,1536]{1,0:T(8,128)(2,1)} async-done(((bf16[1536,1536]{1,0:T(8,128)(2,1)}), bf16[384,1536]{1,0:T(8,128)(2,1)}) %reduce-scatter.15.cloned.1.call-update) | async-done | bytes 1179664 | tf_op jit(solution)/shard_map/reduce_scatter | solution.py:485
  448.4 2.5 fusion.64
  453.8 23.2 %all-gather.28.cloned.1.call-done = bf16[1536,768]{1,0:T(8,128)(2,1)} async-done(((bf16[384,768]{1,0:T(8,128)(2,1)}), bf16[1536,768]{1,0:T(8,128)(2,1)}) %all-gather.28.cloned.1.call-update) | async-done | bytes 2359312 | tf_op jit(solution)/shard_map/all_gather | solution.py:512
  477.1 6.2 fusion.78
  483.3 19.5 %all-gather.26.cloned.1.call-done = bf16[1536,768]{1,0:T(8,128)(2,1)} async-done(((bf16[384,768]{1,0:T(8,128)(2,1)}), bf16[1536,768]{1,0:T(8,128)(2,1)}) %all-gather.26.cloned.1.call-update) | async-done | bytes 2359312 | tf_op jit(solution)/shard_map/all_gather | solution.py:511
  502.8 13.1 %convert_reduce_fusion.1 = (f32[768]{0:T(1024)}, bf16[1536,768]{1,0:T(8,128)(2,1)S(1)}, f32[768]{0:T(1024)}, bf16[1536,768]{1,0:T(8,128)(2,1)S(1)}) fusion(f32[1536,768]{1,0:T(8,128)} %fusion.76, f32[768]{0:T(1024)} %param.52, f32[1536,768]{1,0:T(8,128)} %fusion.78, f32[1536,768]{1,0:T(8,128)} %fusion.77, ...), kind=kOutput, calls=%fused_computation.23 | convolution fusion | flops 1866201600 | bytes 22422528 | tf_op jit(solution)/shard_map/td,fd->tf/dot_general | solution.py:518
  515.9 2.0 convolution_convert_fusion.1
  520.2 2.6 pad_maximum_fusion.2
  522.9 47.9 %reduce-scatter.17.cloned.1.call-done = bf16[384,1536]{1,0:T(8,128)(2,1)} async-done(((bf16[1536,1536]{1,0:T(8,128)(2,1)}), bf16[384,1536]{1,0:T(8,128)(2,1)}) %reduce-scatter.17.cloned.1.call-update) | async-done | bytes 1179664 | tf_op jit(solution)/shard_map/reduce_scatter | solution.py:531
  572.5 2.6 multiply_reduce_fusion
  575.2 2.2 fusion.69
  578.5 5.9 fusion.54
  584.4 6.8 convolution_add_fusion
  592.9 3.9 fusion.79
  596.8 3.6 convolution_add_fusion.1
  601.9 2.3 fusion.37
  604.2 23.0 %all-gather.32.cloned.1.call-done = bf16[1536,768]{1,0:T(8,128)(2,1)} async-done(((bf16[384,768]{1,0:T(8,128)(2,1)}), bf16[1536,768]{1,0:T(8,128)(2,1)}) %all-gather.32.cloned.1.call-update) | async-done | bytes 2359312 | tf_op jit(solution)/shard_map/all_gather | solution.py:551
  627.2 2.3 convolution_add_fusion.2
  630.8 2.6 fusion.14
  635.8 63.6 %shard_map.542 = (bf16[2,1536,768]{2,1,0:T(8,128)(2,1)}, f32[4,192,768]{2,1,0:T(8,128)}, f32[5,192]{1,0:T(8,128)}) custom-call(bf16[1536,768]{1,0:T(8,128)(2,1)} %all-gather.12.cloned.1.call-done.content_ref, bf16[1536,768]{1,0:T(8,128)(2,1)} %all-gather.14.cloned.1.call-done.query_ref, bf16[4,768,192]{2,1,0:T(8,128)(2,1)} %all-gather.16.cloned.1.call-done.weight_ref, ...), custom_call_target="tpu_custom_call" | custom-call | tf_op jit(solution)/shard_map/pallas_call | solution.py:332
  699.4 3.1 copy.179
  702.5 3.1 reshape.346
  705.7 2.7 slice_bitcast_fusion.1
  708.4 2.5 pad_maximum_fusion.3
  714.2 58.1 %reduce-scatter.21.cloned.1.call-done = f32[96,768]{1,0:T(8,128)} async-done(((f32[768,768]{1,0:T(8,128)}), f32[96,768]{1,0:T(8,128)}) %reduce-scatter.21.cloned.1.call-update) | async-done | bytes 294928 | tf_op jit(solution)/shard_map/reduce_scatter | solution.py:580
  774.3 40.8 %all-reduce = (f32[5,12,64]{2,1,0:T(8,128)S(1)}, f32[3072]{0:T(1024)S(1)}, f32[5,768]{1,0:T(8,128)S(1)}) all-reduce(f32[5,12,64]{2,1,0:T(8,128)S(1)} %dynamic_update_slice.6, f32[3072]{0:T(1024)S(1)} %add_dynamic-update-slice_fusion, f32[5,768]{1,0:T(8,128)S(1)} %stack.35), channel_id=1, replica_groups=mesh['dp'=8,'heads'=4] {'dp','heads'}, use_global_device_ids=true, to_apply=%region_33.34 | all-reduce | flops 10752 | bytes 86016 | tf_op jit(solution)/shard_map/psum | solution.py:592
  818.9 18.2 %reduce-scatter.27.cloned.1.call-done = f32[96,192]{1,0:T(8,128)} async-done(((f32[768,192]{1,0:T(8,128)}), f32[96,192]{1,0:T(8,128)}) %reduce-scatter.27.cloned.1.call-update) | async-done | bytes 73744
  838.7 70.2 %reduce-scatter.25.cloned.1.call-done = f32[96,768]{1,0:T(8,128)} async-done(((f32[768,768]{1,0:T(8,128)}), f32[96,768]{1,0:T(8,128)}) %reduce-scatter.25.cloned.1.call-update) | async-done | bytes 294928
  913.9 39.8 %psum.31 = f32[]{:T(128)} all-reduce(f32[]{:T(128)S(6)} %add.481), channel_id=1, replica_groups=mesh['dp'=8,'heads'=4] {'dp','heads'}, use_global_device_ids=true, to_apply=%region_51.52 | all-reduce | flops 1 | bytes 8 | tf_op jit(solution)/shard_map/psum | solution.py:606
  963.9 2.3 multiply_subtract_fusion.1
  (281 shorter events, 61.6 us)
Async XLA Ops:
  7.2 8.3 copy-start.29
  7.2 52.1 %all-gather.16.cloned.1.call-start = ((), (), s32[]{:S(2)}) async-start(), calls=%async_computation.10 | async-start | bytes 1769472 | tf_op jit(solution)/shard_map/all_gather | solution.py:439
  9.0 75.3 %all-gather.12.cloned.1.call-start = ((), (), s32[]{:S(2)}) async-start(), calls=%async_computation.8 | async-start | bytes 2949120 | tf_op jit(solution)/shard_map/all_gather | solution.py:445
  9.7 100.2 %all-gather.14.cloned.1.call-start = ((), (), s32[]{:S(2)}) async-start(), calls=%async_computation.9 | async-start | bytes 2949120 | tf_op jit(solution)/shard_map/all_gather | solution.py:446
  10.5 235.4 %reduce-scatter.13.cloned.1.call-start = ((), (), s32[]{:S(2)}) async-start(), calls=%async_computation.11 | async-start | bytes 11796480 | tf_op jit(solution)/shard_map/reduce_scatter | solution.py:457
  15.6 94.4 %copy-start.26 = (f32[3,8,512]{2,1,0:T(8,128)}, f32[3,8,512]{2,1,0:T(8,128)S(1)}, u32[]{:S(2)}) copy-start(f32[3,8,512]{2,1,0:T(8,128)S(1)} %convert_element_type.92.row_ref) | copy-start | bytes 147460
  50.5 111.2 %copy-start.4 = (bf16[192,768]{0,1:T(8,128)(2,1)}, bf16[192,768]{0,1:T(8,128)(2,1)S(1)}, u32[]{:S(2)}) copy-start(bf16[192,768]{0,1:T(8,128)(2,1)S(1)} %all_gather.39) | copy-start | bytes 884740
  167.4 78.5 %copy-start.8 = (bf16[384,768]{1,0:T(8,128)(2,1)S(1)}, bf16[384,768]{1,0:T(8,128)(2,1)}, u32[]{:S(2)}) copy-start(bf16[384,768]{1,0:T(8,128)(2,1)} %param.30) | copy-start | bytes 1769476
  167.4 78.5 %copy-start.9 = (bf16[384,768]{1,0:T(8,128)(2,1)S(1)}, bf16[384,768]{1,0:T(8,128)(2,1)}, u32[]{:S(2)}) copy-start(bf16[384,768]{1,0:T(8,128)(2,1)} %param.31) | copy-start | bytes 1769476
  167.4 122.2 %all-gather.20.cloned.1.call-start = ((), (), s32[]{:S(2)}) async-start(), calls=%async_computation.13 | async-start | bytes 1327104 | tf_op jit(solution)/shard_map/all_gather | solution.py:441
  169.0 145.4 %all-gather.24.cloned.1.call-start = ((), (), s32[]{:S(2)}) async-start(), calls=%async_computation.15 | async-start | bytes 2949120 | tf_op jit(solution)/shard_map/all_gather | solution.py:477
  248.4 196.1 %copy-start.40 = (f32[384]{0:T(512)}, f32[384]{0:T(512)S(1)}, u32[]{:S(2)}) copy-start(f32[384]{0:T(512)S(1)} %add_rsqrt_fusion.3) | copy-start | bytes 4612
  250.0 90.7 %all-gather.18.cloned.1.call-start = ((), (), s32[]{:S(2)}) async-start(), calls=%async_computation.12 | async-start | bytes 2949120 | tf_op jit(solution)/shard_map/all_gather | solution.py:476
  250.7 133.8 %all-gather.22.cloned.1.call-start = ((), (), s32[]{:S(2)}) async-start(), calls=%async_computation.14 | async-start | bytes 1327104 | tf_op jit(solution)/shard_map/all_gather | solution.py:442
  251.5 191.5 %reduce-scatter.15.cloned.1.call-start = ((), (), s32[]{:S(2)}) async-start(), calls=%async_computation.16 | async-start | bytes 5898240 | tf_op jit(solution)/shard_map/reduce_scatter | solution.py:485
  320.6 64.0 %copy-start.63 = (f32[768]{0:T(1024)S(1)}, f32[768]{0:T(1024)}, u32[]{:S(2)}) copy-start(f32[768]{0:T(1024)} %param.52) | copy-start | bytes 9220
  396.2 48.3 %copy-start.55 = (f32[768]{0:T(1024)S(1)}, f32[768]{0:T(1024)}, u32[]{:S(2)}) copy-start(f32[768]{0:T(1024)} %get-tuple-element.227) | copy-start | bytes 9220
  396.2 80.8 %all-gather.28.cloned.1.call-start = ((), (), s32[]{:S(2)}) async-start(), calls=%async_computation.18 | async-start | bytes 2949120 | tf_op jit(solution)/shard_map/all_gather | solution.py:512
  452.8 50.0 %all-gather.26.cloned.1.call-start = ((), (), s32[]{:S(2)}) async-start(), calls=%async_computation.17 | async-start | bytes 2949120 | tf_op jit(solution)/shard_map/all_gather | solution.py:511
  453.8 117.1 %reduce-scatter.17.cloned.1.call-start = ((), (), s32[]{:S(2)}) async-start(), calls=%async_computation.19 | async-start | bytes 5898240 | tf_op jit(solution)/shard_map/reduce_scatter | solution.py:531
  502.8 13.1 %copy-start.71 = (bf16[768,768]{1,0:T(8,128)(2,1)S(1)}, bf16[768,768]{1,0:T(8,128)(2,1)}, u32[]{:S(2)}) copy-start(bf16[768,768]{1,0:T(8,128)(2,1)} %all-gather.20.cloned.1.call-done) | copy-start | bytes 3538948
  522.9 78.8 %all-gather.30.cloned.1.call-start = ((), (), s32[]{:S(2)}) async-start(), calls=%async_computation.20 | async-start | bytes 2949120 | tf_op jit(solution)/shard_map/all_gather | solution.py:550
  577.4 49.8 %all-gather.32.cloned.1.call-start = ((), (), s32[]{:S(2)}) async-start(), calls=%async_computation.21 | async-start | bytes 2949120 | tf_op jit(solution)/shard_map/all_gather | solution.py:551
  578.0 134.5 %reduce-scatter.23.cloned.1.call-start = ((), (), s32[]{:S(2)}) async-start(), calls=%async_computation.24 | async-start | bytes 2654208 | tf_op jit(solution)/shard_map/reduce_scatter | solution.py:581
  591.2 181.1 %reduce-scatter.21.cloned.1.call-start = ((), (), s32[]{:S(2)}) async-start(), calls=%async_computation.23 | async-start | bytes 2654208 | tf_op jit(solution)/shard_map/reduce_scatter | solution.py:580
  600.5 236.6 %reduce-scatter.27.cloned.1.call-start = ((), (), s32[]{:S(2)}) async-start(), calls=%async_computation.26 | async-start | bytes 884736
  604.2 26.6 %copy-start.5 = (bf16[192,768]{0,1:T(8,128)(2,1)S(1)}, bf16[192,768]{0,1:T(8,128)(2,1)}, u32[]{:S(2)}) copy-start(bf16[192,768]{0,1:T(8,128)(2,1)} %copy-done.4) | copy-start | bytes 884740
  630.8 278.1 %reduce-scatter.25.cloned.1.call-start = ((), (), s32[]{:S(2)}) async-start(), calls=%async_computation.25 | async-start | bytes 2654208
  705.7 260.5 %reduce-scatter.19.cloned.1.call-start = ((), (), s32[]{:S(2)}) async-start(), calls=%async_computation.22 | async-start | bytes 5898240 | tf_op jit(solution)/shard_map/reduce_scatter | solution.py:569
  711.0 63.0 %copy-start.53 = (f32[768]{0:T(1024)S(1)}, f32[768]{0:T(1024)}, u32[]{:S(2)}) copy-start(f32[768]{0:T(1024)} %get-tuple-element.210) | copy-start | bytes 9220
  711.0 63.0 %copy-start.54 = (f32[768]{0:T(1024)S(1)}, f32[768]{0:T(1024)}, u32[]{:S(2)}) copy-start(f32[768]{0:T(1024)} %get-tuple-element.290) | copy-start | bytes 9220
  711.0 63.0 %copy-start.51 = (f32[768]{0:T(1024)S(1)}, f32[768]{0:T(1024)}, u32[]{:S(2)}) copy-start(f32[768]{0:T(1024)} %get-tuple-element.220) | copy-start | bytes 9220
  711.0 63.0 %copy-start.52 = (f32[768]{0:T(1024)S(1)}, f32[768]{0:T(1024)}, u32[]{:S(2)}) copy-start(f32[768]{0:T(1024)} %get-tuple-element.287) | copy-start | bytes 9220
  711.0 63.0 %copy-start.62 = (f32[5,192]{1,0:T(8,128)S(1)}, f32[5,192]{1,0:T(8,128)}, u32[]{:S(2)}) copy-start(f32[5,192]{1,0:T(8,128)} %get-tuple-element.44) | copy-start | bytes 11524
  711.9 201.8 %copy-start.28 = (f32[4,96,192]{2,1,0:T(8,128)S(1)}, f32[4,96,192]{2,1,0:T(8,128)}, u32[]{:S(2)}) copy-start(f32[4,96,192]{2,1,0:T(8,128)} %param.39) | copy-start | bytes 884740
  815.1 98.6 %copy-start.35 = (f32[5,768]{1,0:T(8,128)}, f32[5,768]{1,0:T(8,128)S(1)}, u32[]{:S(2)}) copy-start(f32[5,768]{1,0:T(8,128)S(1)} %get-tuple-element.235) | copy-start | bytes 46084
  815.1 98.6 %copy-start.39 = (f32[5,12,64]{2,1,0:T(8,128)}, f32[5,12,64]{2,1,0:T(8,128)S(1)}, u32[]{:S(2)}) copy-start(f32[5,12,64]{2,1,0:T(8,128)S(1)} %get-tuple-element.233) | copy-start | bytes 46084
  815.1 98.6 %copy-start.47 = (f32[3072]{0:T(1024)}, f32[3072]{0:T(1024)S(1)}, u32[]{:S(2)}) copy-start(f32[3072]{0:T(1024)S(1)} %get-tuple-element.234) | copy-start | bytes 36868
  838.0 124.0 %copy-start.25 = (f32[192,96]{1,0:T(8,128)}, f32[192,96]{1,0:T(8,128)S(1)}, u32[]{:S(2)}) copy-start(f32[192,96]{1,0:T(8,128)S(1)} %copy.182) | copy-start | bytes 221188
  955.2 6.8 copy-start.30
  955.3 6.8 copy-start.33
  955.7 6.4 copy-start.34
  955.7 7.1 copy-start.20
  955.7 7.1 copy-start.24
  955.7 7.1 copy-start.31
  955.7 7.1 copy-start.32
  956.7 7.2 copy-start.22
  956.7 7.2 copy-start.23
  (45 other events, 125.8 us)
Sparse Core Ops, SparseCore 0:
  10.8 48.4 all-gather.15
  60.9 23.3 all-gather.11
  85.8 24.0 all-gather.13
  167.5 78.3 reduce-scatter.12
  248.5 41.0 all-gather.19
  291.6 22.8 all-gather.23
  316.6 24.0 all-gather.17
  343.5 41.0 all-gather.21
  396.3 46.5 reduce-scatter.14
  452.9 24.0 all-gather.27
  478.7 24.0 all-gather.25
  523.0 47.8 reduce-scatter.16
  577.6 24.0 all-gather.29
  603.1 24.0 all-gather.31
  631.1 68.8 reduce-scatter.22
  703.9 68.3 reduce-scatter.20
  775.5 61.5 reduce-scatter.26
  840.8 68.0 reduce-scatter.24
  911.6 47.6 reduce-scatter.18

commit v2 on v1

--- a/solution.py
+++ b/solution.py
@@ -12,7 +12,6 @@
 STEP = 10
 
 
-HIGH_PRECISION = lax.Precision.HIGHEST
 NORM_EPSILON = 1e-05
 CLIP_NORM = 1.0
 MATRIX_RATE = 0.08
@@ -22,6 +21,8 @@
 ADAM_EPSILON = 1e-08
 WEIGHT_DECAY = 0.01
 MASKED_SCORE = -1e30
+GELU_FACTOR = 0.7978845608028654
+GELU_CUBIC = 0.044715
 LOG2E = 1.4426950408889634
 VMEM_LIMIT = 56 << 20
 
@@ -105,19 +106,87 @@
     return content + pltpu.roll(position, half, 1, stride=1, stride_axis=0)[:, :half]
 
 
-def attention_forward_kernel(
-    head_size, content_ref, query_ref, weight_ref, table_ref, bias_ref, row_ref, col_ref,
-    proj_ref, mixed_ref, logsum_ref, relative_ref, mask_ref,
-):
-    length = content_ref.shape[0]
+def start_pieces(pieces, place, sems, base):
+    copies = []
+    for index, piece in enumerate(pieces):
+        copy = pltpu.make_async_copy(piece, place(index), sems.at[base + index])
+        copy.start()
+        copies.append(copy)
+    return copies
+
+
+def start_inputs(content_pieces, query_pieces, weight_pieces, content_ref, query_ref, weight_ref, sems):
+    heads_here, dp_here = lax.axis_index("heads"), lax.axis_index("dp")
+    tokens, rows = content_pieces[0].shape[0], weight_pieces[0].shape[1]
+
+    def token_place(ref):
+        return lambda k: ref.at[pl.ds(pl.multiple_of((heads_here ^ k) * tokens, tokens), tokens)]
+
+    def weight_place(k):
+        if len(weight_pieces) == 1:
+            return weight_ref
+        return weight_ref.at[:, pl.ds(pl.multiple_of((dp_here ^ k) * rows, rows), rows)]
+
+    copies = start_pieces(weight_pieces, weight_place, sems, 0)
+    base = len(weight_pieces)
+    copies += start_pieces(content_pieces, token_place(content_ref), sems, base)
+    base += len(content_pieces)
+    return copies + start_pieces(query_pieces, token_place(query_ref), sems, base)
+
+
+def greet(axis, masks):
+    barrier = pltpu.get_barrier_semaphore()
+    for mask in masks:
+        pl.semaphore_signal(
+            barrier, inc=1, device_id={axis: lax.axis_index(axis) ^ mask}, device_id_type=pl.DeviceIdType.MESH
+        )
+    pl.semaphore_wait(barrier, len(masks))
+
+
+def send_pieces(full_ref, pieces, send_sems, recv_sems, base):
+    tokens = pieces[0].shape[1]
+    here = lax.axis_index("heads")
+    copies = []
+    for k, piece in enumerate(pieces):
+        part = full_ref.at[:, pl.ds(pl.multiple_of((here ^ k) * tokens, tokens), tokens)]
+        if k == 0:
+            copy = pltpu.make_async_copy(part, piece, send_sems.at[base])
+        else:
+            copy = pltpu.make_async_remote_copy(
+                part, piece, send_sems.at[base + k], recv_sems.at[k],
+                device_id={"heads": here ^ k}, device_id_type=pl.DeviceIdType.MESH,
+            )
+        copy.start()
+        copies.append(copy)
+    for copy in copies:
+        copy.wait()
+
+
+def attention_forward_kernel(head_size, group, parts, *refs):
+    content_pieces, query_pieces, refs = refs[:group], refs[group : 2 * group], refs[2 * group :]
+    weight_pieces, refs = refs[:parts], refs[parts:]
+    table_ref, bias_ref, row_ref, col_ref, proj_ref, logsum_ref = refs[:6]
+    mixed_pieces, refs = refs[6 : 6 + group], refs[6 + group :]
+    content_all, query_all, weight_ref, mixed_ref, relative_ref, mask_ref, sems, recv_sems = refs
+    length = row_ref.shape[2]
     half = length // 2
     width = weight_ref.shape[-1]
     heads = width // head_size
     factor = head_size ** (-0.5) * LOG2E
-
-    @pl.when(pl.program_id(0) == 0)
+    row = pl.program_id(0)
+
+    @pl.when(row == 0)
     def _():
+        copies = start_inputs(
+            content_pieces, query_pieces, weight_pieces, content_all, query_all, weight_ref, sems
+        )
+        greet("heads", range(1, group))
+        for copy in copies:
+            copy.wait()
         relative_ref[...] = dot(table_ref[...], weight_ref[3]).astype(jnp.bfloat16)
+
+    here = pl.ds(pl.multiple_of(row * length, length), length)
+    content_ref, query_ref = content_all.at[here], query_all.at[here]
 
     facts_row, facts_col = row_ref[0], col_ref[0]
     write_masks(mask_ref, facts_row, facts_col, half)
@@ -163,24 +232,29 @@
             mixed[stream][head] = jnp.concatenate(pieces, 0).astype(jnp.bfloat16)
     both = jnp.concatenate(mixed[0] + mixed[1], -1)
     both = dot(unroll, both).astype(jnp.bfloat16)
-    mixed_ref[0] = both[:, :width]
-    mixed_ref[1] = both[:, width:]
-
-
-def attention_forward(content_rows, query_rows, projection, table, head_bias, facts):
+    mixed_ref[0, here] = both[:, :width]
+    mixed_ref[1, here] = both[:, width:]
+
+    @pl.when(row == pl.num_programs(0) - 1)
+    def _():
+        send_pieces(mixed_ref, mixed_pieces, sems, recv_sems, 2 * group + parts)
+
+
+def attention_forward(content_pieces, query_pieces, weight_pieces, table, head_bias, facts):
     rows, length = facts[0].shape[0], facts[0].shape[2]
-    tokens, depth = content_rows.shape
-    width = projection.shape[-1]
+    group, parts = len(content_pieces), len(weight_pieces)
+    own, depth = content_pieces[0].shape
+    tokens = own * group
+    width = weight_pieces[0].shape[-1]
     head_size = head_bias.shape[-1]
     half = length // 2
     full = lambda *shape: pl.BlockSpec(shape, lambda r: (0,) * len(shape))
-    return pl.pallas_call(
-        functools.partial(attention_forward_kernel, head_size),
+    outside = pl.BlockSpec(memory_space=pl.ANY)
+    results = pl.pallas_call(
+        functools.partial(attention_forward_kernel, head_size, group, parts),
         grid=(rows,),
-        in_specs=[
-            pl.BlockSpec((length, depth), lambda r: (r, 0)),
-            pl.BlockSpec((length, depth), lambda r: (r, 0)),
-            full(4, depth, width),
+        in_specs=[outside] * (2 * group + parts)
+        + [
             full(length, depth),
             full(5, width),
             pl.BlockSpec((1, 8, length), lambda r: (r, 0, 0)),
@@ -188,48 +262,75 @@
         ],
         out_specs=[
             pl.BlockSpec((1, length, 4 * width), lambda r: (r, 0, 0)),
-            pl.BlockSpec((2, length, width), lambda r: (0, r, 0)),
             pl.BlockSpec((1, length, 8), lambda r: (r, 0, 0)),
-        ],
+        ]
+        + [outside] * group,
         out_shape=[
             jax.ShapeDtypeStruct((rows, length, 4 * width), jnp.bfloat16),
-            jax.ShapeDtypeStruct((2, tokens, width), jnp.bfloat16),
             jax.ShapeDtypeStruct((rows, length, 8), jnp.float32),
-        ],
+        ]
+        + [jax.ShapeDtypeStruct((2, own, width), jnp.bfloat16)] * group,
         scratch_shapes=[
+            pltpu.VMEM((tokens, depth), jnp.bfloat16),
+            pltpu.VMEM((tokens, depth), jnp.bfloat16),
+            pltpu.VMEM((4, depth, width), jnp.bfloat16),
+            pltpu.VMEM((2, tokens, width), jnp.bfloat16),
             pltpu.VMEM((length, width), jnp.bfloat16),
             pltpu.VMEM((2, 2, half, half), jnp.float32),
+            pltpu.SemaphoreType.DMA((3 * group + parts,)),
+            pltpu.SemaphoreType.DMA((group,)),
         ],
-        compiler_params=pltpu.CompilerParams(vmem_limit_bytes=VMEM_LIMIT),
-    )(content_rows, query_rows, projection, table, head_bias.reshape(5, width), *facts)
-
-
-def attention_backward_kernel(
-    head_size, content_ref, query_ref, weight_ref, table_ref, turned_ref, bias_ref, row_ref, col_ref,
-    proj_ref, logsum_ref, upper_ref,
-    dinput_ref, dweight_ref, dhead_ref,
-    relative_ref, backward_ref, mask_ref, drel_ref, dcols_ref, dkeys_ref, dvalues_ref,
-):
-    length = content_ref.shape[0]
+        compiler_params=pltpu.CompilerParams(
+            vmem_limit_bytes=VMEM_LIMIT, collective_id=0, has_side_effects=True
+        ),
+    )(*content_pieces, *query_pieces, *weight_pieces, table, head_bias.reshape(5, width), *facts)
+    return results[0], results[1], results[2:]
+
+
+def attention_backward_kernel(head_size, group, parts, *refs):
+    content_pieces, query_pieces, refs = refs[:group], refs[group : 2 * group], refs[2 * group :]
+    weight_pieces, refs = refs[:parts], refs[parts:]
+    upper_pieces, refs = refs[:group], refs[group:]
+    table_ref, turned_ref, bias_ref, row_ref, col_ref, proj_ref, logsum_ref = refs[:7]
+    dinput_pieces, refs = refs[7 : 7 + group], refs[7 + group :]
+    dweight_pieces, dhead_ref, refs = refs[:parts], refs[parts], refs[parts + 1 :]
+    content_all, query_all, weight_ref, upper_all, dinput_ref, dweight_ref = refs[:6]
+    relative_ref, backward_ref, mask_ref, drel_ref, dcols_ref, dkeys_ref, dvalues_ref, sems = refs[6:]
+    length = row_ref.shape[2]
     half = length // 2
     width = weight_ref.shape[-1]
     heads = width // head_size
     scale = head_size ** (-0.5)
     factor = scale * LOG2E
     row = pl.program_id(0)
+    heads_here, dp_here = lax.axis_index("heads"), lax.axis_index("dp")
 
     @pl.when(row == 0)
     def _():
+        copies = start_inputs(
+            content_pieces, query_pieces, weight_pieces, content_all, query_all, weight_ref, sems
+        )
+        tokens = upper_pieces[0].shape[1]
+        copies += start_pieces(
+            upper_pieces,
+            lambda k: upper_all.at[:, pl.ds(pl.multiple_of((heads_here ^ k) * tokens, tokens), tokens)],
+            sems,
+            2 * group + parts,
+        )
+        for copy in copies:
+            copy.wait()
         relative_ref[...] = dot(table_ref[...], weight_ref[3]).astype(jnp.bfloat16)
         backward_ref[...] = dot(turned_ref[...], weight_ref[3]).astype(jnp.bfloat16)
         drel_ref[...] = jnp.zeros_like(drel_ref)
         dweight_ref[...] = jnp.zeros_like(dweight_ref)
         dhead_ref[...] = jnp.zeros_like(dhead_ref)
 
+    here = pl.ds(pl.multiple_of(row * length, length), length)
+    content_ref, query_ref = content_all.at[here], query_all.at[here]
     facts_row, facts_col = row_ref[0], col_ref[0]
     write_masks(mask_ref, facts_row, facts_col, half)
     roll = roll_matrix(facts_col[:, 3:4], length)
-    upper = dot(roll, jnp.concatenate([upper_ref[0], upper_ref[1]], -1)).astype(jnp.bfloat16)
+    upper = dot(roll, jnp.concatenate([upper_all[0, here], upper_all[1, here]], -1)).astype(jnp.bfloat16)
     segment_col, segment_row = facts_col[:, 2:3], facts_row[2:3, :]
     down = lax.broadcasted_iota(jnp.int32, (half, half), 0)
     along = lax.broadcasted_iota(jnp.int32, (half, half), 1)
@@ -307,12 +408,12 @@
     dweight_ref[0] += dot(joined_t[:width], content) + dot(joined_t[width : 2 * width], query)
     dweight_ref[1] += dot(joined_t[2 * width : 3 * width], content)
     dweight_ref[2] += dot(joined_t[3 * width :], content)
-    dinput_ref[0] = (
+    dinput_ref[0, here] = (
         dot_nt(joined[:, :width], weight_ref[0])
         + dot_nt(joined[:, 2 * width : 3 * width], weight_ref[1])
         + dot_nt(joined[:, 3 * width :], weight_ref[2])
     ).astype(jnp.bfloat16)
-    dinput_ref[1] = dot_nt(joined[:, width : 2 * width], weight_ref[0]).astype(jnp.bfloat16)
+    dinput_ref[1, here] = dot_nt(joined[:, width : 2 * width], weight_ref[0]).astype(jnp.bfloat16)
 
     @pl.when(row == pl.num_programs(0) - 1)
     def _():
@@ -320,22 +421,34 @@
         high = drel.astype(jnp.bfloat16)
         low = (drel - high.astype(jnp.float32)).astype(jnp.bfloat16)
         dweight_ref[3] = dot(high, turned_ref[...]) + dot(low, turned_ref[...])
-
-
-def attention_backward(content_rows, query_rows, projection, tables, head_bias, facts, proj, logsum, upper):
+        tokens, pick = dinput_pieces[0].shape[1], dweight_pieces[0].shape[1]
+        for k in range(group):
+            part = pl.ds(pl.multiple_of((heads_here ^ k) * tokens, tokens), tokens)
+            dinput_pieces[k][...] = dinput_ref[:, part]
+        for kind in range(4):
+            content_all[: weight_ref.shape[1], :width] = dweight_ref[kind].astype(jnp.bfloat16).T
+            for k in range(parts):
+                start = (dp_here ^ k) * pick if parts > 1 else 0
+                dweight_pieces[k][kind] = content_all[pl.ds(pl.multiple_of(start, pick), pick), :width]
+
+
+def attention_backward(
+    content_pieces, query_pieces, weight_pieces, tables, head_bias, facts, proj, logsum, upper_pieces
+):
     rows, length = facts[0].shape[0], facts[0].shape[2]
-    tokens, depth = content_rows.shape
-    width = projection.shape[-1]
+    group, parts = len(content_pieces), len(weight_pieces)
+    own, depth = content_pieces[0].shape
+    tokens = own * group
+    width = weight_pieces[0].shape[-1]
     head_size = head_bias.shape[-1]
     half = length // 2
     full = lambda *shape: pl.BlockSpec(shape, lambda r: (0,) * len(shape))
-    return pl.pallas_call(
-        functools.partial(attention_backward_kernel, head_size),
+    outside = pl.BlockSpec(memory_space=pl.ANY)
+    results = pl.pallas_call(
+        functools.partial(attention_backward_kernel, head_size, group, parts),
         grid=(rows,),
-        in_specs=[
-            pl.BlockSpec((length, depth), lambda r: (r, 0)),
-            pl.BlockSpec((length, depth), lambda r: (r, 0)),
-            full(4, depth, width),
+        in_specs=[outside] * (3 * group + parts)
+        + [
             full(length, depth),
             full(length, depth),
             full(5, width),
@@ -343,19 +456,20 @@
             pl.BlockSpec((1, length, 8), lambda r: (r, 0, 0)),
             pl.BlockSpec((1, length, 4 * width), lambda r: (r, 0, 0)),
             pl.BlockSpec((1, length, 8), lambda r: (r, 0, 0)),
-            pl.BlockSpec((2, length, width), lambda r: (0, r, 0)),
         ],
-        out_specs=[
-            pl.BlockSpec((2, length, depth), lambda r: (0, r, 0)),
-            full(4, width, depth),
-            full(5, width),
-        ],
-        out_shape=[
-            jax.ShapeDtypeStruct((2, tokens, depth), jnp.bfloat16),
-            jax.ShapeDtypeStruct((4, width, depth), jnp.float32),
-            jax.ShapeDtypeStruct((5, width), jnp.float32),
-        ],
+        out_specs=[full(2, own, depth)] * group
+        + [full(*piece.shape) for piece in weight_pieces]
+        + [full(5, width)],
+        out_shape=[jax.ShapeDtypeStruct((2, own, depth), jnp.bfloat16)] * group
+        + [jax.ShapeDtypeStruct(piece.shape, jnp.bfloat16) for piece in weight_pieces]
+        + [jax.ShapeDtypeStruct((5, width), jnp.float32)],
         scratch_shapes=[
+            pltpu.VMEM((tokens, depth), jnp.bfloat16),
+            pltpu.VMEM((tokens, depth), jnp.bfloat16),
+            pltpu.VMEM((4, depth, width), jnp.bfloat16),
+            pltpu.VMEM((2, tokens, width), jnp.bfloat16),
+            pltpu.VMEM((2, tokens, depth), jnp.bfloat16),
+            pltpu.VMEM((4, width, depth), jnp.float32),
             pltpu.VMEM((length, width), jnp.bfloat16),
             pltpu.VMEM((length, width), jnp.bfloat16),
             pltpu.VMEM((2, 2, half, half), jnp.float32),
@@ -363,29 +477,251 @@
             pltpu.VMEM((length, 4 * width), jnp.bfloat16),
             pltpu.VMEM((width, length), jnp.float32),
             pltpu.VMEM((width, length), jnp.float32),
+            pltpu.SemaphoreType.DMA((3 * group + parts,)),
         ],
         compiler_params=pltpu.CompilerParams(vmem_limit_bytes=VMEM_LIMIT),
-    )(content_rows, query_rows, projection, *tables, head_bias.reshape(5, width), *facts, proj, logsum, upper)
-
-
-def layer_norm_parts(values, gain_row, bias_row):
-    row_mean = jnp.mean(values, -1, keepdims=True)
-    centred = values - row_mean
-    row_var = jnp.mean(centred * centred, -1, keepdims=True)
-    inverse = lax.rsqrt(row_var + NORM_EPSILON)
-    normed = centred * inverse
-    return (normed * gain_row + bias_row, normed, inverse)
-
-
-def layer_norm_back(upstream, normed, inverse, gain_row):
-    scaled = upstream * gain_row
-    first_mean = jnp.mean(scaled, -1, keepdims=True)
-    second_mean = jnp.mean(scaled * normed, -1, keepdims=True)
-    return inverse * (scaled - first_mean - normed * second_mean)
-
-
-def gelu_back(before, upstream):
-    return jax.vjp(lambda inner: jax.nn.gelu(inner, approximate=True), before)[1](upstream)[0]
+    )(
+        *content_pieces, *query_pieces, *weight_pieces, *upper_pieces, *tables,
+        head_bias.reshape(5, width), *facts, proj, logsum,
+    )
+    return results[:group], results[group : group + parts], results[-1]
+
+
+def norm_parts(values):
+    centred = values - jnp.mean(values, -1, keepdims=True)
+    inverse = lax.rsqrt(jnp.mean(centred * centred, -1, keepdims=True) + NORM_EPSILON)
+    return centred * inverse, inverse
+
+
+def norm_back(upstream, normed, inverse, gain):
+    scaled = upstream * gain
+    first = jnp.mean(scaled, -1, keepdims=True)
+    second = jnp.mean(scaled * normed, -1, keepdims=True)
+    return inverse * (scaled - first - normed * second)
+
+
+def column_sum(values):
+    return jnp.sum(values, 0, keepdims=True)
+
+
+def feed_kernel(group, *refs):
+    mixed_pieces, refs = refs[:group], refs[group:]
+    bias_pieces, refs = refs[:group], refs[group:]
+    content_ref, query_ref, dcontent_ref, dquery_ref, norm_ref, up_hbm, down_hbm, out_hbm = refs[:8]
+    content_out, query_out, dresid_ref, refs = refs[8], refs[9], refs[10], refs[11:]
+    dmixed_pieces, refs = refs[:group], refs[group:]
+    dup_hbm, ddown_hbm, dout_ref, dsmall_ref, refs = refs[0], refs[1], refs[2], refs[3], refs[4:]
+    up_ref, down_ref, out_ref, hidden_ref, slope_ref, bias_ref = refs[:6]
+    low_ref, low_t_ref, normed_ref, total_ref, sems = refs[6:]
+    own, depth = content_ref.shape
+    tokens = 2 * own
+    here = lax.axis_index("heads")
+    loads = [
+        pltpu.make_async_copy(out_hbm.at[:, j], out_ref.at[j], sems.at[j]) for j in range(group)
+    ]
+    loads += [
+        pltpu.make_async_copy(up_hbm.at[:, j], up_ref.at[j], sems.at[group + j]) for j in range(group)
+    ]
+    loads += [
+        pltpu.make_async_copy(down_hbm.at[:, j], down_ref.at[j], sems.at[2 * group + j])
+        for j in range(group)
+    ]
+    for load in loads:
+        load.start()
+    for k in range(group):
+        bias_ref[here ^ k] = bias_pieces[k][...]
+    gain_one, bias_one, bias_out, gain_two, bias_two = [norm_ref[i : i + 1] for i in range(5)]
+    for load in loads[:group]:
+        load.wait()
+    hidden = up_ref.shape[-1]
+
+    def out_block(k):
+        return out_ref[here ^ k].reshape(depth, out_ref.shape[-1])
+
+    total = jnp.concatenate([content_ref[...], query_ref[...]], 0).astype(jnp.float32)
+    for k in range(group):
+        total = total + dot_nt(mixed_pieces[k][...].reshape(tokens, -1), out_block(k))
+    normed, inverse_one = norm_parts(total)
+    normed_ref[...] = normed
+    middle = normed * gain_one + bias_one
+    low_ref[...] = middle.astype(jnp.bfloat16)
+    low_t_ref[...] = low_ref[...].T
+    total_ref[...] = middle + bias_out
+    for load in loads[group:]:
+        load.wait()
+
+    def forward(j, carry):
+        before = dot(low_ref[...], up_ref[j].reshape(depth, hidden)) + bias_ref[j]
+        square = before * before
+        bent = jnp.tanh(GELU_FACTOR * before * (1.0 + GELU_CUBIC * square))
+        half_up = 0.5 * (1.0 + bent)
+        hidden_now = (before * half_up).astype(jnp.bfloat16)
+        slope_ref[j] = half_up + 0.5 * before * (1.0 - bent * bent) * GELU_FACTOR * (
+            1.0 + 3.0 * GELU_CUBIC * square
+        )
+        hidden_ref[j] = hidden_now.reshape(hidden_ref.shape[1:])
+        total_ref[...] += dot_nt(hidden_now, down_ref[j].reshape(depth, hidden))
+        return carry
+
+    lax.fori_loop(0, group, forward, 0)
+    normed_two, inverse_two = norm_parts(total_ref[...])
+    result = (normed_two * gain_two + bias_two).astype(jnp.bfloat16)
+    content_out[...] = result[:own]
+    query_out[...] = result[own:]
+    upstream = jnp.concatenate([dcontent_ref[...], dquery_ref[...]], 0).astype(jnp.float32)
+    dsmall_ref[group + 3 : group + 4] = column_sum(upstream * normed_two)
+    dsmall_ref[group + 4 : group + 5] = column_sum(upstream)
+    dfinal = norm_back(upstream, normed_two, inverse_two, gain_two)
+    dsmall_ref[group + 2 : group + 3] = column_sum(dfinal)
+    total_ref[...] = dfinal
+    dlow = dfinal.astype(jnp.bfloat16)
+    dlow_t = dlow.T
+
+    def backward(j, carry):
+        hidden_now = hidden_ref[j].reshape(tokens, hidden)
+        down_now = down_ref[j].reshape(depth, hidden)
+        dhidden = dot(dlow, down_now)
+        down_ref[j] = dot(dlow_t, hidden_now).astype(jnp.bfloat16).reshape(down_ref.shape[1:])
+        dbefore = (dhidden * slope_ref[j]).astype(jnp.bfloat16)
+        dsmall_ref[pl.ds(j, 1)] = column_sum(dbefore.astype(jnp.float32))
+        total_ref[...] += dot_nt(dbefore, up_ref[j].reshape(depth, hidden))
+        up_ref[j] = dot(low_t_ref[...], dbefore).astype(jnp.bfloat16).reshape(up_ref.shape[1:])
+        return carry
+
+    lax.fori_loop(0, group, backward, 0)
+    stores = [
+        pltpu.make_async_copy(up_ref.at[j], dup_hbm.at[:, j], sems.at[group + j]) for j in range(group)
+    ]
+    stores += [
+        pltpu.make_async_copy(down_ref.at[j], ddown_hbm.at[:, j], sems.at[2 * group + j])
+        for j in range(group)
+    ]
+    for store in stores:
+        store.start()
+    dmiddle = total_ref[...]
+    normed = normed_ref[...]
+    dsmall_ref[group : group + 1] = column_sum(dmiddle * normed)
+    dsmall_ref[group + 1 : group + 2] = column_sum(dmiddle)
+    dresid = norm_back(dmiddle, normed, inverse_one, gain_one)
+    dresid_ref[...] = dresid.reshape(dresid_ref.shape)
+    dlow = dresid.astype(jnp.bfloat16)
+    dlow_t = dlow.T
+    for k in range(group):
+        mixed = mixed_pieces[k][...].reshape(tokens, -1)
+        dmixed_pieces[k][...] = (
+            dot(dlow, out_block(k)).astype(jnp.bfloat16).reshape(dmixed_pieces[k].shape)
+        )
+        dout_ref[here ^ k] = dot(dlow_t, mixed).astype(jnp.bfloat16).reshape(dout_ref.shape[1:])
+    dsmall_ref[group + 5 :] = jnp.zeros((dsmall_ref.shape[0] - group - 5, depth), jnp.float32)
+    for store in stores:
+        store.wait()
+
+
+def feed_layer(mixed_pieces, bias_pieces, content, query, dcontent, dquery, norm_param, up, down, out):
+    group = len(mixed_pieces)
+    own, depth = content.shape
+    parts, _, pick, hidden = up.shape
+    width = out.shape[-1]
+    inside = pl.BlockSpec(memory_space=pltpu.VMEM)
+    outside = pl.BlockSpec(memory_space=pl.ANY)
+    tokens = 2 * own
+    results = pl.pallas_call(
+        functools.partial(feed_kernel, group),
+        in_specs=[inside] * (2 * group + 5) + [outside] * 3,
+        out_specs=[inside] * (3 + group) + [outside, outside, inside, inside],
+        out_shape=[
+            jax.ShapeDtypeStruct((own, depth), jnp.bfloat16),
+            jax.ShapeDtypeStruct((own, depth), jnp.bfloat16),
+            jax.ShapeDtypeStruct((2, own, depth), jnp.float32),
+        ]
+        + [jax.ShapeDtypeStruct((2, own, width), jnp.bfloat16)] * group
+        + [
+            jax.ShapeDtypeStruct(up.shape, jnp.bfloat16),
+            jax.ShapeDtypeStruct(down.shape, jnp.bfloat16),
+            jax.ShapeDtypeStruct((group, parts, pick, width), jnp.bfloat16),
+            jax.ShapeDtypeStruct((16, depth), jnp.float32),
+        ],
+        scratch_shapes=[
+            pltpu.VMEM((group, parts, pick, hidden), jnp.bfloat16),
+            pltpu.VMEM((group, parts, pick, hidden), jnp.bfloat16),
+            pltpu.VMEM((group, parts, pick, width), jnp.bfloat16),
+            pltpu.VMEM((group, tokens, hidden), jnp.bfloat16),
+            pltpu.VMEM((group, tokens, hidden), jnp.float32),
+            pltpu.VMEM((group, 1, hidden), jnp.float32),
+            pltpu.VMEM((tokens, depth), jnp.bfloat16),
+            pltpu.VMEM((depth, tokens), jnp.bfloat16),
+            pltpu.VMEM((tokens, depth), jnp.float32),
+            pltpu.VMEM((tokens, depth), jnp.float32),
+            pltpu.SemaphoreType.DMA((3 * group,)),
+        ],
+        compiler_params=pltpu.CompilerParams(vmem_limit_bytes=VMEM_LIMIT),
+    )(*mixed_pieces, *bias_pieces, content, query, dcontent, dquery, norm_param, up, down, out)
+    return results[0], results[1], results[2], results[3 : 3 + group], results[3 + group :]
+
+
+def exchange(value, axis, mask):
+    return lax.ppermute(value, axis, [(i, i ^ mask) for i in range(lax.axis_size(axis))])
+
+
+def total_over(value, axis):
+    mask = 1
+    while mask < lax.axis_size(axis):
+        value = value + exchange(value, axis, mask)
+        mask = 2 * mask
+    return value
+
+
+def gather_heads(own):
+    far = exchange(own, "heads", 2)
+    return [own, exchange(own, "heads", 1), far, exchange(far, "heads", 1)]
+
+
+def spread(pieces):
+    return [pieces[0]] + [exchange(pieces[k], "heads", k) for k in range(1, len(pieces))]
+
+
+def by_pieces(pick):
+    return lax.axis_size("dp") <= 8 and pick % 16 == 0
+
+
+def gather_projection(own):
+    if not by_pieces(own.shape[1]):
+        return [lax.all_gather(own, "dp", axis=1, tiled=True)]
+    pieces = {0: own}
+    mask = lax.axis_size("dp") // 2
+    while mask:
+        for k in sorted(pieces):
+            pieces[k ^ mask] = exchange(pieces[k], "dp", mask)
+        mask = mask // 2
+    return [pieces[k] for k in range(len(pieces))]
+
+
+def reduce_projection(pieces):
+    if len(pieces) == 1:
+        return lax.psum_scatter(pieces[0], "dp", scatter_dimension=1, tiled=True).astype(jnp.float32)
+    total = pieces[0].astype(jnp.float32)
+    for k in range(1, len(pieces)):
+        total = total + exchange(pieces[k], "dp", k).astype(jnp.float32)
+    return total
+
+
+def gather_all(own):
+    dp, heads = lax.axis_size("dp"), lax.axis_size("heads")
+    rows, columns = own.shape
+    full = lax.all_gather(own, ("dp", "heads"), axis=0, tiled=False).reshape(dp, heads, rows, columns)
+    if by_pieces(rows):
+        return full
+    return jnp.swapaxes(full, 0, 1).reshape(1, heads, dp * rows, columns)
+
+
+def scatter_all(full):
+    dp, heads = lax.axis_size("dp"), lax.axis_size("heads")
+    parts, _, rows, columns = full.shape
+    if parts == 1:
+        rows = rows // dp
+        full = jnp.swapaxes(full.reshape(heads, dp, rows, columns), 0, 1)
+    full = full.reshape(dp * heads * rows, columns)
+    return lax.psum_scatter(full, ("dp", "heads"), scatter_dimension=0, tiled=True).astype(jnp.float32)
 
 
 def adam_step(master, first, second, gradient, factor, decayed):
@@ -431,179 +767,54 @@
     norm_param_first,
     norm_param_second,
 ):
-    local_rows, width = content_in.shape
-    sequences, length = segment_ids.shape
+    width = content_in.shape[1]
+    length = segment_ids.shape[1]
     local_heads, head_size = (head_bias.shape[1], head_bias.shape[2])
-    hidden_cols = up_bias.shape[0]
-    projection, out_weight, up_weight, down_weight = (
-        lax.all_gather(attn_proj.astype(jnp.bfloat16), "dp", axis=1, tiled=True),
-        lax.all_gather(out_proj.astype(jnp.bfloat16), "dp", axis=1, tiled=True),
-        lax.all_gather(up_proj.astype(jnp.bfloat16), "dp", axis=0, tiled=True),
-        lax.all_gather(down_proj.astype(jnp.bfloat16), "dp", axis=1, tiled=True),
-    )
-    content_rows, query_rows = (
-        lax.all_gather(content_in, "heads", axis=0, tiled=True),
-        lax.all_gather(query_in, "heads", axis=0, tiled=True),
-    )
+    weight_pieces = gather_projection(attn_proj.astype(jnp.bfloat16))
+    content_pieces = gather_heads(content_in)
+    query_pieces = gather_heads(query_in)
+    bias_pieces = [up_bias[None]] + [exchange(up_bias[None], "heads", k) for k in range(1, 4)]
+    out_full = gather_all(out_proj.T.astype(jnp.bfloat16))
+    up_full = gather_all(up_proj.astype(jnp.bfloat16))
+    down_full = gather_all(down_proj.T.astype(jnp.bfloat16))
     table = position_table(length, width)
     tables = (jnp.asarray(table), jnp.asarray(table[::-1].copy()))
     facts = row_facts(segment_ids, doc_lengths, factor_order)
-    proj, mixed, logsum = attention_forward(
-        content_rows, query_rows, projection, tables[0], head_bias, facts
-    )
-    attended_c, attended_q = mixed[0], mixed[1]
-    rows_c = attended_c
-    rows_q = attended_q
-    attention_sum = lax.psum_scatter(
-        jnp.concatenate(
-            [
-                jnp.dot(rows_c, out_weight, preferred_element_type=jnp.float32),
-                jnp.dot(rows_q, out_weight, preferred_element_type=jnp.float32),
-            ],
-            1,
-        ),
-        "heads",
-        scatter_dimension=0,
-        tiled=True,
-    )
-    middle_c, normed1_c, inverse1_c = layer_norm_parts(
-        content_in.astype(jnp.float32) + attention_sum[:, :width], norm_param[0], norm_param[1]
-    )
-    middle_q, normed1_q, inverse1_q = layer_norm_parts(
-        query_in.astype(jnp.float32) + attention_sum[:, width:], norm_param[0], norm_param[1]
-    )
-    middle_rows_c, middle_rows_q = (
-        lax.all_gather(middle_c.astype(jnp.bfloat16), "heads", axis=0, tiled=True),
-        lax.all_gather(middle_q.astype(jnp.bfloat16), "heads", axis=0, tiled=True),
-    )
-    before_c = jnp.dot(middle_rows_c, up_weight, preferred_element_type=jnp.float32) + up_bias
-    before_q = jnp.dot(middle_rows_q, up_weight, preferred_element_type=jnp.float32) + up_bias
-    hidden_c = jax.nn.gelu(before_c, approximate=True).astype(jnp.bfloat16)
-    hidden_q = jax.nn.gelu(before_q, approximate=True).astype(jnp.bfloat16)
-    rows_c = hidden_c
-    rows_q = hidden_q
-    feed_sum = lax.psum_scatter(
-        jnp.concatenate(
-            [
-                jnp.dot(rows_c, down_weight, preferred_element_type=jnp.float32),
-                jnp.dot(rows_q, down_weight, preferred_element_type=jnp.float32),
-            ],
-            1,
-        ).astype(jnp.bfloat16),
-        "heads",
-        scatter_dimension=0,
-        tiled=True,
-    ).astype(jnp.float32)
-    final_c, normed2_c, inverse2_c = layer_norm_parts(
-        middle_c + feed_sum[:, :width] + norm_param[2], norm_param[3], norm_param[4]
-    )
-    final_q, normed2_q, inverse2_q = layer_norm_parts(
-        middle_q + feed_sum[:, width:] + norm_param[2], norm_param[3], norm_param[4]
-    )
-    upstream_c = content_grad.astype(jnp.float32)
-    upstream_q = query_grad.astype(jnp.float32)
-    dfinal_c = layer_norm_back(upstream_c, normed2_c, inverse2_c, norm_param[3])
-    dfinal_q = layer_norm_back(upstream_q, normed2_q, inverse2_q, norm_param[3])
-    gain2_grad = jnp.sum(upstream_c * normed2_c, 0) + jnp.sum(upstream_q * normed2_q, 0)
-    bias2_grad = jnp.sum(upstream_c, 0) + jnp.sum(upstream_q, 0)
-    outbias_grad = jnp.sum(dfinal_c, 0) + jnp.sum(dfinal_q, 0)
-    back_c, back_q = (
-        lax.all_gather(dfinal_c.astype(jnp.bfloat16), "heads", axis=0, tiled=True),
-        lax.all_gather(dfinal_q.astype(jnp.bfloat16), "heads", axis=0, tiled=True),
-    )
-    down_grad = jnp.einsum(
-        "tf,td->fd", hidden_c, back_c, preferred_element_type=jnp.float32
-    ) + jnp.einsum("tf,td->fd", hidden_q, back_q, preferred_element_type=jnp.float32)
-    dbefore_c = gelu_back(
-        before_c, jnp.einsum("td,fd->tf", back_c, down_weight, preferred_element_type=jnp.float32)
-    ).astype(jnp.bfloat16)
-    dbefore_q = gelu_back(
-        before_q, jnp.einsum("td,fd->tf", back_q, down_weight, preferred_element_type=jnp.float32)
-    ).astype(jnp.bfloat16)
-    upbias_local = jnp.sum(dbefore_c.astype(jnp.float32), 0) + jnp.sum(
-        dbefore_q.astype(jnp.float32), 0
-    )
-    up_grad = jnp.einsum(
-        "td,tf->df", middle_rows_c, dbefore_c, preferred_element_type=jnp.float32
-    ) + jnp.einsum("td,tf->df", middle_rows_q, dbefore_q, preferred_element_type=jnp.float32)
-    rows_c = dbefore_c
-    rows_q = dbefore_q
-    feed_back = lax.psum_scatter(
-        jnp.concatenate(
-            [
-                jnp.einsum("tf,df->td", rows_c, up_weight, preferred_element_type=jnp.float32),
-                jnp.einsum("tf,df->td", rows_q, up_weight, preferred_element_type=jnp.float32),
-            ],
-            1,
-        ).astype(jnp.bfloat16),
-        "heads",
-        scatter_dimension=0,
-        tiled=True,
-    ).astype(jnp.float32)
-    dmiddle_c = dfinal_c + feed_back[:, :width]
-    dmiddle_q = dfinal_q + feed_back[:, width:]
-    dresid_c = layer_norm_back(dmiddle_c, normed1_c, inverse1_c, norm_param[0])
-    dresid_q = layer_norm_back(dmiddle_q, normed1_q, inverse1_q, norm_param[0])
-    gain1_grad = jnp.sum(dmiddle_c * normed1_c, 0) + jnp.sum(dmiddle_q * normed1_q, 0)
-    bias1_grad = jnp.sum(dmiddle_c, 0) + jnp.sum(dmiddle_q, 0)
-    dattn_c, dattn_q = (
-        lax.all_gather(dresid_c.astype(jnp.bfloat16), "heads", axis=0, tiled=True),
-        lax.all_gather(dresid_q.astype(jnp.bfloat16), "heads", axis=0, tiled=True),
-    )
-    out_grad = jnp.einsum(
-        "te,td->ed", attended_c, dattn_c, preferred_element_type=jnp.float32
-    ) + jnp.einsum("te,td->ed", attended_q, dattn_q, preferred_element_type=jnp.float32)
-    dmixed_c = jnp.einsum(
-        "td,ed->te", dattn_c, out_weight, preferred_element_type=jnp.float32
-    ).astype(jnp.bfloat16)
-    dmixed_q = jnp.einsum(
-        "td,ed->te", dattn_q, out_weight, preferred_element_type=jnp.float32
-    ).astype(jnp.bfloat16)
-
-    dinput, dweight, head_local = attention_backward(
-        content_rows, query_rows, projection, tables, head_bias, facts, proj, logsum,
-        jnp.stack([dmixed_c, dmixed_q]),
-    )
-    head_local = head_local.reshape(head_bias.shape)
-    proj_grad = jnp.swapaxes(dweight, 1, 2)
-    input_back = lax.psum_scatter(
-        jnp.concatenate([dinput[0], dinput[1]], 1),
-        "heads",
-        scatter_dimension=0,
-        tiled=True,
-    ).astype(jnp.float32)
-    content_in_grad = dresid_c + input_back[:, :width]
-    query_in_grad = dresid_q + input_back[:, width:]
-    proj_share, out_share, up_share, down_share = (
-        lax.psum_scatter(proj_grad, "dp", scatter_dimension=1, tiled=True),
-        lax.psum_scatter(out_grad, "dp", scatter_dimension=1, tiled=True),
-        lax.psum_scatter(up_grad, "dp", scatter_dimension=0, tiled=True),
-        lax.psum_scatter(down_grad, "dp", scatter_dimension=1, tiled=True),
-    )
-    heads_count = lax.axis_size("heads")
-    head_index = lax.axis_index("heads")
-    head_full = jnp.zeros((5, local_heads * heads_count, head_size), jnp.float32)
-    head_full = lax.dynamic_update_slice_in_dim(head_full, head_local, head_index * local_heads, 1)
-    bias_full = jnp.zeros((hidden_cols * heads_count,), jnp.float32)
-    bias_full = lax.dynamic_update_slice_in_dim(
-        bias_full, upbias_local, head_index * hidden_cols, 0
-    )
-    norm_local = jnp.stack([gain1_grad, bias1_grad, outbias_grad, gain2_grad, bias2_grad])
-    head_sum, bias_sum, norm_sum = lax.psum((head_full, bias_full, norm_local), ("dp", "heads"))
-    head_grad = lax.dynamic_slice_in_dim(head_sum, head_index * local_heads, local_heads, 1)
-    bias_grad = lax.dynamic_slice_in_dim(bias_sum, head_index * hidden_cols, hidden_cols, 0)
-    devices = lax.axis_size("dp") * heads_count
-    shared_squares = (
-        jnp.sum(head_sum * head_sum) + jnp.sum(bias_sum * bias_sum) + jnp.sum(norm_sum * norm_sum)
-    )
+    proj, logsum, mixed_pieces = attention_forward(
+        content_pieces, query_pieces, weight_pieces, tables[0], head_bias, facts
+    )
+    content_out, query_out, dresid, dmixed_pieces, (dup, ddown, dout, dsmall) = feed_layer(
+        mixed_pieces, bias_pieces, content_in, query_in, content_grad, query_grad, norm_param,
+        up_full, down_full, out_full,
+    )
+    dinput_pieces, dweight_pieces, dhead = attention_backward(
+        content_pieces, query_pieces, weight_pieces, tables, head_bias, facts, proj, logsum,
+        spread(dmixed_pieces),
+    )
+    small_sum = total_over(total_over(dsmall, "heads"), "dp")
+    up_share = scatter_all(dup)
+    down_share = scatter_all(ddown).T
+    out_share = scatter_all(jnp.swapaxes(dout, 0, 1)).T
+    proj_share = reduce_projection(dweight_pieces)
+    head_grad = total_over(dhead, "dp").reshape(head_bias.shape)
+    near = exchange(dinput_pieces[1], "heads", 1).astype(jnp.float32)
+    far = exchange(dinput_pieces[3], "heads", 1).astype(jnp.float32)
+    far = (dinput_pieces[2].astype(jnp.float32) + far).astype(jnp.bfloat16)
+    far = exchange(far, "heads", 2).astype(jnp.float32)
+    input_grad = dresid + dinput_pieces[0].astype(jnp.float32) + near + far
+    heads_count, head_index = lax.axis_size("heads"), lax.axis_index("heads")
+    bias_sum, norm_sum = small_sum[:heads_count], small_sum[heads_count : heads_count + 5]
+    bias_grad = lax.dynamic_slice_in_dim(bias_sum, head_index, 1, 0)[0]
+    dp_count = lax.axis_size("dp")
     local_squares = (
         jnp.sum(proj_share * proj_share)
         + jnp.sum(out_share * out_share)
         + jnp.sum(up_share * up_share)
         + jnp.sum(down_share * down_share)
-        + shared_squares / devices
-    )
-    grad_norm = jnp.sqrt(lax.psum(local_squares, ("dp", "heads")))
+        + jnp.sum(head_grad * head_grad) / dp_count
+        + (jnp.sum(bias_sum * bias_sum) + jnp.sum(norm_sum * norm_sum)) / (dp_count * heads_count)
+    )
+    grad_norm = jnp.sqrt(total_over(total_over(local_squares.reshape(1, 1), "heads"), "dp"))[0, 0]
     factor = CLIP_NORM / jnp.maximum(grad_norm, CLIP_NORM)
     attn_first, attn_second, attn_new = adam_step(
         attn_proj, attn_proj_first, attn_proj_second, proj_share, factor, True
@@ -627,10 +838,10 @@
         norm_param, norm_param_first, norm_param_second, norm_sum, factor, False
     )
     return (
-        final_c.astype(jnp.bfloat16),
-        final_q.astype(jnp.bfloat16),
-        content_in_grad,
-        query_in_grad,
+        content_out,
+        query_out,
+        input_grad[0],
+        input_grad[1],
         grad_norm,
         proj_share,
         attn_first,

time: 988 us -> 623 us (0.63)
  waiting for transfers between devices: 557 us -> 300 us
  blocking collectives: 114 us -> 0 us
  Pallas kernels: 113 us -> 191 us
  matrix products: 75.8 us -> 0 us
  starting transfers between devices: 11.7 us -> 54.7 us
  other arithmetic: 57.7 us -> 31.7 us
    all_gather x11 -> x3, waiting for transfers between devices: 247 us -> 67.5 us  [gather_all(): lax.all_gather(own, ('dp', 'heads'), axis=0, tiled=False)]
    unnamed x21 -> x7, waiting for transfers between devices: 91.2 us -> 1.09 us
    psum x2 -> x0, blocking collectives: 80.6 us -> none  [the longest x1 40.8 us: local(): lax.psum((head_full, bias_full, norm_local), ('dp', 'heads'))]
    pallas_call x2 -> x3, Pallas kernels: 113 us -> 191 us  [the longest x1 79.8 us: attention_forward(): pl.pallas_call(functools.partial(attention_forward_kernel, head_size, gro...]
    dot_general x18 -> x0, matrix products: 75.8 us -> none  [the longest x1 13.1 us: local(): jnp.einsum('td,fd->tf', back_c, down_weight, preferred_element_type=jnp.f...]
    ppermute x0 -> x42, waiting for transfers between devices: none -> 68.2 us  [exchange(): lax.ppermute(value, axis, [(i, i ^ mask) for i in range(lax.axis_size(axi...]
    reduce_scatter x6 -> x2, waiting for transfers between devices: 218 us -> 163 us  [scatter_all(): lax.psum_scatter(full, ('dp', 'heads'), scatter_dimension=0, tiled=True)]
    ppermute x0 -> x42, starting transfers between devices: none -> 54.4 us  [exchange(): lax.ppermute(value, axis, [(i, i ^ mask) for i in range(lax.axis_size(axi...]
  transfers between devices with their start and end apart: 19 -> 48, of which waited for: 17 -> 24; matrix products, arithmetic and copies ran while one was open for 10% -> 5% of each run, Pallas kernels for 7% -> 24%
where the time goes in v2:
time: 623 us; the launch traced here: 619 us
  waiting for transfers between devices  300 us (48%)
  Pallas kernels  191 us (31%)
  starting transfers between devices  54.7 us (9%)
  other arithmetic  31.7 us (5%)
  between operations  24 us (4%)
  local copies, waits for them, and re-layouts  17.2 us (3%)
    reduce_scatter x2, waiting for transfers between devices, scatter_all(): lax.psum_scatter(full, ('dp', 'heads'), scatter_dimension=0, tiled=True)  163 us
    pallas_call x1, Pallas kernels, attention_forward(): pl.pallas_call(functools.partial(attention_forward_kernel, head_size, gro...  79.8 us
    ppermute x42, waiting for transfers between devices, exchange(): lax.ppermute(value, axis, [(i, i ^ mask) for i in range(lax.axis_size(axi...  68.2 us
    all_gather x3, waiting for transfers between devices, gather_all(): lax.all_gather(own, ('dp', 'heads'), axis=0, tiled=False)  67.5 us
    pallas_call x1, Pallas kernels, attention_backward(): pl.pallas_call(functools.partial(attention_backward_kernel, head_size, gr...  67.1 us
    ppermute x42, starting transfers between devices, exchange(): lax.ppermute(value, axis, [(i, i ^ mask) for i in range(lax.axis_size(axi...  54.4 us
    pallas_call x1, Pallas kernels, feed_layer(): pl.pallas_call(functools.partial(feed_kernel, group), in_specs=[inside] *...  44.5 us
  transfers between devices with their start and end apart: 48, of which 24 were waited for; matrix products, arithmetic and copies ran while one was open for 5% of the time, Pallas kernels for 24%

profile of v2, /device:TPU:0, one launch (start us, length us, event | category | flops | bytes accessed | tf_op | source)
XLA Modules:
  0.0 618.9 jit_solution(1808413661069321473)
XLA Ops:
  7.3 1.6 copy.95
  9.0 1.6 convert_element_type.74
  10.7 1.6 convert_bitcast_fusion.1
  12.4 3.0 collective-permute-start.1
  16.5 3.1 collective-permute-start.9
  19.6 1.6 collective-permute-start.7
  24.3 4.2 collective-permute-done.9.refs_12_
  31.1 3.8 collective-permute-done.11.refs_14_
  37.3 5.9 collective-permute-done.4.refs_6_
  43.3 1.8 select_reduce_fusion
  45.9 2.0 collective-permute-start.12
  47.9 5.5 collective-permute-done.12.refs_15_
  53.3 1.8 collective-permute-start.14
  60.1 1.9 copy.94
  63.7 79.8 %shard_map.541 = (bf16[3,512,768]{2,1,0:T(8,128)(2,1)}, f32[3,512,8]{2,1,0:T(8,128)}, bf16[2,384,192]{2,1,0:T(8,128)(2,1)}, bf16[2,384,192]{2,1,0:T(8,128)(2,1)}...) custom-call(bf16[384,768]{1,0:T(8,128)(2,1)} %refs_0_.3, bf16[384,768]{1,0:T(8,128)(2,1)} %copy-done.2, ...), custom_call_target="tpu_custom_call" | custom-call | tf_op jit(solution)/shard_map/pallas_call | solution.py:253
  145.1 66.0 %all-gather.9.cloned.1.call-done = bf16[3072,768]{1,0:T(8,128)(2,1)} async-done(((bf16[96,768]{1,0:T(8,128)(2,1)}), bf16[3072,768]{1,0:T(8,128)(2,1)}) %all-gather.9.cloned.1.call-update) | async-done | bytes 4718608 | tf_op jit(solution)/shard_map/all_gather | solution.py:711
  211.0 44.5 %shard_map.542 = (bf16[384,768]{1,0:T(8,128)(2,1)}, bf16[384,768]{1,0:T(8,128)(2,1)}, f32[2,384,768]{2,1,0:T(8,128)}, bf16[2,384,192]{2,1,0:T(8,128)(2,1)}, bf16...) custom-call(bf16[2,384,192]{2,1,0:T(8,128)(2,1)} %get-tuple-element., ...), custom_call_target="tpu_custom_call" | custom-call | tf_op jit(solution)/shard_map/pallas_call | solution.py:628
  255.5 2.7 copy.99
  261.7 10.3 %collective-permute-done.17.refs_18_ = bf16[2,384,192]{2,1,0:T(8,128)(2,1)S(1)} collective-permute-done((bf16[2,384,192]{2,1,0:T(8,128)(2,1)S(1)}, bf16[2,384,192]{2,1,0:T(8,128)(2,1)S(1)}, u32[]{:S(2)}, u32[]{:S(2)}) %collective-permute-start.17) | collective-permute-done | bytes 294944 | tf_op jit(solution)/shard_map/ppermute | solution.py:663
  272.1 7.0 %collective-permute-done.18.refs_19_ = bf16[2,384,192]{2,1,0:T(8,128)(2,1)S(1)} collective-permute-done((bf16[2,384,192]{2,1,0:T(8,128)(2,1)S(1)}, bf16[2,384,192]{2,1,0:T(8,128)(2,1)S(1)}, u32[]{:S(2)}, u32[]{:S(2)}) %collective-permute-start.18) | collective-permute-done | bytes 294944 | tf_op jit(solution)/shard_map/ppermute | solution.py:663
  279.9 67.1 %shard_map.543 = (bf16[2,384,768]{2,1,0:T(8,128)(2,1)}, bf16[2,384,768]{2,1,0:T(8,128)(2,1)}, bf16[2,384,768]{2,1,0:T(8,128)(2,1)}, bf16[2,384,768]{2,1,0:T(8,12...) custom-call(bf16[384,768]{1,0:T(8,128)(2,1)} %refs_0_.3, ...), custom_call_target="tpu_custom_call" | custom-call | tf_op jit(solution)/shard_map/pallas_call | solution.py:447
  347.7 2.3 collective-permute-done.32
  351.5 2.6 collective-permute-done.33
  354.2 1.6 collective-permute-start.34
  355.7 2.6 collective-permute-done.34
  358.3 2.0 collective-permute-start.35
  362.5 2.3 collective-permute-start.36
  366.0 2.8 add_convert_fusion
  370.9 2.3 collective-permute-start.31
  375.5 2.4 collective-permute-start.24
  378.0 1.8 collective-permute-start.25
  381.8 5.0 collective-permute-done.23
  386.8 2.1 collective-permute-start.26
  388.9 2.8 collective-permute-done.24
  391.7 1.6 collective-permute-start.27
  394.2 1.9 multiply_reduce_fusion.6
  398.1 9.2 %collective-permute-done.26 = bf16[4,96,192]{2,1,0:T(8,128)(2,1)S(1)} collective-permute-done((bf16[4,96,192]{2,1,0:T(8,128)(2,1)}, bf16[4,96,192]{2,1,0:T(8,128)(2,1)S(1)}, u32[]{:S(2)}, u32[]{:S(2)}) %collective-permute-start.26) | collective-permute-done | bytes 147488 | tf_op jit(solution)/shard_map/ppermute | solution.py:663
  407.9 2.3 multiply_reduce_fusion
  413.1 2.4 convert_add_fusion
  417.3 53.1 %reduce-scatter.6.cloned.1.call-done = bf16[96,768]{1,0:T(8,128)(2,1)} async-done(((bf16[3072,768]{1,0:T(8,128)(2,1)}), bf16[96,768]{1,0:T(8,128)(2,1)}) %reduce-scatter.6.cloned.1.call-update) | async-done | bytes 147472 | tf_op jit(solution)/shard_map/reduce_scatter | solution.py:724
  470.4 1.6 multiply_reduce_fusion.2
  472.7 110.0 %reduce-scatter.8.cloned.1.call-done = bf16[96,768]{1,0:T(8,128)(2,1)} async-done(((bf16[3072,768]{1,0:T(8,128)(2,1)}), bf16[96,768]{1,0:T(8,128)(2,1)}) %reduce-scatter.8.cloned.1.call-update) | async-done | bytes 147472 | tf_op jit(solution)/shard_map/reduce_scatter | solution.py:724
  582.8 1.6 multiply_reduce_fusion.1
  586.8 2.9 collective-permute-start.38
  591.0 2.8 collective-permute-start.39
  595.2 2.7 collective-permute-start.40
  599.4 2.9 collective-permute-start.41
  602.3 1.6 collective-permute-done.41
  (216 shorter events, 48.8 us)
Async XLA Ops:
  7.2 136.4 %all-gather.11.cloned.1.call-start = ((), (), s32[]{:S(2)}) async-start(), calls=%async_computation.7 | async-start | bytes 1622016 | tf_op jit(solution)/shard_map/all_gather | solution.py:711
  8.9 136.2 %all-gather.7.cloned.1.call-start = ((), (), s32[]{:S(2)}) async-start(), calls=%async_computation.5 | async-start | bytes 4866048 | tf_op jit(solution)/shard_map/all_gather | solution.py:711
  10.6 200.4 %all-gather.9.cloned.1.call-start = ((), (), s32[]{:S(2)}) async-start(), calls=%async_computation.6 | async-start | bytes 4866048 | tf_op jit(solution)/shard_map/all_gather | solution.py:711
  12.3 397.9 %reduce-scatter.10.cloned.1.call-start = ((), (), s32[]{:S(2)}) async-start(), calls=%async_computation.8 | async-start | bytes 1622016
  12.4 24.9 %collective-permute-start.1 = (bf16[384,768]{1,0:T(8,128)(2,1)}, bf16[384,768]{1,0:T(8,128)(2,1)S(1)}, u32[]{:S(2)}, u32[]{:S(2)}) collective-permute-start(bf16[384,768]{1,0:T(8,128)(2,1)} %refs_0_.3), channel_id=1, source_target_pairs={{0,2},{1,3},{2,0},{3,1},{4,6},{5,7},{6,4},{7,5},{8,10},{9,11},{10,... | collective-permute-start | bytes 1769480 | tf_op jit(solution)/shard_map/ppermute | solution.py:663
  15.4 27.8 %collective-permute-start.4 = (bf16[384,768]{1,0:T(8,128)(2,1)}, bf16[384,768]{1,0:T(8,128)(2,1)S(1)}, u32[]{:S(2)}, u32[]{:S(2)}) collective-permute-start(bf16[384,768]{1,0:T(8,128)(2,1)} %refs_4_.3), channel_id=1, source_target_pairs={{0,2},{1,3},{2,0},{3,1},{4,6},{5,7},{6,4},{7,5},{8,10},{9,11},{10,... | collective-permute-start | bytes 1769480 | tf_op jit(solution)/shard_map/ppermute | solution.py:663
  16.5 12.0 %collective-permute-start.9 = (bf16[4,96,192]{2,1,0:T(8,128)(2,1)S(1)}, bf16[4,96,192]{2,1,0:T(8,128)(2,1)S(1)}, u32[]{:S(2)}, u32[]{:S(2)}) collective-permute-start(bf16[4,96,192]{2,1,0:T(8,128)(2,1)S(1)} %convert_element_type.71.refs_8_), channel_id=1, source_target_pairs={{0,16},{4,20},{8,24},{12,28},{16,0},{20,4},{24,8},{28,12},{1,17},{... | collective-permute-start | bytes 442376 | tf_op jit(solution)/shard_map/ppermute | solution.py:663
  19.6 9.8 %collective-permute-start.7 = (bf16[4,96,192]{2,1,0:T(8,128)(2,1)S(1)}, bf16[4,96,192]{2,1,0:T(8,128)(2,1)S(1)}, u32[]{:S(2)}, u32[]{:S(2)}) collective-permute-start(bf16[4,96,192]{2,1,0:T(8,128)(2,1)S(1)} %convert_element_type.71.refs_8_), channel_id=1, source_target_pairs={{0,8},{4,12},{8,0},{12,4},{16,24},{20,28},{24,16},{28,20},{1,9},{5... | collective-permute-start | bytes 442376 | tf_op jit(solution)/shard_map/ppermute | solution.py:663
  21.2 9.8 %collective-permute-start.6 = (bf16[4,96,192]{2,1,0:T(8,128)(2,1)S(1)}, bf16[4,96,192]{2,1,0:T(8,128)(2,1)S(1)}, u32[]{:S(2)}, u32[]{:S(2)}) collective-permute-start(bf16[4,96,192]{2,1,0:T(8,128)(2,1)S(1)} %convert_element_type.71.refs_8_), channel_id=1, source_target_pairs={{0,4},{4,0},{8,12},{12,8},{16,20},{20,16},{24,28},{28,24},{1,5},{5... | collective-permute-start | bytes 442376 | tf_op jit(solution)/shard_map/ppermute | solution.py:663
  28.5 6.3 %collective-permute-start.11 = (bf16[4,96,192]{2,1,0:T(8,128)(2,1)S(1)}, bf16[4,96,192]{2,1,0:T(8,128)(2,1)S(1)}, u32[]{:S(2)}, u32[]{:S(2)}) collective-permute-start(bf16[4,96,192]{2,1,0:T(8,128)(2,1)S(1)} %collective-permute-done.9.refs_12_), channel_id=1, source_target_pairs={{0,8},{4,12},{8,0},{12,4},{16,24},{20,28},{24,16},{28,20},{1,9},{5... | collective-permute-start | bytes 442376 | tf_op jit(solution)/shard_map/ppermute | solution.py:663
  29.4 6.4 %collective-permute-start.10 = (bf16[4,96,192]{2,1,0:T(8,128)(2,1)S(1)}, bf16[4,96,192]{2,1,0:T(8,128)(2,1)S(1)}, u32[]{:S(2)}, u32[]{:S(2)}) collective-permute-start(bf16[4,96,192]{2,1,0:T(8,128)(2,1)S(1)} %collective-permute-done.9.refs_12_), channel_id=1, source_target_pairs={{0,4},{4,0},{8,12},{12,8},{16,20},{20,16},{24,28},{28,24},{1,5},{5... | collective-permute-start | bytes 442376 | tf_op jit(solution)/shard_map/ppermute | solution.py:663
  31.0 22.3 %collective-permute-start = (bf16[384,768]{1,0:T(8,128)(2,1)}, bf16[384,768]{1,0:T(8,128)(2,1)S(1)}, u32[]{:S(2)}, u32[]{:S(2)}) collective-permute-start(bf16[384,768]{1,0:T(8,128)(2,1)} %refs_0_.3), channel_id=1, source_target_pairs={{0,1},{1,0},{2,3},{3,2},{4,5},{5,4},{6,7},{7,6},{8,9},{9,8},{10,11... | collective-permute-start | bytes 1769480 | tf_op jit(solution)/shard_map/ppermute | solution.py:663
  34.8 20.3 %collective-permute-start.3 = (bf16[384,768]{1,0:T(8,128)(2,1)}, bf16[384,768]{1,0:T(8,128)(2,1)S(1)}, u32[]{:S(2)}, u32[]{:S(2)}) collective-permute-start(bf16[384,768]{1,0:T(8,128)(2,1)} %refs_4_.3), channel_id=1, source_target_pairs={{0,1},{1,0},{2,3},{3,2},{4,5},{5,4},{6,7},{7,6},{8,9},{9,8},{10,11... | collective-permute-start | bytes 1769480 | tf_op jit(solution)/shard_map/ppermute | solution.py:663
  35.8 10.1 %collective-permute-start.8 = (bf16[4,96,192]{2,1,0:T(8,128)(2,1)S(1)}, bf16[4,96,192]{2,1,0:T(8,128)(2,1)S(1)}, u32[]{:S(2)}, u32[]{:S(2)}) collective-permute-start(bf16[4,96,192]{2,1,0:T(8,128)(2,1)S(1)} %collective-permute-done.7.refs_10_), channel_id=1, source_target_pairs={{0,4},{4,0},{8,12},{12,8},{16,20},{20,16},{24,28},{28,24},{1,5},{5... | collective-permute-start | bytes 442376 | tf_op jit(solution)/shard_map/ppermute | solution.py:663
  37.3 25.4 %collective-permute-start.2 = (bf16[384,768]{1,0:T(8,128)(2,1)S(1)}, bf16[384,768]{1,0:T(8,128)(2,1)S(1)}, u32[]{:S(2)}, u32[]{:S(2)}) collective-permute-start(bf16[384,768]{1,0:T(8,128)(2,1)S(1)} %collective-permute-done.1.refs_2_), channel_id=1, source_target_pairs={{0,1},{1,0},{2,3},{3,2},{4,5},{5,4},{6,7},{7,6},{8,9},{9,8},{10,11... | collective-permute-start | bytes 1769480 | tf_op jit(solution)/shard_map/ppermute | solution.py:663
  43.2 19.5 %collective-permute-start.5 = (bf16[384,768]{1,0:T(8,128)(2,1)S(1)}, bf16[384,768]{1,0:T(8,128)(2,1)S(1)}, u32[]{:S(2)}, u32[]{:S(2)}) collective-permute-start(bf16[384,768]{1,0:T(8,128)(2,1)S(1)} %collective-permute-done.4.refs_6_), channel_id=1, source_target_pairs={{0,1},{1,0},{2,3},{3,2},{4,5},{5,4},{6,7},{7,6},{8,9},{9,8},{10,11... | collective-permute-start | bytes 1769480 | tf_op jit(solution)/shard_map/ppermute | solution.py:663
  45.9 7.4 %collective-permute-start.12 = (bf16[4,96,192]{2,1,0:T(8,128)(2,1)S(1)}, bf16[4,96,192]{2,1,0:T(8,128)(2,1)S(1)}, u32[]{:S(2)}, u32[]{:S(2)}) collective-permute-start(bf16[4,96,192]{2,1,0:T(8,128)(2,1)S(1)} %collective-permute-done.11.refs_14_), channel_id=1, source_target_pairs={{0,4},{4,0},{8,12},{12,8},{16,20},{20,16},{24,28},{28,24},{1,5},{5... | collective-permute-start | bytes 442376 | tf_op jit(solution)/shard_map/ppermute | solution.py:663
  53.3 90.2 %collective-permute-start.13 = (f32[1,768]{1,0:T(1,128)S(1)}, f32[1,768]{1,0:T(1,128)}, u32[]{:S(2)}, u32[]{:S(2)}) collective-permute-start(f32[1,768]{1,0:T(1,128)S(1)} %broadcast_in_dim.76.refs_4_), channel_id=1, source_target_pairs={{0,1},{1,0},{2,3},{3,2},{4,5},{5,4},{6,7},{7,6},{8,9},{9,8},{10,11... | collective-permute-start | bytes 9224 | tf_op jit(solution)/shard_map/ppermute | solution.py:663
  53.3 90.2 %collective-permute-start.14 = (f32[1,768]{1,0:T(1,128)S(1)}, f32[1,768]{1,0:T(1,128)}, u32[]{:S(2)}, u32[]{:S(2)}) collective-permute-start(f32[1,768]{1,0:T(1,128)S(1)} %broadcast_in_dim.76.refs_4_), channel_id=1, source_target_pairs={{0,2},{1,3},{2,0},{3,1},{4,6},{5,7},{6,4},{7,5},{8,10},{9,11},{10,... | collective-permute-start | bytes 9224 | tf_op jit(solution)/shard_map/ppermute | solution.py:663
  55.2 88.4 %collective-permute-start.15 = (f32[1,768]{1,0:T(1,128)S(1)}, f32[1,768]{1,0:T(1,128)}, u32[]{:S(2)}, u32[]{:S(2)}) collective-permute-start(f32[1,768]{1,0:T(1,128)S(1)} %broadcast_in_dim.76.refs_4_), channel_id=1, source_target_pairs={{0,3},{1,2},{2,1},{3,0},{4,7},{5,6},{6,5},{7,4},{8,11},{9,10},{10,... | collective-permute-start | bytes 9224 | tf_op jit(solution)/shard_map/ppermute | solution.py:663
  258.2 212.2 %reduce-scatter.6.cloned.1.call-start = ((), (), s32[]{:S(2)}) async-start(), calls=%async_computation.3 | async-start | bytes 4866048 | tf_op jit(solution)/shard_map/reduce_scatter | solution.py:724
  258.8 323.9 %reduce-scatter.8.cloned.1.call-start = ((), (), s32[]{:S(2)}) async-start(), calls=%async_computation.4 | async-start | bytes 4866048 | tf_op jit(solution)/shard_map/reduce_scatter | solution.py:724
  259.9 1.9 collective-permute-start.16
  260.1 11.9 %collective-permute-start.17 = (bf16[2,384,192]{2,1,0:T(8,128)(2,1)S(1)}, bf16[2,384,192]{2,1,0:T(8,128)(2,1)S(1)}, u32[]{:S(2)}, u32[]{:S(2)}) collective-permute-start(bf16[2,384,192]{2,1,0:T(8,128)(2,1)S(1)} %copy-done.54), channel_id=1, source_target_pairs={{0,2},{1,3},{2,0},{3,1},{4,6},{5,7},{6,4},{7,5},{8,10},{9,11},{10,... | collective-permute-start | bytes 884744 | tf_op jit(solution)/shard_map/ppermute | solution.py:663
  261.6 17.6 %collective-permute-start.18 = (bf16[2,384,192]{2,1,0:T(8,128)(2,1)S(1)}, bf16[2,384,192]{2,1,0:T(8,128)(2,1)S(1)}, u32[]{:S(2)}, u32[]{:S(2)}) collective-permute-start(bf16[2,384,192]{2,1,0:T(8,128)(2,1)S(1)} %copy-done.53), channel_id=1, source_target_pairs={{0,3},{1,2},{2,1},{3,0},{4,7},{5,6},{6,5},{7,4},{8,11},{9,10},{10,... | collective-permute-start | bytes 884744 | tf_op jit(solution)/shard_map/ppermute | solution.py:663
  347.0 19.0 %collective-permute-start.20 = (bf16[2,384,768]{2,1,0:T(8,128)(2,1)}, bf16[2,384,768]{2,1,0:T(8,128)(2,1)S(1)}, u32[]{:S(2)}, u32[]{:S(2)}) collective-permute-start(bf16[2,384,768]{2,1,0:T(8,128)(2,1)} %get-tuple-element.79), channel_id=1, source_target_pairs={{0,1},{1,0},{2,3},{3,2},{4,5},{5,4},{6,7},{7,6},{8,9},{9,8},{10,11... | collective-permute-start | bytes 3538952 | tf_op jit(solution)/shard_map/ppermute | solution.py:663
  347.6 2.4 collective-permute-start.32
  350.0 4.2 collective-permute-start.33
  354.2 4.2 collective-permute-start.34
  358.3 4.2 collective-permute-start.35
  360.3 4.5 collective-permute-start.29
  362.5 7.8 %collective-permute-start.36 = (f32[16,768]{1,0:T(8,128)S(1)}, f32[16,768]{1,0:T(8,128)S(1)}, u32[]{:S(2)}, u32[]{:S(2)}) collective-permute-start(f32[16,768]{1,0:T(8,128)S(1)} %add.286), channel_id=1, source_target_pairs={{0,16},{4,20},{8,24},{12,28},{16,0},{20,4},{24,8},{28,12},{1,17},{... | collective-permute-start | bytes 147464 | tf_op jit(solution)/shard_map/ppermute | solution.py:663
  364.8 48.3 %collective-permute-start.19 = (bf16[2,384,768]{2,1,0:T(8,128)(2,1)}, bf16[2,384,768]{2,1,0:T(8,128)(2,1)}, u32[]{:S(2)}, u32[]{:S(2)}) collective-permute-start(bf16[2,384,768]{2,1,0:T(8,128)(2,1)} %get-tuple-element.77), channel_id=1, source_target_pairs={{0,1},{1,0},{2,3},{3,2},{4,5},{5,4},{6,7},{7,6},{8,9},{9,8},{10,11... | collective-permute-start | bytes 3538952 | tf_op jit(solution)/shard_map/ppermute | solution.py:663
  365.5 5.4 collective-permute-start.30
  368.8 44.3 %collective-permute-start.21 = (bf16[2,384,768]{2,1,0:T(8,128)(2,1)}, bf16[2,384,768]{2,1,0:T(8,128)(2,1)}, u32[]{:S(2)}, u32[]{:S(2)}) collective-permute-start(bf16[2,384,768]{2,1,0:T(8,128)(2,1)} %add_convert_fusion), channel_id=1, source_target_pairs={{0,2},{1,3},{2,0},{3,1},{4,6},{5,7},{6,4},{7,5},{8,10},{9,11},{10,... | collective-permute-start | bytes 3538952 | tf_op jit(solution)/shard_map/ppermute | solution.py:663
  370.2 7.7 %collective-permute-start.22 = (bf16[4,96,192]{2,1,0:T(8,128)(2,1)}, bf16[4,96,192]{2,1,0:T(8,128)(2,1)S(1)}, u32[]{:S(2)}, u32[]{:S(2)}) collective-permute-start(bf16[4,96,192]{2,1,0:T(8,128)(2,1)} %get-tuple-element.81), channel_id=1, source_target_pairs={{0,4},{4,0},{8,12},{12,8},{16,20},{20,16},{24,28},{28,24},{1,5},{5... | collective-permute-start | bytes 442376 | tf_op jit(solution)/shard_map/ppermute | solution.py:663
  370.9 4.6 collective-permute-start.31
  374.4 12.4 %collective-permute-start.23 = (bf16[4,96,192]{2,1,0:T(8,128)(2,1)}, bf16[4,96,192]{2,1,0:T(8,128)(2,1)S(1)}, u32[]{:S(2)}, u32[]{:S(2)}) collective-permute-start(bf16[4,96,192]{2,1,0:T(8,128)(2,1)} %get-tuple-element.82), channel_id=1, source_target_pairs={{0,8},{4,12},{8,0},{12,4},{16,24},{20,28},{24,16},{28,20},{1,9},{5... | collective-permute-start | bytes 442376 | tf_op jit(solution)/shard_map/ppermute | solution.py:663
  375.5 16.2 %collective-permute-start.24 = (bf16[4,96,192]{2,1,0:T(8,128)(2,1)}, bf16[4,96,192]{2,1,0:T(8,128)(2,1)S(1)}, u32[]{:S(2)}, u32[]{:S(2)}) collective-permute-start(bf16[4,96,192]{2,1,0:T(8,128)(2,1)} %get-tuple-element.83), channel_id=1, source_target_pairs={{0,12},{4,8},{8,4},{12,0},{16,28},{20,24},{24,20},{28,16},{1,13},{... | collective-permute-start | bytes 442376 | tf_op jit(solution)/shard_map/ppermute | solution.py:663
  378.0 15.3 %collective-permute-start.25 = (bf16[4,96,192]{2,1,0:T(8,128)(2,1)}, bf16[4,96,192]{2,1,0:T(8,128)(2,1)S(1)}, u32[]{:S(2)}, u32[]{:S(2)}) collective-permute-start(bf16[4,96,192]{2,1,0:T(8,128)(2,1)} %get-tuple-element.84), channel_id=1, source_target_pairs={{0,16},{4,20},{8,24},{12,28},{16,0},{20,4},{24,8},{28,12},{1,17},{... | collective-permute-start | bytes 442376 | tf_op jit(solution)/shard_map/ppermute | solution.py:663
  386.8 20.5 %collective-permute-start.26 = (bf16[4,96,192]{2,1,0:T(8,128)(2,1)}, bf16[4,96,192]{2,1,0:T(8,128)(2,1)S(1)}, u32[]{:S(2)}, u32[]{:S(2)}) collective-permute-start(bf16[4,96,192]{2,1,0:T(8,128)(2,1)} %get-tuple-element.85), channel_id=1, source_target_pairs={{0,20},{4,16},{8,28},{12,24},{16,4},{20,0},{24,12},{28,8},{1,21},{... | collective-permute-start | bytes 442376 | tf_op jit(solution)/shard_map/ppermute | solution.py:663
  391.7 15.6 %collective-permute-start.27 = (bf16[4,96,192]{2,1,0:T(8,128)(2,1)}, bf16[4,96,192]{2,1,0:T(8,128)(2,1)}, u32[]{:S(2)}, u32[]{:S(2)}) collective-permute-start(bf16[4,96,192]{2,1,0:T(8,128)(2,1)} %get-tuple-element.86), channel_id=1, source_target_pairs={{0,24},{4,28},{8,16},{12,20},{16,8},{20,12},{24,0},{28,4},{1,25},{... | collective-permute-start | bytes 442376 | tf_op jit(solution)/shard_map/ppermute | solution.py:663
  393.3 14.0 %collective-permute-start.28 = (bf16[4,96,192]{2,1,0:T(8,128)(2,1)}, bf16[4,96,192]{2,1,0:T(8,128)(2,1)}, u32[]{:S(2)}, u32[]{:S(2)}) collective-permute-start(bf16[4,96,192]{2,1,0:T(8,128)(2,1)} %get-tuple-element.87), channel_id=1, source_target_pairs={{0,28},{4,24},{8,20},{12,16},{16,12},{20,8},{24,4},{28,0},{1,29},{... | collective-permute-start | bytes 442376 | tf_op jit(solution)/shard_map/ppermute | solution.py:663
  585.0 1.2 collective-permute-start.37
  586.8 3.6 collective-permute-start.38
  591.0 3.6 collective-permute-start.39
  595.2 3.6 collective-permute-start.40
  599.4 4.5 collective-permute-start.41
  (56 other events, 4879.2 us)
Sparse Core Ops, SparseCore 0:
  11.5 58.8 all-gather.10
  73.8 71.1 all-gather.6
  148.5 62.4 all-gather.8
  258.3 95.8 reduce-scatter.9
  359.5 110.8 reduce-scatter.5
  476.7 106.0 reduce-scatter.7

commit v3 on v2

--- a/solution.py
+++ b/solution.py
@@ -287,204 +287,462 @@
     return results[0], results[1], results[2:]
 
 
-def attention_backward_kernel(head_size, group, parts, *refs):
+class Links:
+    def __init__(self, send_sems, recv_sems):
+        self.send_sems, self.recv_sems, self.used = send_sems, recv_sems, 0
+
+    def push(self, source, place, axis, distance):
+        index = self.used
+        self.used = index + 1
+        return pltpu.make_async_remote_copy(
+            source, place, self.send_sems.at[index], self.recv_sems.at[index],
+            device_id={axis: lax.axis_index(axis) ^ distance}, device_id_type=pl.DeviceIdType.MESH,
+        )
+
+
+def add_planes(place, first, second):
+    def one(z, carry):
+        place[z] = (first(z).astype(jnp.float32) + second[z].astype(jnp.float32)).astype(place.dtype)
+        return carry
+
+    lax.fori_loop(0, place.shape[0], one, 0)
+
+
+class Scatter:
+    def __init__(self, links, sems, sem, source, order, refs):
+        self.kept, self.got, self.got_two, self.got_last = refs
+        self.order = order
+        heads_here, dp_here = lax.axis_index("heads"), lax.axis_index("dp")
+        x, y, z = heads_here >> 1, dp_here & 1, dp_here >> 1
+        if order == "xy":
+            own, other, first, second, self.mine = source.at[:, :, x], source.at[:, :, 1 - x], ("heads", 2), ("dp", 1), y
+        else:
+            own, other, first, second, self.mine = source.at[:, y], source.at[:, 1 - y], ("dp", 1), ("heads", 2), x
+        self.load = pltpu.make_async_copy(own, self.kept, sems.at[sem])
+        self.copy = links.push(other, self.got, *first)
+        self.copy_two = links.push(self.kept.at[:, 1 - self.mine], self.got_two, *second)
+        self.place = z
+        self.copies_last = [
+            links.push(self.got_two.at[z ^ m], self.got_last.at[m - 1], "dp", 2 * m)
+            for m in range(1, source.shape[0])
+        ]
+
+    def begin(self):
+        self.load.start()
+        self.copy.start()
+
+    def second(self):
+        self.load.wait()
+        self.copy.wait()
+        add_planes(self.kept, lambda z: self.kept[z], self.got)
+        self.copy_two.start()
+
+    def third(self):
+        self.copy_two.wait()
+        add_planes(self.got_two, lambda z: self.kept[z, self.mine], self.got_two)
+        for copy in self.copies_last:
+            copy.start()
+
+    def last(self):
+        for copy in self.copies_last:
+            copy.wait()
+        total = self.got_two[self.place].astype(jnp.float32)
+        for index in range(self.got_last.shape[0]):
+            total = total + self.got_last[index].astype(jnp.float32)
+        return total
+
+
+def square_sum(values):
+    return jnp.sum(jnp.sum(values * values, -1, keepdims=True), 0, keepdims=True)
+
+
+def attention_backward_kernel(head_size, group, parts, fast, *refs):
     content_pieces, query_pieces, refs = refs[:group], refs[group : 2 * group], refs[2 * group :]
     weight_pieces, refs = refs[:parts], refs[parts:]
-    upper_pieces, refs = refs[:group], refs[group:]
+    upper_pieces, dresid_hbm, refs = refs[:group], refs[group], refs[group + 1 :]
     table_ref, turned_ref, bias_ref, row_ref, col_ref, proj_ref, logsum_ref = refs[:7]
-    dinput_pieces, refs = refs[7 : 7 + group], refs[7 + group :]
-    dweight_pieces, dhead_ref, refs = refs[:parts], refs[parts], refs[parts + 1 :]
+    sources, small_ref, refs = refs[7:10], refs[10], refs[11:]
+    outputs, refs = refs[:9] if fast else refs[:4], refs[9:] if fast else refs[4:]
+    content_grad_ref, query_grad_ref, dhead_ref = outputs[:3]
     content_all, query_all, weight_ref, upper_all, dinput_ref, dweight_ref = refs[:6]
-    relative_ref, backward_ref, mask_ref, drel_ref, dcols_ref, dkeys_ref, dvalues_ref, sems = refs[6:]
-    length = row_ref.shape[2]
+    relative_ref, backward_ref, mask_ref, drel_ref, dcols_ref, dkeys_ref, dvalues_ref = refs[6:13]
+    dwide_ref, near_ref, cross_ref, far_ref, dresid_ref, dhead_own, refs = *refs[13:19], refs[19:]
+    sems, send_sems, recv_sems, refs = *refs[:3], refs[3:]
+    rows, length = row_ref.shape[0], row_ref.shape[2]
     half = length // 2
-    width = weight_ref.shape[-1]
+    depth, width = weight_ref.shape[1:]
     heads = width // head_size
     scale = head_size ** (-0.5)
     factor = scale * LOG2E
-    row = pl.program_id(0)
     heads_here, dp_here = lax.axis_index("heads"), lax.axis_index("dp")
-
-    @pl.when(row == 0)
-    def _():
-        copies = start_inputs(
-            content_pieces, query_pieces, weight_pieces, content_all, query_all, weight_ref, sems
+    chip = heads_here >> 1
+    tokens = upper_pieces[0].shape[1]
+    links = Links(send_sems, recv_sems)
+
+    def token_part(k):
+        return pl.ds(pl.multiple_of((heads_here ^ k) * tokens, tokens), tokens)
+
+    copies = start_inputs(
+        content_pieces, query_pieces, weight_pieces, content_all, query_all, weight_ref, sems
+    )
+    copies += start_pieces([upper_pieces[0]], lambda k: upper_all.at[:, token_part(0)], sems, 2 * group + parts)
+    dresid_copy = pltpu.make_async_copy(dresid_hbm, dresid_ref, sems.at[2 * group + parts + 1])
+    dresid_copy.start()
+    barrier = pltpu.get_barrier_semaphore()
+    peers = [("heads", k) for k in range(1, group)] + [("dp", k) for k in range(1, parts)]
+    for axis, k in peers:
+        pl.semaphore_signal(
+            barrier, inc=1, device_id={axis: lax.axis_index(axis) ^ k}, device_id_type=pl.DeviceIdType.MESH
         )
-        tokens = upper_pieces[0].shape[1]
-        copies += start_pieces(
-            upper_pieces,
-            lambda k: upper_all.at[:, pl.ds(pl.multiple_of((heads_here ^ k) * tokens, tokens), tokens)],
-            sems,
-            2 * group + parts,
+    pl.semaphore_wait(barrier, len(peers))
+    upper_copies = [
+        links.push(upper_pieces[k], upper_all.at[:, token_part(0)], "heads", k) for k in range(1, group)
+    ]
+    for copy in upper_copies:
+        copy.start()
+    if fast:
+        scatters = [
+            Scatter(links, sems, 2 * group + parts + 2 + n, sources[n], order, refs[4 * n : 4 * n + 4])
+            for n, order in enumerate(("xy", "yx", "yx"))
+        ]
+        small_got, small_more, small_mid, dweight_got, dweight_more, head_got, tile_ref, tile_got, tile_more = refs[12:]
+        for scatter in scatters:
+            scatter.begin()
+        small_first = [links.push(small_ref, small_got.at[heads_here], "heads", k) for k in range(1, group)]
+        for copy in small_first:
+            copy.start()
+        small_got[heads_here] = small_ref[...]
+        small_second = [links.push(small_mid, small_more.at[dp_here], "dp", k) for k in range(1, parts)]
+    for copy in copies:
+        copy.wait()
+    upper_copies[0].wait()
+    relative_ref[...] = dot(table_ref[...], weight_ref[3]).astype(jnp.bfloat16)
+    backward_ref[...] = dot(turned_ref[...], weight_ref[3]).astype(jnp.bfloat16)
+    drel_ref[...] = jnp.zeros_like(drel_ref)
+    dweight_ref[...] = jnp.zeros_like(dweight_ref)
+    dhead_own[...] = jnp.zeros_like(dhead_own)
+
+    def after(step, place, body):
+        if fast:
+            @pl.when(step == place)
+            def _():
+                body()
+
+    def small_middle():
+        for copy in small_first:
+            copy.wait()
+        total = small_got[0]
+        for k in range(1, group):
+            total = total + small_got[k]
+        small_mid[...] = total
+        small_more[dp_here] = total
+        for copy in small_second:
+            copy.start()
+
+    def one_row(step, carry):
+        row = jnp.where(step == 0, 0, rows - step)
+        row = jnp.where(chip == 0, row, rows - 1 - row)
+
+        @pl.when(step == 1)
+        def _():
+            for copy in upper_copies[1:]:
+                copy.wait()
+
+        row_part(step, row)
+        return carry
+
+    def row_part(step, row):
+        here = pl.ds(pl.multiple_of(row * length, length), length)
+        content_ref, query_ref = content_all.at[here], query_all.at[here]
+        facts_row, facts_col = row_ref[row], col_ref[row]
+        write_masks(mask_ref, facts_row, facts_col, half)
+        roll = roll_matrix(facts_col[:, 3:4], length)
+        upper = dot(roll, jnp.concatenate([upper_all[0, here], upper_all[1, here]], -1)).astype(jnp.bfloat16)
+        segment_col, segment_row = facts_col[:, 2:3], facts_row[2:3, :]
+        down = lax.broadcasted_iota(jnp.int32, (half, half), 0)
+        along = lax.broadcasted_iota(jnp.int32, (half, half), 1)
+        mirror = jnp.where(down + along == half - 1, 1.0, 0.0).astype(jnp.bfloat16)
+        lane = lax.broadcasted_iota(jnp.int32, (length, head_size), 1)
+        extra = jnp.where(lane == 0, segment_col, jnp.where(lane == 1, 1.0, 0.0)).astype(jnp.bfloat16)
+        for head in range(heads):
+            own_cols = slice(head * head_size, (head + 1) * head_size)
+            cols = lambda kind: slice(kind * width + head * head_size, kind * width + (head + 1) * head_size)
+            bias = [bias_ref[kind : kind + 1, own_cols] for kind in range(5)]
+            keys, values = proj_ref[row, :, cols(1)], proj_ref[row, :, cols(2)]
+            keys_twice = jnp.concatenate([keys, keys], -1)
+            keys_extra = jnp.concatenate([keys, extra], -1)
+            relative = relative_ref[:, own_cols]
+            relative_twice = jnp.concatenate([relative, relative], -1)
+            backward = backward_ref[:, own_cols]
+            heads_sums = [jnp.zeros((1, head_size), jnp.float32) for _ in range(5)]
+            for stream in range(2):
+                with_u, with_w, with_c, own, slope = query_sides(
+                    proj_ref[row, :, cols(3 * stream)], bias, segment_col, factor
+                )
+                index = stream * heads + head
+                own = own - logsum_ref[row, :, index : index + 1]
+                upper_now = upper[:, index * head_size : (index + 1) * head_size]
+                with_u_t, with_w_t, upper_t = with_u.T, with_w.T, upper_now.T
+                dquery = []
+                for block in range(2):
+                    part = slice(block * half, (block + 1) * half)
+                    scores = block_scores(
+                        with_u[part], with_w[part], keys_twice[part], relative_twice, half
+                    )
+                    scores = scores + own[part] + slope[part] * segment_row[:, part] + mask_ref[stream, block]
+                    chances = jnp.exp2(scores)
+                    dchance = dot_nt(upper_now[part], values[part])
+                    centre = jnp.sum(chances * dchance, -1, keepdims=True)
+                    dscore = (chances * (dchance - centre)).astype(jnp.bfloat16)
+                    dvalue_part = dot(upper_t[:, part], chances.astype(jnp.bfloat16))
+                    by_key = dot(dscore, keys_extra[part])
+                    turned = dot(dscore, mirror)
+                    wide = pltpu.roll(
+                        jnp.concatenate([turned, jnp.zeros((half, half), jnp.float32)], -1),
+                        0, 1, stride=1, stride_axis=0,
+                    ).astype(jnp.bfloat16)
+                    by_place = dot(wide, backward)
+                    dkey_part = dot(with_u_t[:, part], dscore)
+                    dkey_part = dkey_part[:head_size] + dkey_part[head_size:]
+                    drel_part = dot(with_w_t[:, part], wide)
+                    drel_ref[own_cols] += drel_part[:head_size] + drel_part[head_size:]
+                    if stream == 0:
+                        dkeys_ref[own_cols, part] = dkey_part
+                        dvalues_ref[own_cols, part] = dvalue_part
+                    else:
+                        dkeys_ref[own_cols, part] += dkey_part
+                        dvalues_ref[own_cols, part] += dvalue_part
+                    with_seg, total = by_key[:, head_size : head_size + 1], by_key[:, head_size + 1 : head_size + 2]
+                    seg_i = segment_col[part]
+                    seg_one = with_seg + seg_i * (total - 2.0 * with_seg)
+                    seg_zero = total - seg_one
+                    by_key = by_key[:, :head_size]
+                    by_segment = seg_zero * bias[3] + seg_one * bias[4]
+                    dquery.append((by_key + by_place + by_segment) * scale)
+                    for kind, term in enumerate(
+                        (by_key, by_place, by_segment, seg_zero * with_c[part], seg_one * with_c[part])
+                    ):
+                        heads_sums[kind] = heads_sums[kind] + jnp.sum(term, 0, keepdims=True)
+                dcols_ref[:, cols(stream)] = jnp.concatenate(dquery, 0).astype(jnp.bfloat16)
+            for kind in range(5):
+                dhead_own[kind : kind + 1, own_cols] += heads_sums[kind] * scale
+            if fast and head == 0:
+                after(step, 1, small_middle)
+            if fast and head == heads - 1:
+                after(step, 1, lambda: [scatter.second() for scatter in scatters[1:]])
+                after(step, 2, lambda: [scatter.third() for scatter in scatters])
+        dcols_ref[:, 2 * width : 3 * width] = (dkeys_ref[...] * (1.0 / LOG2E)).astype(jnp.bfloat16).T
+        dcols_ref[:, 3 * width :] = dvalues_ref[...].astype(jnp.bfloat16).T
+        unroll = unroll_matrix(facts_row[3:4, :], length)
+        joined = dot(unroll, dcols_ref[...]).astype(jnp.bfloat16)
+        joined_t = joined.T
+        content, query = content_ref[...], query_ref[...]
+        dweight_ref[0] += dot(joined_t[:width], content) + dot(joined_t[width : 2 * width], query)
+        dweight_ref[1] += dot(joined_t[2 * width : 3 * width], content)
+        dweight_ref[2] += dot(joined_t[3 * width :], content)
+        dinput_ref[0, here] = (
+            dot_nt(joined[:, :width], weight_ref[0])
+            + dot_nt(joined[:, 2 * width : 3 * width], weight_ref[1])
+            + dot_nt(joined[:, 3 * width :], weight_ref[2])
+        ).astype(jnp.bfloat16)
+        dinput_ref[1, here] = dot_nt(joined[:, width : 2 * width], weight_ref[0]).astype(jnp.bfloat16)
+        if fast:
+            after(step, 1, scatters[0].second)
+
+    lax.fori_loop(0, rows, one_row, 0)
+    drel = drel_ref[...] * (1.0 / LOG2E)
+    high = drel.astype(jnp.bfloat16)
+    low = (drel - high.astype(jnp.float32)).astype(jnp.bfloat16)
+    dweight_ref[3] = dot(high, turned_ref[...]) + dot(low, turned_ref[...])
+    cross = [
+        links.push(dinput_ref.at[n, token_part(3)], cross_ref.at[n], "heads", 1) for n in range(2)
+    ]
+    near = [links.push(dinput_ref.at[n, token_part(1)], near_ref.at[n], "heads", 1) for n in range(2)]
+    far = [links.push(cross_ref.at[n], far_ref.at[n], "heads", 2) for n in range(2)]
+    for copy in cross + near:
+        copy.start()
+    for kind in range(4):
+        turned = dweight_ref[kind].astype(jnp.bfloat16).T
+        dwide_ref[kind] = turned.reshape(dwide_ref.shape[1:])
+    if fast:
+        place_y, place_z = dp_here & 1, dp_here >> 1
+        dweight_first = links.push(dwide_ref.at[:, :, 1 - place_y], dweight_got, "dp", 1)
+        dweight_first.start()
+        head_copies = [links.push(dhead_own, head_got.at[dp_here], "dp", k) for k in range(1, parts)]
+        for copy in head_copies:
+            copy.start()
+        head_got[dp_here] = dhead_own[...]
+    for n in range(2):
+        cross[n].wait()
+        both = cross_ref[n].astype(jnp.float32) + dinput_ref[n, token_part(2)].astype(jnp.float32)
+        cross_ref[n] = both.astype(jnp.bfloat16)
+        far[n].start()
+    if fast:
+        dweight_first.wait()
+        dweight_second = []
+        for kind in range(4):
+            dweight_got[kind] = (
+                dweight_got[kind].astype(jnp.float32) + dwide_ref[kind, :, place_y].astype(jnp.float32)
+            ).astype(jnp.bfloat16)
+        for m in range(1, 4):
+            dweight_second.append(
+                links.push(dweight_got.at[:, place_z ^ m], dweight_more.at[m - 1], "dp", 2 * m)
+            )
+            dweight_second[-1].start()
+        up_share, down_share, out_share, proj_share, small_sum, norm_ref = outputs[3:]
+        squares = jnp.zeros((1, 1), jnp.float32)
+        for copy in small_second:
+            copy.wait()
+        total = small_more[0]
+        for k in range(1, parts):
+            total = total + small_more[k]
+        small_sum[...] = total
+        squares = squares + square_sum(total) / (group * parts)
+        for copy in head_copies:
+            copy.wait()
+        total = head_got[0]
+        for k in range(1, parts):
+            total = total + head_got[k]
+        dhead_ref[...] = total
+        squares = squares + square_sum(total) / parts
+        for scatter, share in zip(scatters, (up_share, down_share, out_share)):
+            share[...] = scatter.last()
+            squares = squares + square_sum(share[...])
+        for copy in dweight_second:
+            copy.wait()
+        for kind in range(4):
+            total = dweight_got[kind, place_z].astype(jnp.float32)
+            for m in range(1, 4):
+                total = total + dweight_more[m - 1, kind].astype(jnp.float32)
+            proj_share[kind] = total
+            squares = squares + square_sum(total)
+        tile_ref[...] = jnp.broadcast_to(squares, tile_ref.shape)
+        tile_got[heads_here] = tile_ref[...]
+        tile_first = [links.push(tile_ref, tile_got.at[heads_here], "heads", k) for k in range(1, group)]
+        for copy in tile_first:
+            copy.start()
+    else:
+        dhead_ref[...] = dhead_own[...]
+        outputs[3][...] = dwide_ref[...]
+    if fast:
+        for copy in tile_first:
+            copy.wait()
+        total = tile_got[0]
+        for k in range(1, group):
+            total = total + tile_got[k]
+        tile_more[dp_here] = total
+        tile_ref[...] = total
+        tile_second = [links.push(tile_ref, tile_more.at[dp_here], "dp", k) for k in range(1, parts)]
+        for copy in tile_second:
+            copy.start()
+    dresid_copy.wait()
+    for n, place in enumerate((content_grad_ref, query_grad_ref)):
+        near[n].wait()
+        far[n].wait()
+        place[...] = (
+            dresid_ref[n]
+            + dinput_ref[n, token_part(0)].astype(jnp.float32)
+            + near_ref[n].astype(jnp.float32)
+            + far_ref[n].astype(jnp.float32)
         )
-        for copy in copies:
+    if fast:
+        for copy in tile_second:
             copy.wait()
-        relative_ref[...] = dot(table_ref[...], weight_ref[3]).astype(jnp.bfloat16)
-        backward_ref[...] = dot(turned_ref[...], weight_ref[3]).astype(jnp.bfloat16)
-        drel_ref[...] = jnp.zeros_like(drel_ref)
-        dweight_ref[...] = jnp.zeros_like(dweight_ref)
-        dhead_ref[...] = jnp.zeros_like(dhead_ref)
-
-    here = pl.ds(pl.multiple_of(row * length, length), length)
-    content_ref, query_ref = content_all.at[here], query_all.at[here]
-    facts_row, facts_col = row_ref[0], col_ref[0]
-    write_masks(mask_ref, facts_row, facts_col, half)
-    roll = roll_matrix(facts_col[:, 3:4], length)
-    upper = dot(roll, jnp.concatenate([upper_all[0, here], upper_all[1, here]], -1)).astype(jnp.bfloat16)
-    segment_col, segment_row = facts_col[:, 2:3], facts_row[2:3, :]
-    down = lax.broadcasted_iota(jnp.int32, (half, half), 0)
-    along = lax.broadcasted_iota(jnp.int32, (half, half), 1)
-    mirror = jnp.where(down + along == half - 1, 1.0, 0.0).astype(jnp.bfloat16)
-    lane = lax.broadcasted_iota(jnp.int32, (length, head_size), 1)
-    extra = jnp.where(lane == 0, segment_col, jnp.where(lane == 1, 1.0, 0.0)).astype(jnp.bfloat16)
-    for head in range(heads):
-        own_cols = slice(head * head_size, (head + 1) * head_size)
-        cols = lambda kind: slice(kind * width + head * head_size, kind * width + (head + 1) * head_size)
-        bias = [bias_ref[kind : kind + 1, own_cols] for kind in range(5)]
-        keys, values = proj_ref[0, :, cols(1)], proj_ref[0, :, cols(2)]
-        keys_twice = jnp.concatenate([keys, keys], -1)
-        keys_extra = jnp.concatenate([keys, extra], -1)
-        relative = relative_ref[:, own_cols]
-        relative_twice = jnp.concatenate([relative, relative], -1)
-        backward = backward_ref[:, own_cols]
-        heads_sums = [jnp.zeros((1, head_size), jnp.float32) for _ in range(5)]
-        for stream in range(2):
-            with_u, with_w, with_c, own, slope = query_sides(
-                proj_ref[0, :, cols(3 * stream)], bias, segment_col, factor
-            )
-            index = stream * heads + head
-            own = own - logsum_ref[0, :, index : index + 1]
-            upper_now = upper[:, index * head_size : (index + 1) * head_size]
-            with_u_t, with_w_t, upper_t = with_u.T, with_w.T, upper_now.T
-            dquery = []
-            for block in range(2):
-                part = slice(block * half, (block + 1) * half)
-                scores = block_scores(
-                    with_u[part], with_w[part], keys_twice[part], relative_twice, half
-                )
-                scores = scores + own[part] + slope[part] * segment_row[:, part] + mask_ref[stream, block]
-                chances = jnp.exp2(scores)
-                dchance = dot_nt(upper_now[part], values[part])
-                centre = jnp.sum(chances * dchance, -1, keepdims=True)
-                dscore = (chances * (dchance - centre)).astype(jnp.bfloat16)
-                dvalue_part = dot(upper_t[:, part], chances.astype(jnp.bfloat16))
-                by_key = dot(dscore, keys_extra[part])
-                turned = dot(dscore, mirror)
-                wide = pltpu.roll(
-                    jnp.concatenate([turned, jnp.zeros((half, half), jnp.float32)], -1),
-                    0, 1, stride=1, stride_axis=0,
-                ).astype(jnp.bfloat16)
-                by_place = dot(wide, backward)
-                dkey_part = dot(with_u_t[:, part], dscore)
-                dkey_part = dkey_part[:head_size] + dkey_part[head_size:]
-                drel_part = dot(with_w_t[:, part], wide)
-                drel_ref[own_cols] += drel_part[:head_size] + drel_part[head_size:]
-                if stream == 0:
-                    dkeys_ref[own_cols, part] = dkey_part
-                    dvalues_ref[own_cols, part] = dvalue_part
-                else:
-                    dkeys_ref[own_cols, part] += dkey_part
-                    dvalues_ref[own_cols, part] += dvalue_part
-                with_seg, total = by_key[:, head_size : head_size + 1], by_key[:, head_size + 1 : head_size + 2]
-                seg_i = segment_col[part]
-                seg_one = with_seg + seg_i * (total - 2.0 * with_seg)
-                seg_zero = total - seg_one
-                by_key = by_key[:, :head_size]
-                by_segment = seg_zero * bias[3] + seg_one * bias[4]
-                dquery.append((by_key + by_place + by_segment) * scale)
-                for kind, term in enumerate(
-                    (by_key, by_place, by_segment, seg_zero * with_c[part], seg_one * with_c[part])
-                ):
-                    heads_sums[kind] = heads_sums[kind] + jnp.sum(term, 0, keepdims=True)
-            dcols_ref[:, cols(stream)] = jnp.concatenate(dquery, 0).astype(jnp.bfloat16)
-        for kind in range(5):
-            dhead_ref[kind : kind + 1, own_cols] += heads_sums[kind] * scale
-    dcols_ref[:, 2 * width : 3 * width] = (dkeys_ref[...] * (1.0 / LOG2E)).astype(jnp.bfloat16).T
-    dcols_ref[:, 3 * width :] = dvalues_ref[...].astype(jnp.bfloat16).T
-    unroll = unroll_matrix(facts_row[3:4, :], length)
-    joined = dot(unroll, dcols_ref[...]).astype(jnp.bfloat16)
-    joined_t = joined.T
-    content, query = content_ref[...], query_ref[...]
-    dweight_ref[0] += dot(joined_t[:width], content) + dot(joined_t[width : 2 * width], query)
-    dweight_ref[1] += dot(joined_t[2 * width : 3 * width], content)
-    dweight_ref[2] += dot(joined_t[3 * width :], content)
-    dinput_ref[0, here] = (
-        dot_nt(joined[:, :width], weight_ref[0])
-        + dot_nt(joined[:, 2 * width : 3 * width], weight_ref[1])
-        + dot_nt(joined[:, 3 * width :], weight_ref[2])
-    ).astype(jnp.bfloat16)
-    dinput_ref[1, here] = dot_nt(joined[:, width : 2 * width], weight_ref[0]).astype(jnp.bfloat16)
-
-    @pl.when(row == pl.num_programs(0) - 1)
-    def _():
-        drel = drel_ref[...] * (1.0 / LOG2E)
-        high = drel.astype(jnp.bfloat16)
-        low = (drel - high.astype(jnp.float32)).astype(jnp.bfloat16)
-        dweight_ref[3] = dot(high, turned_ref[...]) + dot(low, turned_ref[...])
-        tokens, pick = dinput_pieces[0].shape[1], dweight_pieces[0].shape[1]
-        for k in range(group):
-            part = pl.ds(pl.multiple_of((heads_here ^ k) * tokens, tokens), tokens)
-            dinput_pieces[k][...] = dinput_ref[:, part]
-        for kind in range(4):
-            content_all[: weight_ref.shape[1], :width] = dweight_ref[kind].astype(jnp.bfloat16).T
-            for k in range(parts):
-                start = (dp_here ^ k) * pick if parts > 1 else 0
-                dweight_pieces[k][kind] = content_all[pl.ds(pl.multiple_of(start, pick), pick), :width]
+        total = tile_more[0]
+        for k in range(1, parts):
+            total = total + tile_more[k]
+        norm_ref[...] = jnp.sqrt(total)
 
 
 def attention_backward(
-    content_pieces, query_pieces, weight_pieces, tables, head_bias, facts, proj, logsum, upper_pieces
+    content_pieces, query_pieces, weight_pieces, tables, head_bias, facts, proj, logsum, upper_pieces,
+    dresid, gradients, small,
 ):
     rows, length = facts[0].shape[0], facts[0].shape[2]
     group, parts = len(content_pieces), len(weight_pieces)
+    fast = parts > 1
     own, depth = content_pieces[0].shape
     tokens = own * group
-    width = weight_pieces[0].shape[-1]
+    pick, width = weight_pieces[0].shape[1:]
     head_size = head_bias.shape[-1]
     half = length // 2
-    full = lambda *shape: pl.BlockSpec(shape, lambda r: (0,) * len(shape))
+    inside = pl.BlockSpec(memory_space=pltpu.VMEM)
     outside = pl.BlockSpec(memory_space=pl.ANY)
-    results = pl.pallas_call(
-        functools.partial(attention_backward_kernel, head_size, group, parts),
-        grid=(rows,),
-        in_specs=[outside] * (3 * group + parts)
-        + [
-            full(length, depth),
-            full(length, depth),
-            full(5, width),
-            pl.BlockSpec((1, 8, length), lambda r: (r, 0, 0)),
-            pl.BlockSpec((1, length, 8), lambda r: (r, 0, 0)),
-            pl.BlockSpec((1, length, 4 * width), lambda r: (r, 0, 0)),
-            pl.BlockSpec((1, length, 8), lambda r: (r, 0, 0)),
-        ],
-        out_specs=[full(2, own, depth)] * group
-        + [full(*piece.shape) for piece in weight_pieces]
-        + [full(5, width)],
-        out_shape=[jax.ShapeDtypeStruct((2, own, depth), jnp.bfloat16)] * group
-        + [jax.ShapeDtypeStruct(piece.shape, jnp.bfloat16) for piece in weight_pieces]
-        + [jax.ShapeDtypeStruct((5, width), jnp.float32)],
-        scratch_shapes=[
-            pltpu.VMEM((tokens, depth), jnp.bfloat16),
-            pltpu.VMEM((tokens, depth), jnp.bfloat16),
-            pltpu.VMEM((4, depth, width), jnp.bfloat16),
-            pltpu.VMEM((2, tokens, width), jnp.bfloat16),
-            pltpu.VMEM((2, tokens, depth), jnp.bfloat16),
-            pltpu.VMEM((4, width, depth), jnp.float32),
-            pltpu.VMEM((length, width), jnp.bfloat16),
-            pltpu.VMEM((length, width), jnp.bfloat16),
-            pltpu.VMEM((2, 2, half, half), jnp.float32),
-            pltpu.VMEM((width, length), jnp.float32),
-            pltpu.VMEM((length, 4 * width), jnp.bfloat16),
-            pltpu.VMEM((width, length), jnp.float32),
-            pltpu.VMEM((width, length), jnp.float32),
-            pltpu.SemaphoreType.DMA((3 * group + parts,)),
-        ],
-        compiler_params=pltpu.CompilerParams(vmem_limit_bytes=VMEM_LIMIT),
+    bfloat, float32 = jnp.bfloat16, jnp.float32
+    out_shape = [
+        jax.ShapeDtypeStruct((own, depth), float32),
+        jax.ShapeDtypeStruct((own, depth), float32),
+        jax.ShapeDtypeStruct((8, width), float32),
+    ]
+    lanes = max(2 * parts, 2)
+    wide_shape = (4, parts // 2, 2, pick, width) if fast else (4, pick, width)
+    scratch = [
+        pltpu.VMEM((tokens, depth), bfloat),
+        pltpu.VMEM((tokens, depth), bfloat),
+        pltpu.VMEM((4, depth, width), bfloat),
+        pltpu.VMEM((2, tokens, width), bfloat),
+        pltpu.VMEM((2, tokens, depth), bfloat),
+        pltpu.VMEM((4, width, depth), float32),
+        pltpu.VMEM((length, width), bfloat),
+        pltpu.VMEM((length, width), bfloat),
+        pltpu.VMEM((2, 2, half, half), float32),
+        pltpu.VMEM((width, length), float32),
+        pltpu.VMEM((length, 4 * width), bfloat),
+        pltpu.VMEM((width, length), float32),
+        pltpu.VMEM((width, length), float32),
+        pltpu.VMEM(wide_shape, bfloat),
+        pltpu.VMEM((2, own, depth), bfloat),
+        pltpu.VMEM((2, own, depth), bfloat),
+        pltpu.VMEM((2, own, depth), bfloat),
+        pltpu.VMEM((2, own, depth), float32),
+        pltpu.VMEM((8, width), float32),
+        pltpu.SemaphoreType.DMA((2 * group + parts + 5,)),
+        pltpu.SemaphoreType.DMA((64,)),
+        pltpu.SemaphoreType.DMA((64,)),
+    ]
+    if fast:
+        planes = parts // 2
+        columns = [gradient.shape[-1] for gradient in gradients]
+        out_shape += [jax.ShapeDtypeStruct((pick, c), float32) for c in columns]
+        out_shape += [
+            jax.ShapeDtypeStruct((4, pick, width), float32),
+            jax.ShapeDtypeStruct(small.shape, float32),
+            jax.ShapeDtypeStruct((8, 128), float32),
+        ]
+        gradients = [g.reshape(planes, 2, group // 2, pick, g.shape[-1]) for g in gradients]
+        for c in columns:
+            scratch += [
+                pltpu.VMEM((planes, 2, pick, c), bfloat),
+                pltpu.VMEM((planes, 2, pick, c), bfloat),
+                pltpu.VMEM((planes, pick, c), bfloat),
+                pltpu.VMEM((planes - 1, pick, c), bfloat),
+            ]
+        scratch += [
+            pltpu.VMEM((group,) + small.shape, float32),
+            pltpu.VMEM((parts,) + small.shape, float32),
+            pltpu.VMEM(small.shape, float32),
+            pltpu.VMEM((4, planes, pick, width), bfloat),
+            pltpu.VMEM((planes - 1, 4, pick, width), bfloat),
+            pltpu.VMEM((parts, 8, width), float32),
+            pltpu.VMEM((8, 128), float32),
+            pltpu.VMEM((group, 8, 128), float32),
+            pltpu.VMEM((parts, 8, 128), float32),
+        ]
+    else:
+        out_shape += [jax.ShapeDtypeStruct(wide_shape, bfloat)]
+    return pl.pallas_call(
+        functools.partial(attention_backward_kernel, head_size, group, parts, fast),
+        in_specs=[outside] * (3 * group + parts + 1) + [inside] * 7 + [outside] * 3 + [inside],
+        out_specs=[inside] * len(out_shape),
+        out_shape=out_shape,
+        scratch_shapes=scratch,
+        compiler_params=pltpu.CompilerParams(
+            vmem_limit_bytes=VMEM_LIMIT, collective_id=2, has_side_effects=True
+        ),
     )(
-        *content_pieces, *query_pieces, *weight_pieces, *upper_pieces, *tables,
-        head_bias.reshape(5, width), *facts, proj, logsum,
-    )
-    return results[:group], results[group : group + parts], results[-1]
+        *content_pieces, *query_pieces, *weight_pieces, *upper_pieces, dresid, *tables,
+        head_bias.reshape(5, width), *facts, proj, logsum, *gradients, small,
+    )
 
 
 def norm_parts(values):
@@ -512,10 +770,13 @@
     dmixed_pieces, refs = refs[:group], refs[group:]
     dup_hbm, ddown_hbm, dout_ref, dsmall_ref, refs = refs[0], refs[1], refs[2], refs[3], refs[4:]
     up_ref, down_ref, out_ref, hidden_ref, slope_ref, bias_ref = refs[:6]
-    low_ref, low_t_ref, normed_ref, total_ref, sems = refs[6:]
+    low_ref, low_t_ref, normed_ref, total_ref, up_got, down_got, out_got, out_sent = refs[6:14]
+    sems, send_sems, recv_sems = refs[14:]
     own, depth = content_ref.shape
     tokens = 2 * own
     here = lax.axis_index("heads")
+    core = here & 1
+    chips = group // 2
     loads = [
         pltpu.make_async_copy(out_hbm.at[:, j], out_ref.at[j], sems.at[j]) for j in range(group)
     ]
@@ -528,6 +789,7 @@
     ]
     for load in loads:
         load.start()
+    greet("heads", [1])
     for k in range(group):
         bias_ref[here ^ k] = bias_pieces[k][...]
     gain_one, bias_one, bias_out, gain_two, bias_two = [norm_ref[i : i + 1] for i in range(5)]
@@ -551,16 +813,17 @@
         load.wait()
 
     def forward(j, carry):
-        before = dot(low_ref[...], up_ref[j].reshape(depth, hidden)) + bias_ref[j]
-        square = before * before
-        bent = jnp.tanh(GELU_FACTOR * before * (1.0 + GELU_CUBIC * square))
-        half_up = 0.5 * (1.0 + bent)
-        hidden_now = (before * half_up).astype(jnp.bfloat16)
-        slope_ref[j] = half_up + 0.5 * before * (1.0 - bent * bent) * GELU_FACTOR * (
-            1.0 + 3.0 * GELU_CUBIC * square
-        )
-        hidden_ref[j] = hidden_now.reshape(hidden_ref.shape[1:])
-        total_ref[...] += dot_nt(hidden_now, down_ref[j].reshape(depth, hidden))
+        for part in (slice(0, own), slice(own, tokens)):
+            before = dot(low_ref[part], up_ref[j].reshape(depth, hidden)) + bias_ref[j]
+            square = before * before
+            bent = jnp.tanh(GELU_FACTOR * before * (1.0 + GELU_CUBIC * square))
+            half_up = 0.5 * (1.0 + bent)
+            hidden_now = (before * half_up).astype(jnp.bfloat16)
+            slope_ref[j, part] = half_up + 0.5 * before * (1.0 - bent * bent) * GELU_FACTOR * (
+                1.0 + 3.0 * GELU_CUBIC * square
+            )
+            hidden_ref[j, part] = hidden_now
+            total_ref[part] += dot_nt(hidden_now, down_ref[j].reshape(depth, hidden))
         return carry
 
     lax.fori_loop(0, group, forward, 0)
@@ -577,44 +840,99 @@
     dlow = dfinal.astype(jnp.bfloat16)
     dlow_t = dlow.T
 
-    def backward(j, carry):
-        hidden_now = hidden_ref[j].reshape(tokens, hidden)
-        down_now = down_ref[j].reshape(depth, hidden)
-        dhidden = dot(dlow, down_now)
-        down_ref[j] = dot(dlow_t, hidden_now).astype(jnp.bfloat16).reshape(down_ref.shape[1:])
-        dbefore = (dhidden * slope_ref[j]).astype(jnp.bfloat16)
-        dsmall_ref[pl.ds(j, 1)] = column_sum(dbefore.astype(jnp.float32))
-        total_ref[...] += dot_nt(dbefore, up_ref[j].reshape(depth, hidden))
-        up_ref[j] = dot(low_t_ref[...], dbefore).astype(jnp.bfloat16).reshape(up_ref.shape[1:])
+    def to_sibling(source, place, index):
+        return pltpu.make_async_remote_copy(
+            source, place, send_sems.at[index], recv_sems.at[index],
+            device_id={"heads": here ^ 1}, device_id_type=pl.DeviceIdType.MESH,
+        )
+
+    def back_block(j):
+        ddown = dot(dlow_t, hidden_ref[j])
+        bias_grad = jnp.zeros((1, hidden), jnp.float32)
+        for part in (slice(0, own), slice(own, tokens)):
+            dhidden = dot(dlow[part], down_ref[j].reshape(depth, hidden))
+            dbefore = (dhidden * slope_ref[j, part]).astype(jnp.bfloat16)
+            bias_grad = bias_grad + column_sum(dbefore.astype(jnp.float32))
+            total_ref[part] += dot_nt(dbefore, up_ref[j].reshape(depth, hidden))
+            hidden_ref[j, part] = dbefore
+        dsmall_ref[pl.ds(j, 1)] = bias_grad
+        return dot(low_t_ref[...], hidden_ref[j]), ddown
+
+    def sent(chip):
+        j = 2 * chip + 1 - core
+        return [
+            to_sibling(up_ref.at[j], up_got.at[chip], 2 * chip),
+            to_sibling(down_ref.at[j], down_got.at[chip], 2 * chip + 1),
+        ]
+
+    def kept(chip):
+        j = 2 * chip + core
+        return [
+            pltpu.make_async_copy(up_ref.at[j], dup_hbm.at[:, chip], sems.at[chip]),
+            pltpu.make_async_copy(down_ref.at[j], ddown_hbm.at[:, chip], sems.at[group + chip]),
+        ]
+
+    def backward_sent(chip, carry):
+        j = 2 * chip + 1 - core
+        dup, ddown = back_block(j)
+        up_ref[j] = dup.astype(jnp.bfloat16).reshape(up_ref.shape[1:])
+        down_ref[j] = ddown.astype(jnp.bfloat16).reshape(down_ref.shape[1:])
+        for copy in sent(chip):
+            copy.start()
         return carry
 
-    lax.fori_loop(0, group, backward, 0)
-    stores = [
-        pltpu.make_async_copy(up_ref.at[j], dup_hbm.at[:, j], sems.at[group + j]) for j in range(group)
-    ]
-    stores += [
-        pltpu.make_async_copy(down_ref.at[j], ddown_hbm.at[:, j], sems.at[2 * group + j])
-        for j in range(group)
-    ]
-    for store in stores:
-        store.start()
+    def backward_kept(chip, carry):
+        j = 2 * chip + core
+        dup, ddown = back_block(j)
+        for copy in sent(chip):
+            copy.wait_recv()
+        dup = dup + up_got[chip].astype(jnp.float32).reshape(depth, hidden)
+        ddown = ddown + down_got[chip].astype(jnp.float32).reshape(depth, hidden)
+        up_ref[j] = dup.astype(jnp.bfloat16).reshape(up_ref.shape[1:])
+        down_ref[j] = ddown.astype(jnp.bfloat16).reshape(down_ref.shape[1:])
+        for copy in kept(chip):
+            copy.start()
+        return carry
+
+    lax.fori_loop(0, chips, backward_sent, 0)
+    lax.fori_loop(0, chips, backward_kept, 0)
     dmiddle = total_ref[...]
     normed = normed_ref[...]
     dsmall_ref[group : group + 1] = column_sum(dmiddle * normed)
     dsmall_ref[group + 1 : group + 2] = column_sum(dmiddle)
     dresid = norm_back(dmiddle, normed, inverse_one, gain_one)
-    dresid_ref[...] = dresid.reshape(dresid_ref.shape)
+    total_ref[...] = dresid
+    dresid_copy = pltpu.make_async_copy(total_ref, dresid_ref, sems.at[0])
+    dresid_copy.start()
     dlow = dresid.astype(jnp.bfloat16)
     dlow_t = dlow.T
+    out_copies = [
+        to_sibling(out_sent.at[chip], out_got.at[chip], 2 * chips + chip) for chip in range(chips)
+    ]
+    for chip in range(chips):
+        k = 2 * chip + 1
+        mixed = mixed_pieces[k][...].reshape(tokens, -1)
+        out_sent[chip] = dot(dlow_t, mixed).astype(jnp.bfloat16).reshape(out_sent.shape[1:])
+        out_copies[chip].start()
     for k in range(group):
-        mixed = mixed_pieces[k][...].reshape(tokens, -1)
         dmixed_pieces[k][...] = (
             dot(dlow, out_block(k)).astype(jnp.bfloat16).reshape(dmixed_pieces[k].shape)
         )
-        dout_ref[here ^ k] = dot(dlow_t, mixed).astype(jnp.bfloat16).reshape(dout_ref.shape[1:])
+    for chip in range(chips):
+        k = 2 * chip
+        mixed = mixed_pieces[k][...].reshape(tokens, -1)
+        dout = dot(dlow_t, mixed)
+        out_copies[chip].wait_recv()
+        dout = dout + out_got[chip].astype(jnp.float32).reshape(dout.shape)
+        dout_ref[:, (here ^ k) >> 1] = dout.astype(jnp.bfloat16).reshape(out_sent.shape[1:])
     dsmall_ref[group + 5 :] = jnp.zeros((dsmall_ref.shape[0] - group - 5, depth), jnp.float32)
-    for store in stores:
-        store.wait()
+    dresid_copy.wait()
+    for chip in range(chips):
+        for copy in sent(chip):
+            copy.wait_send()
+        out_copies[chip].wait_send()
+        for copy in kept(chip):
+            copy.wait()
 
 
 def feed_layer(mixed_pieces, bias_pieces, content, query, dcontent, dquery, norm_param, up, down, out):
@@ -628,17 +946,17 @@
     results = pl.pallas_call(
         functools.partial(feed_kernel, group),
         in_specs=[inside] * (2 * group + 5) + [outside] * 3,
-        out_specs=[inside] * (3 + group) + [outside, outside, inside, inside],
+        out_specs=[inside, inside, outside] + [inside] * group + [outside, outside, inside, inside],
         out_shape=[
             jax.ShapeDtypeStruct((own, depth), jnp.bfloat16),
             jax.ShapeDtypeStruct((own, depth), jnp.bfloat16),
-            jax.ShapeDtypeStruct((2, own, depth), jnp.float32),
+            jax.ShapeDtypeStruct((tokens, depth), jnp.float32),
         ]
         + [jax.ShapeDtypeStruct((2, own, width), jnp.bfloat16)] * group
         + [
-            jax.ShapeDtypeStruct(up.shape, jnp.bfloat16),
-            jax.ShapeDtypeStruct(down.shape, jnp.bfloat16),
-            jax.ShapeDtypeStruct((group, parts, pick, width), jnp.bfloat16),
+            jax.ShapeDtypeStruct((parts, group // 2, pick, hidden), jnp.bfloat16),
+            jax.ShapeDtypeStruct((parts, group // 2, pick, hidden), jnp.bfloat16),
+            jax.ShapeDtypeStruct((parts, group // 2, pick, width), jnp.bfloat16),
             jax.ShapeDtypeStruct((16, depth), jnp.float32),
         ],
         scratch_shapes=[
@@ -652,11 +970,19 @@
             pltpu.VMEM((depth, tokens), jnp.bfloat16),
             pltpu.VMEM((tokens, depth), jnp.float32),
             pltpu.VMEM((tokens, depth), jnp.float32),
+            pltpu.VMEM((group // 2, parts, pick, hidden), jnp.bfloat16),
+            pltpu.VMEM((group // 2, parts, pick, hidden), jnp.bfloat16),
+            pltpu.VMEM((group // 2, parts, pick, width), jnp.bfloat16),
+            pltpu.VMEM((group // 2, parts, pick, width), jnp.bfloat16),
             pltpu.SemaphoreType.DMA((3 * group,)),
+            pltpu.SemaphoreType.DMA((3 * group // 2,)),
+            pltpu.SemaphoreType.DMA((3 * group // 2,)),
         ],
-        compiler_params=pltpu.CompilerParams(vmem_limit_bytes=VMEM_LIMIT),
+        compiler_params=pltpu.CompilerParams(
+            vmem_limit_bytes=VMEM_LIMIT, collective_id=1, has_side_effects=True
+        ),
     )(*mixed_pieces, *bias_pieces, content, query, dcontent, dquery, norm_param, up, down, out)
-    return results[0], results[1], results[2], results[3 : 3 + group], results[3 + group :]
+    return results[0], results[1], results[2].reshape(2, own, depth), results[3 : 3 + group], results[3 + group :]
 
 
 def exchange(value, axis, mask):
@@ -674,10 +1000,6 @@
 def gather_heads(own):
     far = exchange(own, "heads", 2)
     return [own, exchange(own, "heads", 1), far, exchange(far, "heads", 1)]
-
-
-def spread(pieces):
-    return [pieces[0]] + [exchange(pieces[k], "heads", k) for k in range(1, len(pieces))]
 
 
 def by_pieces(pick):
@@ -697,12 +1019,7 @@
 
 
 def reduce_projection(pieces):
-    if len(pieces) == 1:
-        return lax.psum_scatter(pieces[0], "dp", scatter_dimension=1, tiled=True).astype(jnp.float32)
-    total = pieces[0].astype(jnp.float32)
-    for k in range(1, len(pieces)):
-        total = total + exchange(pieces[k], "dp", k).astype(jnp.float32)
-    return total
+    return lax.psum_scatter(pieces[0], "dp", scatter_dimension=1, tiled=True).astype(jnp.float32)
 
 
 def gather_all(own):
@@ -715,13 +1032,11 @@
 
 
 def scatter_all(full):
-    dp, heads = lax.axis_size("dp"), lax.axis_size("heads")
-    parts, _, rows, columns = full.shape
-    if parts == 1:
-        rows = rows // dp
-        full = jnp.swapaxes(full.reshape(heads, dp, rows, columns), 0, 1)
-    full = full.reshape(dp * heads * rows, columns)
-    return lax.psum_scatter(full, ("dp", "heads"), scatter_dimension=0, tiled=True).astype(jnp.float32)
+    chip = lax.axis_index("heads") // 2
+    mine = lax.dynamic_index_in_dim(full[0], chip, 0, False)
+    theirs = lax.dynamic_index_in_dim(full[0], 1 - chip, 0, False)
+    mine = mine.astype(jnp.float32) + exchange(theirs, "heads", 2).astype(jnp.float32)
+    return lax.psum_scatter(mine, "dp", scatter_dimension=0, tiled=True)
 
 
 def adam_step(master, first, second, gradient, factor, decayed):
@@ -787,34 +1102,28 @@
         mixed_pieces, bias_pieces, content_in, query_in, content_grad, query_grad, norm_param,
         up_full, down_full, out_full,
     )
-    dinput_pieces, dweight_pieces, dhead = attention_backward(
+    backward = attention_backward(
         content_pieces, query_pieces, weight_pieces, tables, head_bias, facts, proj, logsum,
-        spread(dmixed_pieces),
-    )
-    small_sum = total_over(total_over(dsmall, "heads"), "dp")
-    up_share = scatter_all(dup)
-    down_share = scatter_all(ddown).T
-    out_share = scatter_all(jnp.swapaxes(dout, 0, 1)).T
-    proj_share = reduce_projection(dweight_pieces)
-    head_grad = total_over(dhead, "dp").reshape(head_bias.shape)
-    near = exchange(dinput_pieces[1], "heads", 1).astype(jnp.float32)
-    far = exchange(dinput_pieces[3], "heads", 1).astype(jnp.float32)
-    far = (dinput_pieces[2].astype(jnp.float32) + far).astype(jnp.bfloat16)
-    far = exchange(far, "heads", 2).astype(jnp.float32)
-    input_grad = dresid + dinput_pieces[0].astype(jnp.float32) + near + far
+        dmixed_pieces, dresid, (dup, ddown, dout), dsmall,
+    )
     heads_count, head_index = lax.axis_size("heads"), lax.axis_index("heads")
+    if len(weight_pieces) > 1:
+        input_grad, dhead = backward[:2], backward[2]
+        up_share, down_share, out_share, proj_share, small_sum, norm_tile = backward[3:]
+        grad_norm = norm_tile[0, 0]
+    else:
+        input_grad, dhead = backward[:2], total_over(backward[2], "dp")
+        proj_share = reduce_projection([backward[3]])
+        up_share, down_share, out_share = scatter_all(dup), scatter_all(ddown), scatter_all(dout)
+        small_sum = total_over(total_over(dsmall, "heads"), "dp")
+        squares = sum(jnp.sum(share * share) for share in (up_share, down_share, out_share, proj_share))
+        squares = squares + jnp.sum(dhead * dhead) / lax.axis_size("dp")
+        squares = squares + jnp.sum(small_sum * small_sum) / (lax.axis_size("dp") * heads_count)
+        grad_norm = jnp.sqrt(total_over(total_over(squares.reshape(1, 1), "heads"), "dp"))[0, 0]
+    down_share, out_share = down_share.T, out_share.T
+    head_grad = dhead[:5].reshape(head_bias.shape)
     bias_sum, norm_sum = small_sum[:heads_count], small_sum[heads_count : heads_count + 5]
     bias_grad = lax.dynamic_slice_in_dim(bias_sum, head_index, 1, 0)[0]
-    dp_count = lax.axis_size("dp")
-    local_squares = (
-        jnp.sum(proj_share * proj_share)
-        + jnp.sum(out_share * out_share)
-        + jnp.sum(up_share * up_share)
-        + jnp.sum(down_share * down_share)
-        + jnp.sum(head_grad * head_grad) / dp_count
-        + (jnp.sum(bias_sum * bias_sum) + jnp.sum(norm_sum * norm_sum)) / (dp_count * heads_count)
-    )
-    grad_norm = jnp.sqrt(total_over(total_over(local_squares.reshape(1, 1), "heads"), "dp"))[0, 0]
     factor = CLIP_NORM / jnp.maximum(grad_norm, CLIP_NORM)
     attn_first, attn_second, attn_new = adam_step(
         attn_proj, attn_proj_first, attn_proj_second, proj_share, factor, True

time: 623 us -> 427 us (0.69)
  waiting for transfers between devices: 300 us -> 71.7 us
  Pallas kernels: 191 us -> 276 us
  starting transfers between devices: 54.7 us -> 17.4 us
  other arithmetic: 31.7 us -> 19.8 us
  between operations: 24 us -> 15.2 us
  local copies, waits for them, and re-layouts: 17.2 us -> 24 us
    reduce_scatter x2 -> x0, waiting for transfers between devices: 163 us -> none  [scatter_all(): lax.psum_scatter(full, ('dp', 'heads'), scatter_dimension=0, tiled=True)]
    pallas_call x1, Pallas kernels: 67.1 us -> 141 us  [attention_backward(): pl.pallas_call(functools.partial(attention_backward_kernel, head_size, gr...]
    ppermute x42 -> x16, waiting for transfers between devices: 68.2 us -> 20.3 us  [exchange(): lax.ppermute(value, axis, [(i, i ^ mask) for i in range(lax.axis_size(axi...]
    ppermute x42 -> x16, starting transfers between devices: 54.4 us -> 17.2 us  [exchange(): lax.ppermute(value, axis, [(i, i ^ mask) for i in range(lax.axis_size(axi...]
    all_gather x3, waiting for transfers between devices: 67.5 us -> 51.4 us  [gather_all(): lax.all_gather(own, ('dp', 'heads'), axis=0, tiled=False)]
    pallas_call x1, Pallas kernels: 79.8 us -> 90.6 us  [attention_forward(): pl.pallas_call(functools.partial(attention_forward_kernel, head_size, gro...]
    reduce_sum x6 -> x0, other arithmetic: 9.23 us -> none  [the longest x1 2.29 us: local(): jnp.sum(proj_share * proj_share) + jnp.sum(out_share * out_share)]
    unnamed x115 -> x100, local copies, waits for them, and re-layouts: 8.31 us -> 15.1 us
  transfers between devices with their start and end apart: 48 -> 19, of which waited for: 24 -> 6; matrix products, arithmetic and copies ran while one was open for 5% -> 5% of each run, Pallas kernels for 24% -> 21%
where the time goes in v3:
time: 427 us; the launch traced here: 424 us
  Pallas kernels  276 us (65%)
  waiting for transfers between devices  71.7 us (17%)
  local copies, waits for them, and re-layouts  24 us (6%)
  other arithmetic  19.8 us (5%)
  starting transfers between devices  17.4 us (4%)
  between operations  15.2 us (4%)
    pallas_call x1, Pallas kernels, attention_backward(): pl.pallas_call(functools.partial(attention_backward_kernel, head_size, gr...  141 us
    pallas_call x1, Pallas kernels, attention_forward(): pl.pallas_call(functools.partial(attention_forward_kernel, head_size, gro...  90.6 us
    all_gather x3, waiting for transfers between devices, gather_all(): lax.all_gather(own, ('dp', 'heads'), axis=0, tiled=False)  51.4 us
    pallas_call x1, Pallas kernels, feed_layer(): pl.pallas_call(functools.partial(feed_kernel, group), in_specs=[inside] *...  43.6 us
    ppermute x16, waiting for transfers between devices, exchange(): lax.ppermute(value, axis, [(i, i ^ mask) for i in range(lax.axis_size(axi...  20.3 us
    ppermute x16, starting transfers between devices, exchange(): lax.ppermute(value, axis, [(i, i ^ mask) for i in range(lax.axis_size(axi...  17.2 us
    unnamed x100, local copies, waits for them, and re-layouts  15.1 us
  transfers between devices with their start and end apart: 19, of which 6 were waited for; matrix products, arithmetic and copies ran while one was open for 5% of the time, Pallas kernels for 21%

profile of v3, /device:TPU:0, one launch (start us, length us, event | category | flops | bytes accessed | tf_op | source)
XLA Modules:
  0.0 423.7 jit_solution(18254381094692243705)
XLA Ops:
  7.3 1.0 copy.124
  9.0 1.6 convert_element_type.27
  10.7 1.6 convert_bitcast_fusion
  12.4 3.0 collective-permute-start.1
  15.5 1.0 convert_element_type.24.refs_8_
  16.5 3.1 collective-permute-start.9
  19.6 1.6 collective-permute-start.7
  21.2 1.5 collective-permute-start.6
  22.7 0.8 select_reduce_fusion.2
  23.5 0.8 select_reduce_fusion.3
  24.3 4.2 %collective-permute-done.9.refs_12_ = bf16[4,96,192]{2,1,0:T(8,128)(2,1)S(1)} collective-permute-done((bf16[4,96,192]{2,1,0:T(8,128)(2,1)S(1)}, bf16[4,96,192]{2,1,0:T(8,128)(2,1)S(1)}, u32[]{:S(2)}, u32[]{:S(2)}) %collective-permute-start.9) | collective-permute-done | bytes 147488 | tf_op jit(solution)/shard_map/ppermute | solution.py:989
  28.5 0.9 collective-permute-start.11
  29.4 1.5 collective-permute-start.10
  31.1 3.8 collective-permute-done.11.refs_14_
  34.9 0.9 collective-permute-done.10.refs_13_
  35.8 1.5 collective-permute-start.8
  37.3 5.8 %collective-permute-done.4.refs_6_ = bf16[384,768]{1,0:T(8,128)(2,1)S(1)} collective-permute-done((bf16[384,768]{1,0:T(8,128)(2,1)}, bf16[384,768]{1,0:T(8,128)(2,1)S(1)}, u32[]{:S(2)}, u32[]{:S(2)}) %collective-permute-start.4) | collective-permute-done | bytes 589856 | tf_op jit(solution)/shard_map/ppermute | solution.py:989
  43.2 1.8 select_reduce_fusion
  45.8 2.0 collective-permute-start.12
  47.8 5.5 %collective-permute-done.12.refs_15_ = bf16[4,96,192]{2,1,0:T(8,128)(2,1)S(1)} collective-permute-done((bf16[4,96,192]{2,1,0:T(8,128)(2,1)S(1)}, bf16[4,96,192]{2,1,0:T(8,128)(2,1)S(1)}, u32[]{:S(2)}, u32[]{:S(2)}) %collective-permute-start.12) | collective-permute-done | bytes 147488 | tf_op jit(solution)/shard_map/ppermute | solution.py:989
  53.3 1.8 collective-permute-start.14
  57.2 1.5 stack.14
  58.6 1.4 convert_element_type.26.refs_18_.refs_24_
  60.1 1.9 copy.123
  62.7 1.6 copy.125
  64.3 1.6 copy.126
  66.0 0.8 copy-done.4
  67.0 90.6 %shard_map.541 = (bf16[3,512,768]{2,1,0:T(8,128)(2,1)}, f32[3,512,8]{2,1,0:T(8,128)}, bf16[2,384,192]{2,1,0:T(8,128)(2,1)}, bf16[2,384,192]{2,1,0:T(8,128)(2,1)}...) custom-call(bf16[384,768]{1,0:T(8,128)(2,1)} %refs_0_.3, bf16[384,768]{1,0:T(8,128)(2,1)} %copy-done.2, ...), custom_call_target="tpu_custom_call" | custom-call | tf_op jit(solution)/shard_map/pallas_call | solution.py:253
  157.7 51.3 %all-gather.9.cloned.1.call-done = bf16[3072,768]{1,0:T(8,128)(2,1)} async-done(((bf16[96,768]{1,0:T(8,128)(2,1)}), bf16[3072,768]{1,0:T(8,128)(2,1)}) %all-gather.9.cloned.1.call-update) | async-done | bytes 4718608 | tf_op jit(solution)/shard_map/all_gather | solution.py:1028
  209.0 43.6 %shard_map.542 = (bf16[384,768]{1,0:T(8,128)(2,1)}, bf16[384,768]{1,0:T(8,128)(2,1)}, f32[768,768]{1,0:T(8,128)}, bf16[2,384,192]{2,1,0:T(8,128)(2,1)}, bf16[2,3...) custom-call(bf16[2,384,192]{2,1,0:T(8,128)(2,1)} %get-tuple-element., ...), custom_call_target="tpu_custom_call" | custom-call | tf_op jit(solution)/shard_map/pallas_call | solution.py:946
  252.8 141.4 %shard_map.543 = (f32[384,768]{1,0:T(8,128)}, f32[384,768]{1,0:T(8,128)}, f32[8,192]{1,0:T(8,128)}, f32[96,768]{1,0:T(8,128)}, f32[96,768]{1,0:T(8,128)}, /*inde...) custom-call(bf16[384,768]{1,0:T(8,128)(2,1)} %refs_0_.3, ...), custom_call_target="tpu_custom_call" | custom-call | tf_op jit(solution)/shard_map/pallas_call | solution.py:733
  394.2 1.3 slice.12
  396.3 0.7 slice.14
  397.0 0.8 reshape.232
  397.8 1.0 multiply_subtract_fusion.3
  398.8 0.7 copy.130
  399.5 0.7 copy.131
  400.3 0.7 copy.132
  401.0 1.6 copy.129
  402.7 1.4 multiply_subtract_fusion.4
  404.2 2.2 multiply_subtract_fusion.1
  406.4 2.2 multiply_subtract_fusion.2
  408.7 1.2 multiply_subtract_fusion
  411.2 0.8 copy.142
  412.0 0.8 copy.143
  412.8 1.0 copy.144
  413.8 1.0 copy.145
  414.8 0.7 copy.146
  (126 shorter events, 7.8 us)
Async XLA Ops:
  7.2 54.8 %copy-start.32 = (f32[5,3,64]{2,1,0:T(4,128)S(1)}, f32[5,3,64]{2,1,0:T(4,128)}, u32[]{:S(2)}) copy-start(f32[5,3,64]{2,1,0:T(4,128)} %param.49) | copy-start | bytes 11524
  7.2 150.5 %all-gather.11.cloned.1.call-start = ((), (), s32[]{:S(2)}) async-start(), calls=%async_computation.2 | async-start | bytes 1622016 | tf_op jit(solution)/shard_map/all_gather | solution.py:1028
  8.9 148.8 %all-gather.7.cloned.1.call-start = ((), (), s32[]{:S(2)}) async-start(), calls=%async_computation | async-start | bytes 4866048 | tf_op jit(solution)/shard_map/all_gather | solution.py:1028
  10.7 198.4 %all-gather.9.cloned.1.call-start = ((), (), s32[]{:S(2)}) async-start(), calls=%async_computation.1 | async-start | bytes 4866048 | tf_op jit(solution)/shard_map/all_gather | solution.py:1028
  12.4 24.9 %collective-permute-start.1 = (bf16[384,768]{1,0:T(8,128)(2,1)}, bf16[384,768]{1,0:T(8,128)(2,1)S(1)}, u32[]{:S(2)}, u32[]{:S(2)}) collective-permute-start(bf16[384,768]{1,0:T(8,128)(2,1)} %refs_0_.3), channel_id=1, source_target_pairs={{0,2},{1,3},{2,0},{3,1},{4,6},{5,7},{6,4},{7,5},{8,10},{9,11},{10,... | collective-permute-start | bytes 1769480 | tf_op jit(solution)/shard_map/ppermute | solution.py:989
  15.4 27.7 %collective-permute-start.4 = (bf16[384,768]{1,0:T(8,128)(2,1)}, bf16[384,768]{1,0:T(8,128)(2,1)S(1)}, u32[]{:S(2)}, u32[]{:S(2)}) collective-permute-start(bf16[384,768]{1,0:T(8,128)(2,1)} %refs_4_.3), channel_id=1, source_target_pairs={{0,2},{1,3},{2,0},{3,1},{4,6},{5,7},{6,4},{7,5},{8,10},{9,11},{10,... | collective-permute-start | bytes 1769480 | tf_op jit(solution)/shard_map/ppermute | solution.py:989
  16.5 26.6 %copy-start.6 = (bf16[4,96,192]{2,1,0:T(8,128)(2,1)}, bf16[4,96,192]{2,1,0:T(8,128)(2,1)S(1)}, u32[]{:S(2)}) copy-start(bf16[4,96,192]{2,1,0:T(8,128)(2,1)S(1)} %convert_element_type.24.refs_8_) | copy-start | bytes 442372
  16.5 12.0 %collective-permute-start.9 = (bf16[4,96,192]{2,1,0:T(8,128)(2,1)S(1)}, bf16[4,96,192]{2,1,0:T(8,128)(2,1)S(1)}, u32[]{:S(2)}, u32[]{:S(2)}) collective-permute-start(bf16[4,96,192]{2,1,0:T(8,128)(2,1)S(1)} %convert_element_type.24.refs_8_), channel_id=1, source_target_pairs={{0,16},{4,20},{8,24},{12,28},{16,0},{20,4},{24,8},{28,12},{1,17},{... | collective-permute-start | bytes 442376 | tf_op jit(solution)/shard_map/ppermute | solution.py:989
  19.6 9.8 %collective-permute-start.7 = (bf16[4,96,192]{2,1,0:T(8,128)(2,1)S(1)}, bf16[4,96,192]{2,1,0:T(8,128)(2,1)S(1)}, u32[]{:S(2)}, u32[]{:S(2)}) collective-permute-start(bf16[4,96,192]{2,1,0:T(8,128)(2,1)S(1)} %convert_element_type.24.refs_8_), channel_id=1, source_target_pairs={{0,8},{4,12},{8,0},{12,4},{16,24},{20,28},{24,16},{28,20},{1,9},{5... | collective-permute-start | bytes 442376 | tf_op jit(solution)/shard_map/ppermute | solution.py:989
  21.2 9.8 %collective-permute-start.6 = (bf16[4,96,192]{2,1,0:T(8,128)(2,1)S(1)}, bf16[4,96,192]{2,1,0:T(8,128)(2,1)S(1)}, u32[]{:S(2)}, u32[]{:S(2)}) collective-permute-start(bf16[4,96,192]{2,1,0:T(8,128)(2,1)S(1)} %convert_element_type.24.refs_8_), channel_id=1, source_target_pairs={{0,4},{4,0},{8,12},{12,8},{16,20},{20,16},{24,28},{28,24},{1,5},{5... | collective-permute-start | bytes 442376 | tf_op jit(solution)/shard_map/ppermute | solution.py:989
  28.5 14.6 %copy-start.17 = (bf16[4,96,192]{2,1,0:T(8,128)(2,1)}, bf16[4,96,192]{2,1,0:T(8,128)(2,1)S(1)}, u32[]{:S(2)}) copy-start(bf16[4,96,192]{2,1,0:T(8,128)(2,1)S(1)} %collective-permute-done.9.refs_12_) | copy-start | bytes 442372
  28.5 6.3 %collective-permute-start.11 = (bf16[4,96,192]{2,1,0:T(8,128)(2,1)S(1)}, bf16[4,96,192]{2,1,0:T(8,128)(2,1)S(1)}, u32[]{:S(2)}, u32[]{:S(2)}) collective-permute-start(bf16[4,96,192]{2,1,0:T(8,128)(2,1)S(1)} %collective-permute-done.9.refs_12_), channel_id=1, source_target_pairs={{0,8},{4,12},{8,0},{12,4},{16,24},{20,28},{24,16},{28,20},{1,9},{5... | collective-permute-start | bytes 442376 | tf_op jit(solution)/shard_map/ppermute | solution.py:989
  29.4 25.8 %copy-start.18 = (bf16[4,96,192]{2,1,0:T(8,128)(2,1)}, bf16[4,96,192]{2,1,0:T(8,128)(2,1)S(1)}, u32[]{:S(2)}) copy-start(bf16[4,96,192]{2,1,0:T(8,128)(2,1)S(1)} %collective-permute-done.7.refs_10_) | copy-start | bytes 442372
  29.4 6.4 %collective-permute-start.10 = (bf16[4,96,192]{2,1,0:T(8,128)(2,1)S(1)}, bf16[4,96,192]{2,1,0:T(8,128)(2,1)S(1)}, u32[]{:S(2)}, u32[]{:S(2)}) collective-permute-start(bf16[4,96,192]{2,1,0:T(8,128)(2,1)S(1)} %collective-permute-done.9.refs_12_), channel_id=1, source_target_pairs={{0,4},{4,0},{8,12},{12,8},{16,20},{20,16},{24,28},{28,24},{1,5},{5... | collective-permute-start | bytes 442376 | tf_op jit(solution)/shard_map/ppermute | solution.py:989
  31.0 12.1 %copy-start.19 = (bf16[4,96,192]{2,1,0:T(8,128)(2,1)}, bf16[4,96,192]{2,1,0:T(8,128)(2,1)S(1)}, u32[]{:S(2)}) copy-start(bf16[4,96,192]{2,1,0:T(8,128)(2,1)S(1)} %collective-permute-done.6.refs_9_) | copy-start | bytes 442372
  31.0 22.3 %collective-permute-start = (bf16[384,768]{1,0:T(8,128)(2,1)}, bf16[384,768]{1,0:T(8,128)(2,1)S(1)}, u32[]{:S(2)}, u32[]{:S(2)}) collective-permute-start(bf16[384,768]{1,0:T(8,128)(2,1)} %refs_0_.3), channel_id=1, source_target_pairs={{0,1},{1,0},{2,3},{3,2},{4,5},{5,4},{6,7},{7,6},{8,9},{9,8},{10,11... | collective-permute-start | bytes 1769480 | tf_op jit(solution)/shard_map/ppermute | solution.py:989
  34.9 20.4 %copy-start.20 = (bf16[4,96,192]{2,1,0:T(8,128)(2,1)}, bf16[4,96,192]{2,1,0:T(8,128)(2,1)S(1)}, u32[]{:S(2)}) copy-start(bf16[4,96,192]{2,1,0:T(8,128)(2,1)S(1)} %collective-permute-done.11.refs_14_) | copy-start | bytes 442372
  34.9 20.3 %collective-permute-start.3 = (bf16[384,768]{1,0:T(8,128)(2,1)}, bf16[384,768]{1,0:T(8,128)(2,1)S(1)}, u32[]{:S(2)}, u32[]{:S(2)}) collective-permute-start(bf16[384,768]{1,0:T(8,128)(2,1)} %refs_4_.3), channel_id=1, source_target_pairs={{0,1},{1,0},{2,3},{3,2},{4,5},{5,4},{6,7},{7,6},{8,9},{9,8},{10,11... | collective-permute-start | bytes 1769480 | tf_op jit(solution)/shard_map/ppermute | solution.py:989
  35.8 7.3 %copy-start.21 = (bf16[4,96,192]{2,1,0:T(8,128)(2,1)}, bf16[4,96,192]{2,1,0:T(8,128)(2,1)S(1)}, u32[]{:S(2)}) copy-start(bf16[4,96,192]{2,1,0:T(8,128)(2,1)S(1)} %collective-permute-done.10.refs_13_) | copy-start | bytes 442372
  35.8 10.0 %collective-permute-start.8 = (bf16[4,96,192]{2,1,0:T(8,128)(2,1)S(1)}, bf16[4,96,192]{2,1,0:T(8,128)(2,1)S(1)}, u32[]{:S(2)}, u32[]{:S(2)}) collective-permute-start(bf16[4,96,192]{2,1,0:T(8,128)(2,1)S(1)} %collective-permute-done.7.refs_10_), channel_id=1, source_target_pairs={{0,4},{4,0},{8,12},{12,8},{16,20},{20,16},{24,28},{28,24},{1,5},{5... | collective-permute-start | bytes 442376 | tf_op jit(solution)/shard_map/ppermute | solution.py:989
  37.3 28.7 %copy-start = (bf16[384,768]{1,0:T(8,128)(2,1)}, bf16[384,768]{1,0:T(8,128)(2,1)S(1)}, u32[]{:S(2)}) copy-start(bf16[384,768]{1,0:T(8,128)(2,1)S(1)} %collective-permute-done.1.refs_2_) | copy-start | bytes 1769476
  37.3 28.7 %collective-permute-start.2 = (bf16[384,768]{1,0:T(8,128)(2,1)S(1)}, bf16[384,768]{1,0:T(8,128)(2,1)S(1)}, u32[]{:S(2)}, u32[]{:S(2)}) collective-permute-start(bf16[384,768]{1,0:T(8,128)(2,1)S(1)} %collective-permute-done.1.refs_2_), channel_id=1, source_target_pairs={{0,1},{1,0},{2,3},{3,2},{4,5},{5,4},{6,7},{7,6},{8,9},{9,8},{10,11... | collective-permute-start | bytes 1769480 | tf_op jit(solution)/shard_map/ppermute | solution.py:989
  43.1 22.8 %copy-start.1 = (bf16[384,768]{1,0:T(8,128)(2,1)}, bf16[384,768]{1,0:T(8,128)(2,1)S(1)}, u32[]{:S(2)}) copy-start(bf16[384,768]{1,0:T(8,128)(2,1)S(1)} %collective-permute-done.4.refs_6_) | copy-start | bytes 1769476
  43.1 22.8 %collective-permute-start.5 = (bf16[384,768]{1,0:T(8,128)(2,1)S(1)}, bf16[384,768]{1,0:T(8,128)(2,1)S(1)}, u32[]{:S(2)}, u32[]{:S(2)}) collective-permute-start(bf16[384,768]{1,0:T(8,128)(2,1)S(1)} %collective-permute-done.4.refs_6_), channel_id=1, source_target_pairs={{0,1},{1,0},{2,3},{3,2},{4,5},{5,4},{6,7},{7,6},{8,9},{9,8},{10,11... | collective-permute-start | bytes 1769480 | tf_op jit(solution)/shard_map/ppermute | solution.py:989
  45.7 163.4 %copy-start.38 = (f32[1,768]{1,0:T(1,128)}, f32[1,768]{1,0:T(1,128)S(1)}, u32[]{:S(2)}) copy-start(f32[1,768]{1,0:T(1,128)S(1)} %broadcast_in_dim.76.refs_4_) | copy-start | bytes 9220
  45.8 9.5 %copy-start.22 = (bf16[4,96,192]{2,1,0:T(8,128)(2,1)}, bf16[4,96,192]{2,1,0:T(8,128)(2,1)S(1)}, u32[]{:S(2)}) copy-start(bf16[4,96,192]{2,1,0:T(8,128)(2,1)S(1)} %collective-permute-done.8.refs_11_) | copy-start | bytes 442372
  45.8 7.5 %collective-permute-start.12 = (bf16[4,96,192]{2,1,0:T(8,128)(2,1)S(1)}, bf16[4,96,192]{2,1,0:T(8,128)(2,1)S(1)}, u32[]{:S(2)}, u32[]{:S(2)}) collective-permute-start(bf16[4,96,192]{2,1,0:T(8,128)(2,1)S(1)} %collective-permute-done.11.refs_14_), channel_id=1, source_target_pairs={{0,4},{4,0},{8,12},{12,8},{16,20},{20,16},{24,28},{28,24},{1,5},{5... | collective-permute-start | bytes 442376 | tf_op jit(solution)/shard_map/ppermute | solution.py:989
  53.3 104.3 %collective-permute-start.13 = (f32[1,768]{1,0:T(1,128)S(1)}, f32[1,768]{1,0:T(1,128)}, u32[]{:S(2)}, u32[]{:S(2)}) collective-permute-start(f32[1,768]{1,0:T(1,128)S(1)} %broadcast_in_dim.76.refs_4_), channel_id=1, source_target_pairs={{0,1},{1,0},{2,3},{3,2},{4,5},{5,4},{6,7},{7,6},{8,9},{9,8},{10,11... | collective-permute-start | bytes 9224 | tf_op jit(solution)/shard_map/ppermute | solution.py:989
  53.3 12.7 %copy-start.2 = (bf16[384,768]{1,0:T(8,128)(2,1)}, bf16[384,768]{1,0:T(8,128)(2,1)S(1)}, u32[]{:S(2)}) copy-start(bf16[384,768]{1,0:T(8,128)(2,1)S(1)} %collective-permute-done.refs_1_) | copy-start | bytes 1769476
  53.3 104.3 %collective-permute-start.14 = (f32[1,768]{1,0:T(1,128)S(1)}, f32[1,768]{1,0:T(1,128)}, u32[]{:S(2)}, u32[]{:S(2)}) collective-permute-start(f32[1,768]{1,0:T(1,128)S(1)} %broadcast_in_dim.76.refs_4_), channel_id=1, source_target_pairs={{0,2},{1,3},{2,0},{3,1},{4,6},{5,7},{6,4},{7,5},{8,10},{9,11},{10,... | collective-permute-start | bytes 9224 | tf_op jit(solution)/shard_map/ppermute | solution.py:989
  55.1 10.9 %copy-start.3 = (bf16[384,768]{1,0:T(8,128)(2,1)}, bf16[384,768]{1,0:T(8,128)(2,1)S(1)}, u32[]{:S(2)}) copy-start(bf16[384,768]{1,0:T(8,128)(2,1)S(1)} %collective-permute-done.3.refs_5_) | copy-start | bytes 1769476
  55.1 102.5 %collective-permute-start.15 = (f32[1,768]{1,0:T(1,128)S(1)}, f32[1,768]{1,0:T(1,128)}, u32[]{:S(2)}, u32[]{:S(2)}) collective-permute-start(f32[1,768]{1,0:T(1,128)S(1)} %broadcast_in_dim.76.refs_4_), channel_id=1, source_target_pairs={{0,3},{1,2},{2,1},{3,0},{4,7},{5,6},{6,5},{7,4},{8,11},{9,10},{10,... | collective-permute-start | bytes 9224 | tf_op jit(solution)/shard_map/ppermute | solution.py:989
  252.7 145.1 %copy-start.16 = (f32[192,96]{0,1:T(8,128)S(1)}, f32[192,96]{0,1:T(8,128)}, u32[]{:S(2)}) copy-start(f32[192,96]{0,1:T(8,128)} %copy-done.15) | copy-start | bytes 221188
  252.7 145.1 %copy-start.26 = (f32[192,96]{0,1:T(8,128)S(1)}, f32[192,96]{0,1:T(8,128)}, u32[]{:S(2)}) copy-start(f32[192,96]{0,1:T(8,128)} %copy.125) | copy-start | bytes 221188
  252.7 145.1 %copy-start.27 = (f32[192,96]{0,1:T(8,128)S(1)}, f32[192,96]{0,1:T(8,128)}, u32[]{:S(2)}) copy-start(f32[192,96]{0,1:T(8,128)} %copy.126) | copy-start | bytes 221188
  252.7 149.9 %copy-start.31 = (f32[5,768]{1,0:T(8,128)S(1)}, f32[5,768]{1,0:T(8,128)}, u32[]{:S(2)}) copy-start(f32[5,768]{1,0:T(8,128)} %refs_12_.1) | copy-start | bytes 46084
  252.7 149.9 %copy-start.34 = (f32[5,768]{1,0:T(8,128)S(1)}, f32[5,768]{1,0:T(8,128)}, u32[]{:S(2)}) copy-start(f32[5,768]{1,0:T(8,128)} %param.57) | copy-start | bytes 46084
  252.7 149.9 %copy-start.35 = (f32[5,768]{1,0:T(8,128)S(1)}, f32[5,768]{1,0:T(8,128)}, u32[]{:S(2)}) copy-start(f32[5,768]{1,0:T(8,128)} %param.56) | copy-start | bytes 46084
  252.8 151.4 %copy-start.9 = (f32[768,96]{0,1:T(8,128)S(1)}, f32[768,96]{0,1:T(8,128)}, u32[]{:S(2)}) copy-start(f32[768,96]{0,1:T(8,128)} %param.46) | copy-start | bytes 884740
  252.8 151.4 %copy-start.30 = (f32[768,96]{0,1:T(8,128)S(1)}, f32[768,96]{0,1:T(8,128)}, u32[]{:S(2)}) copy-start(f32[768,96]{0,1:T(8,128)} %param.48) | copy-start | bytes 884740
  394.2 12.2 %copy-start.10 = (f32[96,768]{1,0:T(8,128)S(1)}, f32[96,768]{1,0:T(8,128)}, u32[]{:S(2)}) copy-start(f32[96,768]{1,0:T(8,128)} %param.43) | copy-start | bytes 884740
  394.2 12.2 %copy-start.12 = (f32[96,768]{1,0:T(8,128)S(1)}, f32[96,768]{1,0:T(8,128)}, u32[]{:S(2)}) copy-start(f32[96,768]{1,0:T(8,128)} %get-tuple-element.323) | copy-start | bytes 884740
  394.2 14.4 %copy-start.7 = (f32[4,96,192]{2,1,0:T(8,128)S(1)}, f32[4,96,192]{2,1,0:T(8,128)}, u32[]{:S(2)}) copy-start(f32[4,96,192]{2,1,0:T(8,128)} %param.37) | copy-start | bytes 884740
  394.2 14.4 %copy-start.8 = (f32[4,96,192]{2,1,0:T(8,128)S(1)}, f32[4,96,192]{2,1,0:T(8,128)}, u32[]{:S(2)}) copy-start(f32[4,96,192]{2,1,0:T(8,128)} %get-tuple-element.315) | copy-start | bytes 884740
  394.2 14.4 %copy-start.28 = (f32[4,96,192]{2,1,0:T(8,128)S(1)}, f32[4,96,192]{2,1,0:T(8,128)}, u32[]{:S(2)}) copy-start(f32[4,96,192]{2,1,0:T(8,128)} %param.39) | copy-start | bytes 884740
  394.2 14.4 %copy-start.29 = (f32[4,96,192]{2,1,0:T(8,128)S(1)}, f32[4,96,192]{2,1,0:T(8,128)}, u32[]{:S(2)}) copy-start(f32[4,96,192]{2,1,0:T(8,128)} %param.38) | copy-start | bytes 884740
  397.8 12.7 %copy-start.33 = (f32[5,3,64]{2,1,0:T(4,128)}, f32[5,3,64]{2,1,0:T(4,128)S(1)}, u32[]{:S(2)}) copy-start(f32[5,3,64]{2,1,0:T(4,128)S(1)} %reshape.232) | copy-start | bytes 11524
  404.2 6.9 %copy-start.25 = (bf16[384,768]{1,0:T(8,128)(2,1)S(1)}, bf16[384,768]{1,0:T(8,128)(2,1)}, u32[]{:S(2)}) copy-start(bf16[384,768]{1,0:T(8,128)(2,1)} %get-tuple-element.310) | copy-start | bytes 1769476
  (14 other events, 64.0 us)
Sparse Core Ops, SparseCore 0:
  11.5 58.8 all-gather.10
  73.8 69.3 all-gather.6
  146.7 62.3 all-gather.8

commit v4 on v3

--- a/solution.py
+++ b/solution.py
@@ -48,28 +48,6 @@
     return jnp.concatenate([high, low], -1)
 
 
-def row_facts(segment_ids, doc_lengths, factor_order):
-    rows, length = segment_ids.shape
-    places = jnp.arange(length, dtype=jnp.int32)
-    counts = doc_lengths.shape[1]
-    earlier = jnp.arange(counts)[:, None] <= jnp.arange(counts)[None, :]
-    ends = jnp.sum(jnp.where(earlier[None], doc_lengths[:, :, None], 0), 1)
-    start = jnp.sum(jnp.where(doc_lengths == length // 2, ends - doc_lengths, 0), -1)
-    token = (places[None] + start[:, None]) % length
-    document = jnp.sum((token[:, :, None] >= ends[:, None, :]).astype(jnp.int32), -1)
-    ranking = jnp.sum(
-        jnp.where(factor_order[:, :, None] == token[:, None, :], places[None, :, None], 0), 1
-    )
-    segment = jnp.sum(
-        jnp.where(places[None, :, None] == token[:, None, :], segment_ids[:, :, None], 0), 1
-    )
-    base = document * length
-    zero = jnp.zeros_like(base)
-    facts = jnp.stack([base + ranking, base, segment, token, zero, zero, zero, zero], 1)
-    facts = facts.astype(jnp.float32)
-    return facts, jnp.swapaxes(facts, 1, 2)
-
-
 def roll_matrix(token_col, length):
     lanes = lax.broadcasted_iota(jnp.int32, (length, length), 1).astype(jnp.float32)
     return jnp.where(token_col == lanes, 1.0, 0.0).astype(jnp.bfloat16)
@@ -106,34 +84,6 @@
     return content + pltpu.roll(position, half, 1, stride=1, stride_axis=0)[:, :half]
 
 
-def start_pieces(pieces, place, sems, base):
-    copies = []
-    for index, piece in enumerate(pieces):
-        copy = pltpu.make_async_copy(piece, place(index), sems.at[base + index])
-        copy.start()
-        copies.append(copy)
-    return copies
-
-
-def start_inputs(content_pieces, query_pieces, weight_pieces, content_ref, query_ref, weight_ref, sems):
-    heads_here, dp_here = lax.axis_index("heads"), lax.axis_index("dp")
-    tokens, rows = content_pieces[0].shape[0], weight_pieces[0].shape[1]
-
-    def token_place(ref):
-        return lambda k: ref.at[pl.ds(pl.multiple_of((heads_here ^ k) * tokens, tokens), tokens)]
-
-    def weight_place(k):
-        if len(weight_pieces) == 1:
-            return weight_ref
-        return weight_ref.at[:, pl.ds(pl.multiple_of((dp_here ^ k) * rows, rows), rows)]
-
-    copies = start_pieces(weight_pieces, weight_place, sems, 0)
-    base = len(weight_pieces)
-    copies += start_pieces(content_pieces, token_place(content_ref), sems, base)
-    base += len(content_pieces)
-    return copies + start_pieces(query_pieces, token_place(query_ref), sems, base)
-
-
 def greet(axis, masks):
     barrier = pltpu.get_barrier_semaphore()
     for mask in masks:
@@ -141,150 +91,6 @@
             barrier, inc=1, device_id={axis: lax.axis_index(axis) ^ mask}, device_id_type=pl.DeviceIdType.MESH
         )
     pl.semaphore_wait(barrier, len(masks))
-
-
-def send_pieces(full_ref, pieces, send_sems, recv_sems, base):
-    tokens = pieces[0].shape[1]
-    here = lax.axis_index("heads")
-    copies = []
-    for k, piece in enumerate(pieces):
-        part = full_ref.at[:, pl.ds(pl.multiple_of((here ^ k) * tokens, tokens), tokens)]
-        if k == 0:
-            copy = pltpu.make_async_copy(part, piece, send_sems.at[base])
-        else:
-            copy = pltpu.make_async_remote_copy(
-                part, piece, send_sems.at[base + k], recv_sems.at[k],
-                device_id={"heads": here ^ k}, device_id_type=pl.DeviceIdType.MESH,
-            )
-        copy.start()
-        copies.append(copy)
-    for copy in copies:
-        copy.wait()
-
-
-def attention_forward_kernel(head_size, group, parts, *refs):
-    content_pieces, query_pieces, refs = refs[:group], refs[group : 2 * group], refs[2 * group :]
-    weight_pieces, refs = refs[:parts], refs[parts:]
-    table_ref, bias_ref, row_ref, col_ref, proj_ref, logsum_ref = refs[:6]
-    mixed_pieces, refs = refs[6 : 6 + group], refs[6 + group :]
-    content_all, query_all, weight_ref, mixed_ref, relative_ref, mask_ref, sems, recv_sems = refs
-    length = row_ref.shape[2]
-    half = length // 2
-    width = weight_ref.shape[-1]
-    heads = width // head_size
-    factor = head_size ** (-0.5) * LOG2E
-    row = pl.program_id(0)
-
-    @pl.when(row == 0)
-    def _():
-        copies = start_inputs(
-            content_pieces, query_pieces, weight_pieces, content_all, query_all, weight_ref, sems
-        )
-        greet("heads", range(1, group))
-        for copy in copies:
-            copy.wait()
-        relative_ref[...] = dot(table_ref[...], weight_ref[3]).astype(jnp.bfloat16)
-
-    here = pl.ds(pl.multiple_of(row * length, length), length)
-    content_ref, query_ref = content_all.at[here], query_all.at[here]
-
-    facts_row, facts_col = row_ref[0], col_ref[0]
-    write_masks(mask_ref, facts_row, facts_col, half)
-    roll = roll_matrix(facts_col[:, 3:4], length)
-    unroll = unroll_matrix(facts_row[3:4, :], length)
-    content, query = content_ref[...], query_ref[...]
-    joined = jnp.concatenate(
-        [
-            dot(content, weight_ref[0]).astype(jnp.bfloat16),
-            dot(content, weight_ref[1]).astype(jnp.bfloat16),
-            dot(content, weight_ref[2]).astype(jnp.bfloat16),
-            dot(query, weight_ref[0]).astype(jnp.bfloat16),
-        ],
-        -1,
-    )
-    proj_ref[0] = dot(roll, joined).astype(jnp.bfloat16)
-    segment_col, segment_row = facts_col[:, 2:3], facts_row[2:3, :]
-    mixed = [[None] * heads, [None] * heads]
-    for head in range(heads):
-        cols = lambda kind: slice(kind * width + head * head_size, kind * width + (head + 1) * head_size)
-        bias = [bias_ref[kind : kind + 1, head * head_size : (head + 1) * head_size] for kind in range(5)]
-        keys, values = proj_ref[0, :, cols(1)], proj_ref[0, :, cols(2)]
-        keys_twice = jnp.concatenate([keys, keys], -1)
-        relative = relative_ref[:, head * head_size : (head + 1) * head_size]
-        relative_twice = jnp.concatenate([relative, relative], -1)
-        for stream in range(2):
-            with_u, with_w, _, own, slope = query_sides(
-                proj_ref[0, :, cols(3 * stream)], bias, segment_col, factor
-            )
-            pieces = []
-            for block in range(2):
-                part = slice(block * half, (block + 1) * half)
-                scores = block_scores(
-                    with_u[part], with_w[part], keys_twice[part], relative_twice, half
-                )
-                scores = scores + own[part] + slope[part] * segment_row[:, part] + mask_ref[stream, block]
-                highest = jnp.maximum(jnp.max(scores, -1, keepdims=True), 0.0)
-                weights = jnp.exp2(scores - highest)
-                totals = jnp.exp2(-highest) + jnp.sum(weights, -1, keepdims=True)
-                pieces.append(dot(weights.astype(jnp.bfloat16), values[part]) / totals)
-                index = stream * heads + head
-                logsum_ref[0, part, index : index + 1] = highest + jnp.log2(totals)
-            mixed[stream][head] = jnp.concatenate(pieces, 0).astype(jnp.bfloat16)
-    both = jnp.concatenate(mixed[0] + mixed[1], -1)
-    both = dot(unroll, both).astype(jnp.bfloat16)
-    mixed_ref[0, here] = both[:, :width]
-    mixed_ref[1, here] = both[:, width:]
-
-    @pl.when(row == pl.num_programs(0) - 1)
-    def _():
-        send_pieces(mixed_ref, mixed_pieces, sems, recv_sems, 2 * group + parts)
-
-
-def attention_forward(content_pieces, query_pieces, weight_pieces, table, head_bias, facts):
-    rows, length = facts[0].shape[0], facts[0].shape[2]
-    group, parts = len(content_pieces), len(weight_pieces)
-    own, depth = content_pieces[0].shape
-    tokens = own * group
-    width = weight_pieces[0].shape[-1]
-    head_size = head_bias.shape[-1]
-    half = length // 2
-    full = lambda *shape: pl.BlockSpec(shape, lambda r: (0,) * len(shape))
-    outside = pl.BlockSpec(memory_space=pl.ANY)
-    results = pl.pallas_call(
-        functools.partial(attention_forward_kernel, head_size, group, parts),
-        grid=(rows,),
-        in_specs=[outside] * (2 * group + parts)
-        + [
-            full(length, depth),
-            full(5, width),
-            pl.BlockSpec((1, 8, length), lambda r: (r, 0, 0)),
-            pl.BlockSpec((1, length, 8), lambda r: (r, 0, 0)),
-        ],
-        out_specs=[
-            pl.BlockSpec((1, length, 4 * width), lambda r: (r, 0, 0)),
-            pl.BlockSpec((1, length, 8), lambda r: (r, 0, 0)),
-        ]
-        + [outside] * group,
-        out_shape=[
-            jax.ShapeDtypeStruct((rows, length, 4 * width), jnp.bfloat16),
-            jax.ShapeDtypeStruct((rows, length, 8), jnp.float32),
-        ]
-        + [jax.ShapeDtypeStruct((2, own, width), jnp.bfloat16)] * group,
-        scratch_shapes=[
-            pltpu.VMEM((tokens, depth), jnp.bfloat16),
-            pltpu.VMEM((tokens, depth), jnp.bfloat16),
-            pltpu.VMEM((4, depth, width), jnp.bfloat16),
-            pltpu.VMEM((2, tokens, width), jnp.bfloat16),
-            pltpu.VMEM((length, width), jnp.bfloat16),
-            pltpu.VMEM((2, 2, half, half), jnp.float32),
-            pltpu.SemaphoreType.DMA((3 * group + parts,)),
-            pltpu.SemaphoreType.DMA((group,)),
-        ],
-        compiler_params=pltpu.CompilerParams(
-            vmem_limit_bytes=VMEM_LIMIT, collective_id=0, has_side_effects=True
-        ),
-    )(*content_pieces, *query_pieces, *weight_pieces, table, head_bias.reshape(5, width), *facts)
-    return results[0], results[1], results[2:]
 
 
 class Links:
@@ -356,9 +162,387 @@
     return jnp.sum(jnp.sum(values * values, -1, keepdims=True), 0, keepdims=True)
 
 
+class Gather:
+    def __init__(self, links, sem, full, own, rows, order):
+        heads_here, dp_here = lax.axis_index("heads"), lax.axis_index("dp")
+        x, core, y, z = heads_here >> 1, heads_here & 1, dp_here & 1, dp_here >> 1
+
+        def same(*place):
+            part = full.at[place + (rows,)]
+            return part, part
+
+        everything = slice(None)
+        planes = full.shape[0]
+        mine = full.at[z, y, x, core, rows]
+        self.keep = pltpu.make_async_copy(own.at[rows], mine, sem)
+        self.along_z = [links.push(own.at[rows], mine, "dp", 2 * m) for m in range(1, planes)]
+        column = same(everything, y, x, core)
+        across = ("heads", 2), ("dp", 1)
+        if order == "xy":
+            near, wide = same(everything, y, 1 - x, core), same(everything, y, everything, core)
+            last = same(everything, 1 - y, everything, core)
+        else:
+            near, wide = same(everything, 1 - y, x, core), same(everything, everything, x, core)
+            last = same(everything, everything, 1 - x, core)
+            across = across[1], across[0]
+        self.first = links.push(*column, *across[0])
+        self.second = links.push(*wide, *across[1])
+        self.to_sibling = [links.push(*part, "heads", 1) for part in (column, near, last)]
+
+    def begin(self):
+        self.keep.start()
+        for copy in self.along_z:
+            copy.start()
+
+    def step_one(self):
+        self.keep.wait()
+        for copy in self.along_z:
+            copy.wait()
+        self.first.start()
+        self.to_sibling[0].start()
+
+    def step_two(self):
+        self.first.wait()
+        self.second.start()
+        self.to_sibling[1].start()
+
+    def step_three(self):
+        self.second.wait()
+        self.to_sibling[2].start()
+
+    def finish(self):
+        for copy in self.to_sibling:
+            copy.wait()
+
+
+def write_facts(lengths_ref, order_ref, segment_ref, row_ref, col_ref):
+    rows, length = order_ref.shape
+    down = lax.broadcasted_iota(jnp.int32, (length, length), 0).astype(jnp.float32)
+    along = lax.broadcasted_iota(jnp.int32, (length, length), 1).astype(jnp.float32)
+    places_col, places_row = down[:, 0:1], along[0:1, :]
+    row_ref[...] = jnp.zeros_like(row_ref)
+    col_ref[...] = jnp.zeros_like(col_ref)
+
+    def as_column(values):
+        return jnp.sum(jnp.where(down == along, values, 0.0), 1, keepdims=True)
+
+    for row in range(rows):
+        ends, start, end = [], 0, 0
+        for document in range(lengths_ref.shape[1]):
+            count = lengths_ref[row, document]
+            start = start + (count == length // 2).astype(jnp.int32) * end
+            end = end + count
+            ends.append(end.astype(jnp.float32))
+        start = start.astype(jnp.float32)
+        order = order_ref[row : row + 1].astype(jnp.float32)
+        segment = segment_ref[row : row + 1].astype(jnp.float32)
+        order_col, segment_col = as_column(order), as_column(segment)
+        for place, turned in ((places_row, False), (places_col, True)):
+            token = place + start
+            token = jnp.where(token >= length, token - length, token)
+            base = jnp.zeros_like(token)
+            for end in ends:
+                base = base + jnp.where(token >= end, float(length), 0.0)
+            if turned:
+                rank = jnp.sum(jnp.where(order == token, along, 0.0), 1, keepdims=True)
+                kind = jnp.sum(jnp.where(along == token, segment, 0.0), 1, keepdims=True)
+                for index, values in enumerate((base + rank, base, kind, token)):
+                    col_ref[row, :, index : index + 1] = values
+            else:
+                rank = jnp.sum(jnp.where(order_col == token, down, 0.0), 0, keepdims=True)
+                kind = jnp.sum(jnp.where(down == token, segment_col, 0.0), 0, keepdims=True)
+                for index, values in enumerate((base + rank, base, kind, token)):
+                    row_ref[row, index : index + 1] = values
+
+
+def turn(values):
+    size = values.shape[1]
+    same = lax.broadcasted_iota(jnp.int32, (size, size), 0) == lax.broadcasted_iota(jnp.int32, (size, size), 1)
+    identity = jnp.where(same, 1.0, 0.0).astype(jnp.bfloat16)
+    return dot_nt(identity, values.astype(jnp.bfloat16)).astype(jnp.bfloat16)
+
+
+def attention_forward_kernel(head_size, group, parts, fast, *refs):
+    content_hbm, query_hbm, weight_in, up_in, down_in, out_in, bias_in, refs = *refs[:7], refs[7:]
+    lengths_ref, order_ref, segment_ref, table_ref, head_ref, refs = *refs[:5], refs[5:]
+    proj_ref, logsum_ref, row_ref, col_ref, bias_all, refs = *refs[:5], refs[5:]
+    mixed_pieces, refs = refs[:group], refs[group:]
+    content_out, query_out, weight_out, refs = *refs[:3], refs[3:]
+    if fast:
+        up_all, down_all, out_all, refs = *refs[:3], refs[3:]
+    content_all, query_all, weight_ref, mixed_ref, relative_ref, mask_ref, refs = *refs[:6], refs[6:]
+    sems, send_sems, recv_sems, refs = *refs[:3], refs[3:]
+    rows, length = row_ref.shape[0], row_ref.shape[2]
+    half = length // 2
+    tokens, depth = content_hbm.shape
+    width = weight_ref.shape[-1]
+    heads = width // head_size
+    factor = head_size ** (-0.5) * LOG2E
+    heads_here, dp_here = lax.axis_index("heads"), lax.axis_index("dp")
+    chip = heads_here >> 1
+    links = Links(send_sems, recv_sems)
+
+    def token_part(k):
+        return pl.ds(pl.multiple_of((heads_here ^ k) * tokens, tokens), tokens)
+
+    streams = ((content_hbm, content_all), (query_hbm, query_all))
+    local = [pltpu.make_async_copy(own, full.at[token_part(0)], sems.at[n]) for n, (own, full) in enumerate(streams)]
+    if not fast:
+        local.append(pltpu.make_async_copy(weight_in, weight_ref, sems.at[2]))
+    for copy in local:
+        copy.start()
+    barrier = pltpu.get_barrier_semaphore()
+    peers = [("heads", k) for k in range(1, group)] + [("dp", k) for k in range(1, parts)]
+    for axis, k in peers:
+        pl.semaphore_signal(
+            barrier, inc=1, device_id={axis: lax.axis_index(axis) ^ k}, device_id_type=pl.DeviceIdType.MESH
+        )
+    if fast:
+        weight_send, up_send, down_send, out_send = refs
+        weight_send[...] = weight_in[...].astype(jnp.bfloat16)
+    pl.semaphore_wait(barrier, len(peers))
+    far = [links.push(own, full.at[token_part(0)], "heads", 2) for own, full in streams]
+    near = [links.push(own, full.at[token_part(0)], "heads", 1) for own, full in streams]
+    passed = [links.push(full.at[token_part(2)], full.at[token_part(2)], "heads", 1) for _, full in streams]
+    bias_copies = [links.push(bias_in, bias_all.at[heads_here], "heads", k) for k in range(1, group)]
+    for copy in far + near + bias_copies:
+        copy.start()
+    if fast:
+        y, z = dp_here & 1, dp_here >> 1
+        weight_z, weight_y = [], []
+        for pair in (slice(0, 2), slice(2, 4)):
+            mine = weight_ref.at[pair, z, y]
+            weight_z.append([links.push(weight_send.at[pair], mine, "dp", 2 * m) for m in range(1, parts // 2)])
+            column = weight_ref.at[pair, :, y]
+            weight_y.append(links.push(column, column, "dp", 1))
+            for copy in weight_z[-1]:
+                copy.start()
+        weight_ref[:, z, y] = weight_send[...]
+        up_send[...] = up_in[...].astype(jnp.bfloat16)
+        down_send[...] = turn(down_in[...])
+        out_send[...] = turn(out_in[...])
+        pick = up_send.shape[0]
+        early, late = pl.ds(0, pick // 2), pl.ds(pick // 2, pick // 2)
+        up_one = Gather(links, sems.at[3], up_all, up_send, early, "xy")
+        up_two = Gather(links, sems.at[4], up_all, up_send, late, "xy")
+        down_one = Gather(links, sems.at[5], down_all, down_send, early, "yx")
+        down_two = Gather(links, sems.at[6], down_all, down_send, late, "xy")
+        out_one = Gather(links, sems.at[7], out_all, out_send, pl.ds(0, pick), "yx")
+        gathers = (up_one, up_two, down_one, down_two, out_one)
+    bias_all[heads_here] = bias_in[...]
+    write_facts(lengths_ref, order_ref, segment_ref, row_ref, col_ref)
+    if fast:
+        for first, second in zip(weight_z, weight_y):
+            for copy in first:
+                copy.wait()
+            second.start()
+        down_one.begin()
+        out_one.begin()
+        for copy in weight_y[:1]:
+            copy.wait()
+        up_one.begin()
+        weight_y[1].wait()
+    for copy in local + near:
+        copy.wait()
+
+    def weight(kind):
+        return weight_ref[kind].reshape(depth, width)
+
+    saves = [
+        pltpu.make_async_copy(content_all, content_out, sems.at[0]),
+        pltpu.make_async_copy(query_all, query_out, sems.at[1]),
+        pltpu.make_async_copy(weight_ref, weight_out, sems.at[2]),
+    ]
+    saves[2].start()
+    relative_ref[...] = dot(table_ref[...], weight(3)).astype(jnp.bfloat16)
+
+    def pass_on():
+        for arrived, onward in zip(far, passed):
+            arrived.wait()
+            onward.start()
+
+    def nothing():
+        pass
+
+    events = {(0, 0): [pass_on]}
+    if fast:
+        events = {
+            (0, 0): [pass_on, down_one.step_one, up_two.begin],
+            (0, 1): [up_one.step_one, down_two.begin],
+            (0, 2): [out_one.step_one, down_one.step_two],
+            (1, 0): [up_one.step_two, up_two.step_one],
+            (1, 1): [down_two.step_one, out_one.step_two],
+            (1, 2): [up_two.step_two, down_one.step_three],
+            (2, 0): [down_two.step_two, up_one.step_three],
+            (2, 1): [out_one.step_three],
+        }
+
+    def one_row(step, carry):
+        row = jnp.where(step == 0, 0, rows - step)
+        row = jnp.where(chip == 0, row, rows - 1 - row)
+
+        @pl.when(step == 1)
+        def _():
+            for copy in passed:
+                copy.wait()
+            for save in saves[:2]:
+                save.start()
+
+        here = pl.ds(pl.multiple_of(row * length, length), length)
+        facts_row, facts_col = row_ref[row], col_ref[row]
+        write_masks(mask_ref, facts_row, facts_col, half)
+        roll = roll_matrix(facts_col[:, 3:4], length)
+        unroll = unroll_matrix(facts_row[3:4, :], length)
+        content, query = content_all[here], query_all[here]
+        joined = jnp.concatenate(
+            [
+                dot(content, weight(0)).astype(jnp.bfloat16),
+                dot(content, weight(1)).astype(jnp.bfloat16),
+                dot(content, weight(2)).astype(jnp.bfloat16),
+                dot(query, weight(0)).astype(jnp.bfloat16),
+            ],
+            -1,
+        )
+        proj_ref[row] = dot(roll, joined).astype(jnp.bfloat16)
+        segment_col, segment_row = facts_col[:, 2:3], facts_row[2:3, :]
+        mixed = [[None] * heads, [None] * heads]
+        for head in range(heads):
+            cols = lambda kind: slice(kind * width + head * head_size, kind * width + (head + 1) * head_size)
+            own_cols = slice(head * head_size, (head + 1) * head_size)
+            bias = [head_ref[kind : kind + 1, own_cols] for kind in range(5)]
+            keys, values = proj_ref[row, :, cols(1)], proj_ref[row, :, cols(2)]
+            keys_twice = jnp.concatenate([keys, keys], -1)
+            relative = relative_ref[:, own_cols]
+            relative_twice = jnp.concatenate([relative, relative], -1)
+            for stream in range(2):
+                with_u, with_w, _, own, slope = query_sides(
+                    proj_ref[row, :, cols(3 * stream)], bias, segment_col, factor
+                )
+                pieces = []
+                for block in range(2):
+                    part = slice(block * half, (block + 1) * half)
+                    scores = block_scores(
+                        with_u[part], with_w[part], keys_twice[part], relative_twice, half
+                    )
+                    scores = scores + own[part] + slope[part] * segment_row[:, part] + mask_ref[stream, block]
+                    highest = jnp.maximum(jnp.max(scores, -1, keepdims=True), 0.0)
+                    weights = jnp.exp2(scores - highest)
+                    totals = jnp.exp2(-highest) + jnp.sum(weights, -1, keepdims=True)
+                    pieces.append(dot(weights.astype(jnp.bfloat16), values[part]) / totals)
+                    index = stream * heads + head
+                    logsum_ref[row, part, index : index + 1] = highest + jnp.log2(totals)
+                mixed[stream][head] = jnp.concatenate(pieces, 0).astype(jnp.bfloat16)
+            for when, actions in events.items():
+                if when[1] == head:
+                    @pl.when(step == when[0])
+                    def _():
+                        for action in actions:
+                            action()
+        both = jnp.concatenate(mixed[0] + mixed[1], -1)
+        both = dot(unroll, both).astype(jnp.bfloat16)
+        mixed_ref[0, here] = both[:, :width]
+        mixed_ref[1, here] = both[:, width:]
+        return carry
+
+    lax.fori_loop(0, rows, one_row, 0)
+    keep = pltpu.make_async_copy(mixed_ref.at[:, token_part(0)], mixed_pieces[0], sems.at[8])
+    keep.start()
+    sends = [
+        links.push(mixed_ref.at[:, token_part(k)], mixed_pieces[k], "heads", k) for k in (2, 3, 1)[: group - 1]
+    ]
+    for copy in sends:
+        copy.start()
+    if fast:
+        up_two.step_three()
+        down_two.step_three()
+    for copy in [keep] + saves + sends + bias_copies:
+        copy.wait()
+    if fast:
+        for gather in gathers:
+            gather.finish()
+
+
+def attention_forward(
+    content, query, attn_proj, up_proj, down_proj, out_proj, up_bias, doc_lengths, factor_order, segment_ids,
+    table, head_bias,
+):
+    rows, length = segment_ids.shape
+    group, parts = lax.axis_size("heads"), lax.axis_size("dp")
+    fast = by_pieces(attn_proj.shape[1])
+    own, depth = content.shape
+    tokens = own * group
+    pick, width = attn_proj.shape[1:]
+    hidden = up_proj.shape[1]
+    head_size = head_bias.shape[-1]
+    half = length // 2
+    inside = pl.BlockSpec(memory_space=pltpu.VMEM)
+    outside = pl.BlockSpec(memory_space=pl.ANY)
+    scalars = pl.BlockSpec(memory_space=pltpu.SMEM)
+    bfloat, float32 = jnp.bfloat16, jnp.float32
+    weight_shape = (4, parts // 2, 2, pick, width) if fast else (4, depth, width)
+    out_shape = [
+        jax.ShapeDtypeStruct((rows, length, 4 * width), bfloat),
+        jax.ShapeDtypeStruct((rows, length, 8), float32),
+        jax.ShapeDtypeStruct((rows, 8, length), float32),
+        jax.ShapeDtypeStruct((rows, length, 8), float32),
+        jax.ShapeDtypeStruct((group, 1, hidden), float32),
+    ]
+    out_specs = [inside] * 5 + [outside] * (group + 3)
+    out_shape += [jax.ShapeDtypeStruct((2, own, width), bfloat)] * group
+    out_shape += [jax.ShapeDtypeStruct((tokens, depth), bfloat)] * 2
+    out_shape += [jax.ShapeDtypeStruct(weight_shape, bfloat)]
+    scratch = [
+        pltpu.VMEM((tokens, depth), bfloat),
+        pltpu.VMEM((tokens, depth), bfloat),
+        pltpu.VMEM(weight_shape, bfloat),
+        pltpu.VMEM((2, tokens, width), bfloat),
+        pltpu.VMEM((length, width), bfloat),
+        pltpu.VMEM((2, 2, half, half), float32),
+        pltpu.SemaphoreType.DMA((9,)),
+        pltpu.SemaphoreType.DMA((72,)),
+        pltpu.SemaphoreType.DMA((72,)),
+    ]
+    if fast:
+        weight_spec = inside
+        out_specs += [outside] * 3
+        out_shape += [
+            jax.ShapeDtypeStruct((parts // 2, 2, group // 2, 2, pick, c), bfloat) for c in (hidden, hidden, width)
+        ]
+        scratch += [
+            pltpu.VMEM((4, pick, width), bfloat),
+            pltpu.VMEM((pick, hidden), bfloat),
+            pltpu.VMEM((pick, hidden), bfloat),
+            pltpu.VMEM((pick, width), bfloat),
+        ]
+    else:
+        weight_spec = outside
+        attn_proj = lax.all_gather(attn_proj.astype(bfloat), "dp", axis=1, tiled=True)
+    results = pl.pallas_call(
+        functools.partial(attention_forward_kernel, head_size, group, parts if fast else 1, fast),
+        in_specs=[outside, outside, weight_spec] + [inside] * 4 + [scalars] + [inside] * 4,
+        out_specs=out_specs,
+        out_shape=out_shape,
+        scratch_shapes=scratch,
+        compiler_params=pltpu.CompilerParams(
+            vmem_limit_bytes=VMEM_LIMIT, collective_id=0, has_side_effects=True
+        ),
+    )(
+        content, query, attn_proj, up_proj, down_proj, out_proj, up_bias[None], doc_lengths, factor_order,
+        segment_ids, table, head_bias.reshape(5, width),
+    )
+    proj, logsum, facts_row, facts_col, bias_all = results[:5]
+    mixed_pieces, results = results[5 : 5 + group], results[5 + group :]
+    content_all, query_all, weight_all = results[:3]
+    if fast:
+        wide = [full.reshape(parts, group, pick, full.shape[-1]) for full in results[3:]]
+    else:
+        wide = [gather_all(m) for m in (up_proj.astype(bfloat), down_proj.T.astype(bfloat), out_proj.T.astype(bfloat))]
+    kept = (content_all, query_all, weight_all, (facts_row, facts_col), proj, logsum)
+    return kept, bias_all, mixed_pieces, wide
+
+
 def attention_backward_kernel(head_size, group, parts, fast, *refs):
-    content_pieces, query_pieces, refs = refs[:group], refs[group : 2 * group], refs[2 * group :]
-    weight_pieces, refs = refs[:parts], refs[parts:]
+    content_hbm, query_hbm, weight_hbm, refs = *refs[:3], refs[3:]
     upper_pieces, dresid_hbm, refs = refs[:group], refs[group], refs[group + 1 :]
     table_ref, turned_ref, bias_ref, row_ref, col_ref, proj_ref, logsum_ref = refs[:7]
     sources, small_ref, refs = refs[7:10], refs[10], refs[11:]
@@ -370,7 +554,7 @@
     sems, send_sems, recv_sems, refs = *refs[:3], refs[3:]
     rows, length = row_ref.shape[0], row_ref.shape[2]
     half = length // 2
-    depth, width = weight_ref.shape[1:]
+    depth, width = content_all.shape[1], weight_ref.shape[-1]
     heads = width // head_size
     scale = head_size ** (-0.5)
     factor = scale * LOG2E
@@ -382,12 +566,20 @@
     def token_part(k):
         return pl.ds(pl.multiple_of((heads_here ^ k) * tokens, tokens), tokens)
 
-    copies = start_inputs(
-        content_pieces, query_pieces, weight_pieces, content_all, query_all, weight_ref, sems
-    )
-    copies += start_pieces([upper_pieces[0]], lambda k: upper_all.at[:, token_part(0)], sems, 2 * group + parts)
-    dresid_copy = pltpu.make_async_copy(dresid_hbm, dresid_ref, sems.at[2 * group + parts + 1])
+    copies = [
+        pltpu.make_async_copy(content_hbm, content_all, sems.at[0]),
+        pltpu.make_async_copy(query_hbm, query_all, sems.at[1]),
+        pltpu.make_async_copy(weight_hbm, weight_ref, sems.at[2]),
+        pltpu.make_async_copy(upper_pieces[0], upper_all.at[:, token_part(0)], sems.at[3]),
+    ]
+    for copy in copies:
+        copy.start()
+    dresid_copy = pltpu.make_async_copy(dresid_hbm, dresid_ref, sems.at[4])
     dresid_copy.start()
+
+    def weight(kind):
+        return weight_ref[kind].reshape(depth, width)
+
     barrier = pltpu.get_barrier_semaphore()
     peers = [("heads", k) for k in range(1, group)] + [("dp", k) for k in range(1, parts)]
     for axis, k in peers:
@@ -402,7 +594,7 @@
         copy.start()
     if fast:
         scatters = [
-            Scatter(links, sems, 2 * group + parts + 2 + n, sources[n], order, refs[4 * n : 4 * n + 4])
+            Scatter(links, sems, 5 + n, sources[n], order, refs[4 * n : 4 * n + 4])
             for n, order in enumerate(("xy", "yx", "yx"))
         ]
         small_got, small_more, small_mid, dweight_got, dweight_more, head_got, tile_ref, tile_got, tile_more = refs[12:]
@@ -416,8 +608,8 @@
     for copy in copies:
         copy.wait()
     upper_copies[0].wait()
-    relative_ref[...] = dot(table_ref[...], weight_ref[3]).astype(jnp.bfloat16)
-    backward_ref[...] = dot(turned_ref[...], weight_ref[3]).astype(jnp.bfloat16)
+    relative_ref[...] = dot(table_ref[...], weight(3)).astype(jnp.bfloat16)
+    backward_ref[...] = dot(turned_ref[...], weight(3)).astype(jnp.bfloat16)
     drel_ref[...] = jnp.zeros_like(drel_ref)
     dweight_ref[...] = jnp.zeros_like(dweight_ref)
     dhead_own[...] = jnp.zeros_like(dhead_own)
@@ -541,11 +733,11 @@
         dweight_ref[1] += dot(joined_t[2 * width : 3 * width], content)
         dweight_ref[2] += dot(joined_t[3 * width :], content)
         dinput_ref[0, here] = (
-            dot_nt(joined[:, :width], weight_ref[0])
-            + dot_nt(joined[:, 2 * width : 3 * width], weight_ref[1])
-            + dot_nt(joined[:, 3 * width :], weight_ref[2])
+            dot_nt(joined[:, :width], weight(0))
+            + dot_nt(joined[:, 2 * width : 3 * width], weight(1))
+            + dot_nt(joined[:, 3 * width :], weight(2))
         ).astype(jnp.bfloat16)
-        dinput_ref[1, here] = dot_nt(joined[:, width : 2 * width], weight_ref[0]).astype(jnp.bfloat16)
+        dinput_ref[1, here] = dot_nt(joined[:, width : 2 * width], weight(0)).astype(jnp.bfloat16)
         if fast:
             after(step, 1, scatters[0].second)
 
@@ -655,15 +847,16 @@
 
 
 def attention_backward(
-    content_pieces, query_pieces, weight_pieces, tables, head_bias, facts, proj, logsum, upper_pieces,
-    dresid, gradients, small,
+    kept, tables, head_bias, upper_pieces, dresid, gradients, small
 ):
+    content_all, query_all, weight_all, facts, proj, logsum = kept
     rows, length = facts[0].shape[0], facts[0].shape[2]
-    group, parts = len(content_pieces), len(weight_pieces)
-    fast = parts > 1
-    own, depth = content_pieces[0].shape
-    tokens = own * group
-    pick, width = weight_pieces[0].shape[1:]
+    group = len(upper_pieces)
+    fast = weight_all.ndim == 5
+    tokens, depth = content_all.shape
+    own = tokens // group
+    pick, width = weight_all.shape[-2:]
+    parts = depth // pick
     head_size = head_bias.shape[-1]
     half = length // 2
     inside = pl.BlockSpec(memory_space=pltpu.VMEM)
@@ -674,12 +867,11 @@
         jax.ShapeDtypeStruct((own, depth), float32),
         jax.ShapeDtypeStruct((8, width), float32),
     ]
-    lanes = max(2 * parts, 2)
     wide_shape = (4, parts // 2, 2, pick, width) if fast else (4, pick, width)
     scratch = [
         pltpu.VMEM((tokens, depth), bfloat),
         pltpu.VMEM((tokens, depth), bfloat),
-        pltpu.VMEM((4, depth, width), bfloat),
+        pltpu.VMEM(weight_all.shape, bfloat),
         pltpu.VMEM((2, tokens, width), bfloat),
         pltpu.VMEM((2, tokens, depth), bfloat),
         pltpu.VMEM((4, width, depth), float32),
@@ -696,7 +888,7 @@
         pltpu.VMEM((2, own, depth), bfloat),
         pltpu.VMEM((2, own, depth), float32),
         pltpu.VMEM((8, width), float32),
-        pltpu.SemaphoreType.DMA((2 * group + parts + 5,)),
+        pltpu.SemaphoreType.DMA((8,)),
         pltpu.SemaphoreType.DMA((64,)),
         pltpu.SemaphoreType.DMA((64,)),
     ]
@@ -732,7 +924,7 @@
         out_shape += [jax.ShapeDtypeStruct(wide_shape, bfloat)]
     return pl.pallas_call(
         functools.partial(attention_backward_kernel, head_size, group, parts, fast),
-        in_specs=[outside] * (3 * group + parts + 1) + [inside] * 7 + [outside] * 3 + [inside],
+        in_specs=[outside] * (group + 4) + [inside] * 7 + [outside] * 3 + [inside],
         out_specs=[inside] * len(out_shape),
         out_shape=out_shape,
         scratch_shapes=scratch,
@@ -740,7 +932,7 @@
             vmem_limit_bytes=VMEM_LIMIT, collective_id=2, has_side_effects=True
         ),
     )(
-        *content_pieces, *query_pieces, *weight_pieces, *upper_pieces, dresid, *tables,
+        content_all, query_all, weight_all, *upper_pieces, dresid, *tables,
         head_bias.reshape(5, width), *facts, proj, logsum, *gradients, small,
     )
 
@@ -764,14 +956,14 @@
 
 def feed_kernel(group, *refs):
     mixed_pieces, refs = refs[:group], refs[group:]
-    bias_pieces, refs = refs[:group], refs[group:]
+    bias_ref, refs = refs[0], refs[1:]
     content_ref, query_ref, dcontent_ref, dquery_ref, norm_ref, up_hbm, down_hbm, out_hbm = refs[:8]
     content_out, query_out, dresid_ref, refs = refs[8], refs[9], refs[10], refs[11:]
     dmixed_pieces, refs = refs[:group], refs[group:]
     dup_hbm, ddown_hbm, dout_ref, dsmall_ref, refs = refs[0], refs[1], refs[2], refs[3], refs[4:]
-    up_ref, down_ref, out_ref, hidden_ref, slope_ref, bias_ref = refs[:6]
-    low_ref, low_t_ref, normed_ref, total_ref, up_got, down_got, out_got, out_sent = refs[6:14]
-    sems, send_sems, recv_sems = refs[14:]
+    up_ref, down_ref, out_ref, hidden_ref, slope_ref = refs[:5]
+    low_ref, low_t_ref, normed_ref, total_ref, up_got, down_got, out_got, out_sent = refs[5:13]
+    sems, send_sems, recv_sems = refs[13:]
     own, depth = content_ref.shape
     tokens = 2 * own
     here = lax.axis_index("heads")
@@ -790,8 +982,6 @@
     for load in loads:
         load.start()
     greet("heads", [1])
-    for k in range(group):
-        bias_ref[here ^ k] = bias_pieces[k][...]
     gain_one, bias_one, bias_out, gain_two, bias_two = [norm_ref[i : i + 1] for i in range(5)]
     for load in loads[:group]:
         load.wait()
@@ -935,7 +1125,7 @@
             copy.wait()
 
 
-def feed_layer(mixed_pieces, bias_pieces, content, query, dcontent, dquery, norm_param, up, down, out):
+def feed_layer(mixed_pieces, bias_all, content, query, dcontent, dquery, norm_param, up, down, out):
     group = len(mixed_pieces)
     own, depth = content.shape
     parts, _, pick, hidden = up.shape
@@ -945,7 +1135,7 @@
     tokens = 2 * own
     results = pl.pallas_call(
         functools.partial(feed_kernel, group),
-        in_specs=[inside] * (2 * group + 5) + [outside] * 3,
+        in_specs=[inside] * (group + 6) + [outside] * 3,
         out_specs=[inside, inside, outside] + [inside] * group + [outside, outside, inside, inside],
         out_shape=[
             jax.ShapeDtypeStruct((own, depth), jnp.bfloat16),
@@ -965,7 +1155,6 @@
             pltpu.VMEM((group, parts, pick, width), jnp.bfloat16),
             pltpu.VMEM((group, tokens, hidden), jnp.bfloat16),
             pltpu.VMEM((group, tokens, hidden), jnp.float32),
-            pltpu.VMEM((group, 1, hidden), jnp.float32),
             pltpu.VMEM((tokens, depth), jnp.bfloat16),
             pltpu.VMEM((depth, tokens), jnp.bfloat16),
             pltpu.VMEM((tokens, depth), jnp.float32),
@@ -981,7 +1170,7 @@
         compiler_params=pltpu.CompilerParams(
             vmem_limit_bytes=VMEM_LIMIT, collective_id=1, has_side_effects=True
         ),
-    )(*mixed_pieces, *bias_pieces, content, query, dcontent, dquery, norm_param, up, down, out)
+    )(*mixed_pieces, bias_all, content, query, dcontent, dquery, norm_param, up, down, out)
     return results[0], results[1], results[2].reshape(2, own, depth), results[3 : 3 + group], results[3 + group :]
 
 
@@ -997,25 +1186,8 @@
     return value
 
 
-def gather_heads(own):
-    far = exchange(own, "heads", 2)
-    return [own, exchange(own, "heads", 1), far, exchange(far, "heads", 1)]
-
-
 def by_pieces(pick):
     return lax.axis_size("dp") <= 8 and pick % 16 == 0
-
-
-def gather_projection(own):
-    if not by_pieces(own.shape[1]):
-        return [lax.all_gather(own, "dp", axis=1, tiled=True)]
-    pieces = {0: own}
-    mask = lax.axis_size("dp") // 2
-    while mask:
-        for k in sorted(pieces):
-            pieces[k ^ mask] = exchange(pieces[k], "dp", mask)
-        mask = mask // 2
-    return [pieces[k] for k in range(len(pieces))]
 
 
 def reduce_projection(pieces):
@@ -1084,30 +1256,21 @@
 ):
     width = content_in.shape[1]
     length = segment_ids.shape[1]
-    local_heads, head_size = (head_bias.shape[1], head_bias.shape[2])
-    weight_pieces = gather_projection(attn_proj.astype(jnp.bfloat16))
-    content_pieces = gather_heads(content_in)
-    query_pieces = gather_heads(query_in)
-    bias_pieces = [up_bias[None]] + [exchange(up_bias[None], "heads", k) for k in range(1, 4)]
-    out_full = gather_all(out_proj.T.astype(jnp.bfloat16))
-    up_full = gather_all(up_proj.astype(jnp.bfloat16))
-    down_full = gather_all(down_proj.T.astype(jnp.bfloat16))
     table = position_table(length, width)
     tables = (jnp.asarray(table), jnp.asarray(table[::-1].copy()))
-    facts = row_facts(segment_ids, doc_lengths, factor_order)
-    proj, logsum, mixed_pieces = attention_forward(
-        content_pieces, query_pieces, weight_pieces, tables[0], head_bias, facts
+    kept, bias_all, mixed_pieces, (up_full, down_full, out_full) = attention_forward(
+        content_in, query_in, attn_proj, up_proj, down_proj, out_proj, up_bias, doc_lengths, factor_order,
+        segment_ids, tables[0], head_bias,
     )
     content_out, query_out, dresid, dmixed_pieces, (dup, ddown, dout, dsmall) = feed_layer(
-        mixed_pieces, bias_pieces, content_in, query_in, content_grad, query_grad, norm_param,
+        mixed_pieces, bias_all, content_in, query_in, content_grad, query_grad, norm_param,
         up_full, down_full, out_full,
     )
     backward = attention_backward(
-        content_pieces, query_pieces, weight_pieces, tables, head_bias, facts, proj, logsum,
-        dmixed_pieces, dresid, (dup, ddown, dout), dsmall,
+        kept, tables, head_bias, dmixed_pieces, dresid, (dup, ddown, dout), dsmall
     )
     heads_count, head_index = lax.axis_size("heads"), lax.axis_index("heads")
-    if len(weight_pieces) > 1:
+    if by_pieces(attn_proj.shape[1]):
         input_grad, dhead = backward[:2], backward[2]
         up_share, down_share, out_share, proj_share, small_sum, norm_tile = backward[3:]
         grad_norm = norm_tile[0, 0]

time: 427 us -> 333 us (0.78); the launches traced: 424 us -> 335 us
  waiting for transfers between devices: 71.7 us -> 0 us
  Pallas kernels: 276 us -> 307 us
  starting transfers between devices: 17.4 us -> 0 us
  between operations: 15.2 us -> 1.92 us
  other arithmetic: 19.8 us -> 8.32 us
  local copies, waits for them, and re-layouts: 24 us -> 17.8 us
    all_gather x3 -> x0, waiting for transfers between devices: 51.4 us -> none  [gather_all(): lax.all_gather(own, ('dp', 'heads'), axis=0, tiled=False)]
    pallas_call x1, Pallas kernels: 90.6 us -> 120 us  [attention_forward(): pl.pallas_call(functools.partial(attention_forward_kernel, head_size, gro...]
    ppermute x16 -> x0, waiting for transfers between devices: 20.3 us -> none  [exchange(): lax.ppermute(value, axis, [(i, i ^ mask) for i in range(lax.axis_size(axi...]
    ppermute x16 -> x0, starting transfers between devices: 17.2 us -> none  [exchange(): lax.ppermute(value, axis, [(i, i ^ mask) for i in range(lax.axis_size(axi...]
    convert_element_type x5 -> x0, other arithmetic: 6.36 us -> none  [the longest x1 1.64 us: local(): down_full = gather_all(down_proj.T.astype(jnp.bfloat16))]
    unnamed x100 -> x71, local copies, waits for them, and re-layouts: 15.1 us -> 12.3 us
  transfers between devices with their start and end apart: 19 -> 0, of which waited for: 6 -> 0; matrix products, arithmetic and copies ran while one was open for 5% -> 0% of each run, Pallas kernels for 21% -> 0%
where the time goes in v4:
time: 333 us; the launch traced here: 335 us
  Pallas kernels  307 us (92%)
  local copies, waits for them, and re-layouts  17.8 us (5%)
  other arithmetic  8.32 us (2%)
    pallas_call x1, Pallas kernels, attention_backward(): pl.pallas_call(functools.partial(attention_backward_kernel, head_size, gr...  142 us
    pallas_call x1, Pallas kernels, attention_forward(): pl.pallas_call(functools.partial(attention_forward_kernel, head_size, gro...  120 us
    pallas_call x1, Pallas kernels, feed_layer(): pl.pallas_call(functools.partial(feed_kernel, group), in_specs=[inside] *...  45.2 us
    unnamed x71, local copies, waits for them, and re-layouts  12.3 us

profile of v4, /device:TPU:0, one launch (start us, length us, event | category | flops | bytes accessed | tf_op | source)
XLA Modules:
  0.0 335.1 jit_solution(7986969895934089322)
XLA Ops:
  0.7 1.4 reshape.94.refs_11_.refs_10_
  2.1 1.9 copy.63.refs_4_
  3.9 1.3 broadcast_in_dim.3.refs_6_
  5.2 120.0 %shard_map.541 = (bf16[3,512,768]{2,1,0:T(8,128)(2,1)}, f32[3,512,8]{2,1,0:T(8,128)}, f32[3,8,512]{2,1,0:T(8,128)}, f32[3,512,8]{2,1,0:T(8,128)}, f32[4,1,768]{2...) custom-call(bf16[384,768]{1,0:T(8,128)(2,1)} %refs_5_.3, ...), custom_call_target="tpu_custom_call" | custom-call | tf_op jit(solution)/shard_map/pallas_call | solution.py:520
  125.3 45.2 %shard_map.542 = (bf16[384,768]{1,0:T(8,128)(2,1)}, bf16[384,768]{1,0:T(8,128)(2,1)}, f32[768,768]{1,0:T(8,128)}, bf16[2,384,192]{2,1,0:T(8,128)(2,1)}, bf16[2,3...) custom-call(bf16[2,384,192]{2,1,0:T(8,128)(2,1)} %get-tuple-element., ...), custom_call_target="tpu_custom_call" | custom-call | tf_op jit(solution)/shard_map/pallas_call | solution.py:1136
  170.4 0.0 copy-start.15
  170.4 0.0 copy-start.20
  170.4 0.0 copy-start.21
  170.5 0.0 copy-start.22
  170.5 0.0 copy-start.26
  170.5 0.0 copy-start.27
  170.5 0.0 copy-start.18
  170.5 0.0 copy-start.24
  170.5 0.0 copy-start.25
  170.5 0.0 copy-start.5
  170.5 0.0 copy-start.11
  170.6 0.0 copy-start.12
  170.6 141.8 %shard_map.543 = (f32[384,768]{1,0:T(8,128)}, f32[384,768]{1,0:T(8,128)}, f32[8,192]{1,0:T(8,128)}, f32[96,768]{1,0:T(8,128)}, f32[96,768]{1,0:T(8,128)}, /*inde...) custom-call(bf16[1536,768]{1,0:T(8,128)(2,1)} %get-tuple-element.78.refs_0_, ...), custom_call_target="tpu_custom_call" | custom-call | tf_op jit(solution)/shard_map/pallas_call | solution.py:925
  312.4 0.0 copy-start.2
  312.4 0.0 copy-start.13
  312.5 0.0 copy-start.16
  312.5 1.3 slice.12
  314.5 0.0 copy-start.17
  314.5 1.5 multiply_subtract_fusion.4
  316.0 0.8 slice.14
  316.8 0.0 copy-start.23
  316.8 0.6 multiply_subtract_fusion.6
  317.4 0.8 reshape.102
  318.2 0.0 copy-start.19
  318.2 0.6 multiply_subtract_fusion.5
  318.9 2.0 multiply_subtract_fusion.1
  321.0 1.1 multiply_subtract_fusion.2
  322.0 0.1 copy.64
  322.1 0.1 copy.65
  322.2 0.1 copy.67
  322.4 0.1 multiply_subtract_fusion.3
  322.5 0.7 copy.69
  323.2 0.7 copy.70
  323.9 0.7 copy.71
  324.7 2.4 multiply_subtract_fusion
  327.1 0.7 copy.68
  327.8 2.0 copy.79
  329.9 0.8 copy.80
  330.7 1.0 copy.81
  331.7 1.0 copy.82
  332.7 0.7 copy.83
  333.5 0.7 copy.84
  334.2 0.7 copy.85
  (39 shorter events, 0.1 us)
Async XLA Ops:
  170.4 144.0 %copy-start.15 = (f32[5,768]{1,0:T(8,128)S(1)}, f32[5,768]{1,0:T(8,128)}, u32[]{:S(2)}) copy-start(f32[5,768]{1,0:T(8,128)} %refs_9_.4) | copy-start | bytes 46084
  170.4 144.0 %copy-start.20 = (f32[5,768]{1,0:T(8,128)S(1)}, f32[5,768]{1,0:T(8,128)}, u32[]{:S(2)}) copy-start(f32[5,768]{1,0:T(8,128)} %param.57) | copy-start | bytes 46084
  170.4 144.0 %copy-start.21 = (f32[5,768]{1,0:T(8,128)S(1)}, f32[5,768]{1,0:T(8,128)}, u32[]{:S(2)}) copy-start(f32[5,768]{1,0:T(8,128)} %param.56) | copy-start | bytes 46084
  170.5 146.3 %copy-start.22 = (f32[768]{0:T(1024)S(1)}, f32[768]{0:T(1024)}, u32[]{:S(2)}) copy-start(f32[768]{0:T(1024)} %param.52) | copy-start | bytes 9220
  170.5 146.3 %copy-start.26 = (f32[768]{0:T(1024)S(1)}, f32[768]{0:T(1024)}, u32[]{:S(2)}) copy-start(f32[768]{0:T(1024)} %param.54) | copy-start | bytes 9220
  170.5 146.3 %copy-start.27 = (f32[768]{0:T(1024)S(1)}, f32[768]{0:T(1024)}, u32[]{:S(2)}) copy-start(f32[768]{0:T(1024)} %param.53) | copy-start | bytes 9220
  170.5 147.7 %copy-start.18 = (f32[5,3,64]{2,1,0:T(4,128)S(1)}, f32[5,3,64]{2,1,0:T(4,128)}, u32[]{:S(2)}) copy-start(f32[5,3,64]{2,1,0:T(4,128)} %param.49) | copy-start | bytes 11524
  170.5 147.7 %copy-start.24 = (f32[5,3,64]{2,1,0:T(4,128)S(1)}, f32[5,3,64]{2,1,0:T(4,128)}, u32[]{:S(2)}) copy-start(f32[5,3,64]{2,1,0:T(4,128)} %param.51) | copy-start | bytes 11524
  170.5 147.7 %copy-start.25 = (f32[5,3,64]{2,1,0:T(4,128)S(1)}, f32[5,3,64]{2,1,0:T(4,128)}, u32[]{:S(2)}) copy-start(f32[5,3,64]{2,1,0:T(4,128)} %param.50) | copy-start | bytes 11524
  170.5 148.3 %copy-start.5 = (f32[768,96]{0,1:T(8,128)S(1)}, f32[768,96]{0,1:T(8,128)}, u32[]{:S(2)}) copy-start(f32[768,96]{0,1:T(8,128)} %param.46) | copy-start | bytes 884740
  170.5 148.3 %copy-start.11 = (f32[768,96]{0,1:T(8,128)S(1)}, f32[768,96]{0,1:T(8,128)}, u32[]{:S(2)}) copy-start(f32[768,96]{0,1:T(8,128)} %param.48) | copy-start | bytes 884740
  170.6 148.3 %copy-start.12 = (f32[768,96]{0,1:T(8,128)S(1)}, f32[768,96]{0,1:T(8,128)}, u32[]{:S(2)}) copy-start(f32[768,96]{0,1:T(8,128)} %param.47) | copy-start | bytes 884740
  312.4 8.5 %copy-start.2 = (f32[96,768]{1,0:T(8,128)S(1)}, f32[96,768]{1,0:T(8,128)}, u32[]{:S(2)}) copy-start(f32[96,768]{1,0:T(8,128)} %refs_3_.1) | copy-start | bytes 884740
  312.4 8.5 %copy-start.4 = (f32[96,768]{1,0:T(8,128)S(1)}, f32[96,768]{1,0:T(8,128)}, u32[]{:S(2)}) copy-start(f32[96,768]{1,0:T(8,128)} %get-tuple-element.204) | copy-start | bytes 884740
  312.4 8.5 %copy-start.13 = (f32[96,768]{1,0:T(8,128)S(1)}, f32[96,768]{1,0:T(8,128)}, u32[]{:S(2)}) copy-start(f32[96,768]{1,0:T(8,128)} %param.45) | copy-start | bytes 884740
  312.5 8.5 %copy-start.14 = (f32[96,768]{1,0:T(8,128)S(1)}, f32[96,768]{1,0:T(8,128)}, u32[]{:S(2)}) copy-start(f32[96,768]{1,0:T(8,128)} %param.44) | copy-start | bytes 884740
  312.5 9.5 %copy-start.16 = (f32[192,96]{1,0:T(8,128)S(1)}, f32[192,96]{1,0:T(8,128)}, u32[]{:S(2)}) copy-start(f32[192,96]{1,0:T(8,128)} %param.41) | copy-start | bytes 221188
  314.5 7.6 %copy-start.17 = (f32[192,96]{1,0:T(8,128)S(1)}, f32[192,96]{1,0:T(8,128)}, u32[]{:S(2)}) copy-start(f32[192,96]{1,0:T(8,128)} %param.42) | copy-start | bytes 221188
  316.0 6.2 %copy-start.9 = (f32[192,96]{1,0:T(8,128)S(1)}, f32[192,96]{1,0:T(8,128)}, u32[]{:S(2)}) copy-start(f32[192,96]{1,0:T(8,128)} %refs_5_.2) | copy-start | bytes 221188
  316.8 5.5 %copy-start.23 = (f32[768]{0:T(1024)}, f32[768]{0:T(1024)S(1)}, u32[]{:S(2)}) copy-start(f32[768]{0:T(1024)S(1)} %dynamic-slice_reduce_fusion) | copy-start | bytes 9220
  318.2 4.1 %copy-start.19 = (f32[5,3,64]{2,1,0:T(4,128)}, f32[5,3,64]{2,1,0:T(4,128)S(1)}, u32[]{:S(2)}) copy-start(f32[5,3,64]{2,1,0:T(4,128)S(1)} %reshape.102) | copy-start | bytes 11524
  318.9 3.5 %copy-start.10 = (f32[96,192]{1,0:T(8,128)S(1)}, f32[96,192]{1,0:T(8,128)}, u32[]{:S(2)}) copy-start(f32[96,192]{1,0:T(8,128)} %get-tuple-element.98) | copy-start | bytes 221188
  320.9 3.8 %copy-start = (f32[4,96,192]{2,1,0:T(8,128)S(1)}, f32[4,96,192]{2,1,0:T(8,128)}, u32[]{:S(2)}) copy-start(f32[4,96,192]{2,1,0:T(8,128)} %get-tuple-element.196) | copy-start | bytes 884740
  320.9 3.8 %copy-start.1 = (f32[4,96,192]{2,1,0:T(8,128)S(1)}, f32[4,96,192]{2,1,0:T(8,128)}, u32[]{:S(2)}) copy-start(f32[4,96,192]{2,1,0:T(8,128)} %refs_2_.1) | copy-start | bytes 884740
  322.5 7.4 %copy-start.8 = (bf16[384,768]{1,0:T(8,128)(2,1)S(1)}, bf16[384,768]{1,0:T(8,128)(2,1)}, u32[]{:S(2)}) copy-start(bf16[384,768]{1,0:T(8,128)(2,1)} %get-tuple-element.192) | copy-start | bytes 1769476
  324.7 6.0 %copy-start.7 = (f32[384,768]{1,0:T(8,128)S(1)}, f32[384,768]{1,0:T(8,128)}, u32[]{:S(2)}) copy-start(f32[384,768]{1,0:T(8,128)} %get-tuple-element.193) | copy-start | bytes 3538948
  327.8 3.9 %copy-start.6 = (f32[384,768]{1,0:T(8,128)S(1)}, f32[384,768]{1,0:T(8,128)}, u32[]{:S(2)}) copy-start(f32[384,768]{1,0:T(8,128)} %get-tuple-element.194) | copy-start | bytes 3538948
  331.7 2.5 copy-start.3

commit v5 on v4

--- a/solution.py
+++ b/solution.py
@@ -115,16 +115,15 @@
 
 
 class Scatter:
-    def __init__(self, links, sems, sem, source, order, refs):
+    def __init__(self, links, sem, source, rows, order, refs):
         self.kept, self.got, self.got_two, self.got_last = refs
-        self.order = order
         heads_here, dp_here = lax.axis_index("heads"), lax.axis_index("dp")
         x, y, z = heads_here >> 1, dp_here & 1, dp_here >> 1
         if order == "xy":
-            own, other, first, second, self.mine = source.at[:, :, x], source.at[:, :, 1 - x], ("heads", 2), ("dp", 1), y
+            own, other, first, second, self.mine = source.at[:, :, x, rows], source.at[:, :, 1 - x, rows], ("heads", 2), ("dp", 1), y
         else:
-            own, other, first, second, self.mine = source.at[:, y], source.at[:, 1 - y], ("dp", 1), ("heads", 2), x
-        self.load = pltpu.make_async_copy(own, self.kept, sems.at[sem])
+            own, other, first, second, self.mine = source.at[:, y, :, rows], source.at[:, 1 - y, :, rows], ("dp", 1), ("heads", 2), x
+        self.load = pltpu.make_async_copy(own, self.kept, sem)
         self.copy = links.push(other, self.got, *first)
         self.copy_two = links.push(self.kept.at[:, 1 - self.mine], self.got_two, *second)
         self.place = z
@@ -160,6 +159,26 @@
 
 def square_sum(values):
     return jnp.sum(jnp.sum(values * values, -1, keepdims=True), 0, keepdims=True)
+
+
+def unit_copies(links, source, places, starts, size, base):
+    heads_here = lax.axis_index("heads")
+    own = places.shape[1]
+    copies = []
+    for start in starts:
+        owner = start // own
+        distance = owner ^ heads_here
+        index = links.used
+        links.used = index + 1
+        copies.append(
+            pltpu.make_async_remote_copy(
+                source.at[pl.ds(pl.multiple_of(start, size), size)],
+                places.at[distance, pl.ds(pl.multiple_of(start - owner * own, size), size)],
+                links.send_sems.at[index], links.recv_sems.at[base + distance],
+                device_id={"heads": owner}, device_id_type=pl.DeviceIdType.MESH,
+            )
+        )
+    return copies
 
 
 class Gather:
@@ -265,17 +284,17 @@
 def attention_forward_kernel(head_size, group, parts, fast, *refs):
     content_hbm, query_hbm, weight_in, up_in, down_in, out_in, bias_in, refs = *refs[:7], refs[7:]
     lengths_ref, order_ref, segment_ref, table_ref, head_ref, refs = *refs[:5], refs[5:]
-    proj_ref, logsum_ref, row_ref, col_ref, bias_all, refs = *refs[:5], refs[5:]
-    mixed_pieces, refs = refs[:group], refs[group:]
-    content_out, query_out, weight_out, refs = *refs[:3], refs[3:]
+    proj_ref, row_ref, col_ref, bias_all, refs = *refs[:4], refs[4:]
+    mixed_pieces, refs = refs[0], refs[1:]
+    content_out, query_out, weight_out, chance_out, refs = *refs[:4], refs[4:]
     if fast:
         up_all, down_all, out_all, refs = *refs[:3], refs[3:]
-    content_all, query_all, weight_ref, mixed_ref, relative_ref, mask_ref, refs = *refs[:6], refs[6:]
+    content_all, query_all, weight_ref, mixed_ref, relative_ref, mask_ref, chance_ref, refs = *refs[:7], refs[7:]
     sems, send_sems, recv_sems, refs = *refs[:3], refs[3:]
     rows, length = row_ref.shape[0], row_ref.shape[2]
     half = length // 2
     tokens, depth = content_hbm.shape
-    width = weight_ref.shape[-1]
+    width = weight_ref.shape[-1] // 4
     heads = width // head_size
     factor = head_size ** (-0.5) * LOG2E
     heads_here, dp_here = lax.axis_index("heads"), lax.axis_index("dp")
@@ -299,7 +318,7 @@
         )
     if fast:
         weight_send, up_send, down_send, out_send = refs
-        weight_send[...] = weight_in[...].astype(jnp.bfloat16)
+        weight_send[...] = jnp.concatenate([weight_in[kind] for kind in range(4)], -1).astype(jnp.bfloat16)
     pl.semaphore_wait(barrier, len(peers))
     far = [links.push(own, full.at[token_part(0)], "heads", 2) for own, full in streams]
     near = [links.push(own, full.at[token_part(0)], "heads", 1) for own, full in streams]
@@ -310,16 +329,16 @@
     if fast:
         y, z = dp_here & 1, dp_here >> 1
         weight_z, weight_y = [], []
-        for pair in (slice(0, 2), slice(2, 4)):
-            mine = weight_ref.at[pair, z, y]
-            weight_z.append([links.push(weight_send.at[pair], mine, "dp", 2 * m) for m in range(1, parts // 2)])
-            column = weight_ref.at[pair, :, y]
+        for pair in (pl.ds(0, 2 * width), pl.ds(2 * width, 2 * width)):
+            mine = weight_ref.at[z, y, :, pair]
+            weight_z.append([links.push(weight_send.at[:, pair], mine, "dp", 2 * m) for m in range(1, parts // 2)])
+            column = weight_ref.at[:, y, :, pair]
             weight_y.append(links.push(column, column, "dp", 1))
             for copy in weight_z[-1]:
                 copy.start()
-        weight_ref[:, z, y] = weight_send[...]
+        weight_ref[z, y] = weight_send[...]
         up_send[...] = up_in[...].astype(jnp.bfloat16)
-        down_send[...] = turn(down_in[...])
+        down_send[...] = down_in[...].astype(jnp.bfloat16)
         out_send[...] = turn(out_in[...])
         pick = up_send.shape[0]
         early, late = pl.ds(0, pick // 2), pl.ds(pick // 2, pick // 2)
@@ -345,8 +364,8 @@
     for copy in local + near:
         copy.wait()
 
-    def weight(kind):
-        return weight_ref[kind].reshape(depth, width)
+    def weight(first, last):
+        return weight_ref[..., first * width : last * width].reshape(depth, (last - first) * width)
 
     saves = [
         pltpu.make_async_copy(content_all, content_out, sems.at[0]),
@@ -354,7 +373,7 @@
         pltpu.make_async_copy(weight_ref, weight_out, sems.at[2]),
     ]
     saves[2].start()
-    relative_ref[...] = dot(table_ref[...], weight(3)).astype(jnp.bfloat16)
+    relative_ref[...] = dot(table_ref[...], weight(3, 4)).astype(jnp.bfloat16)
 
     def pass_on():
         for arrived, onward in zip(far, passed):
@@ -396,10 +415,8 @@
         content, query = content_all[here], query_all[here]
         joined = jnp.concatenate(
             [
-                dot(content, weight(0)).astype(jnp.bfloat16),
-                dot(content, weight(1)).astype(jnp.bfloat16),
-                dot(content, weight(2)).astype(jnp.bfloat16),
-                dot(query, weight(0)).astype(jnp.bfloat16),
+                dot(content, weight(0, 3)).astype(jnp.bfloat16),
+                dot(query, weight(0, 1)).astype(jnp.bfloat16),
             ],
             -1,
         )
@@ -409,7 +426,7 @@
         for head in range(heads):
             cols = lambda kind: slice(kind * width + head * head_size, kind * width + (head + 1) * head_size)
             own_cols = slice(head * head_size, (head + 1) * head_size)
-            bias = [head_ref[kind : kind + 1, own_cols] for kind in range(5)]
+            bias = [head_ref[kind, head : head + 1] for kind in range(5)]
             keys, values = proj_ref[row, :, cols(1)], proj_ref[row, :, cols(2)]
             keys_twice = jnp.concatenate([keys, keys], -1)
             relative = relative_ref[:, own_cols]
@@ -428,9 +445,9 @@
                     highest = jnp.maximum(jnp.max(scores, -1, keepdims=True), 0.0)
                     weights = jnp.exp2(scores - highest)
                     totals = jnp.exp2(-highest) + jnp.sum(weights, -1, keepdims=True)
-                    pieces.append(dot(weights.astype(jnp.bfloat16), values[part]) / totals)
-                    index = stream * heads + head
-                    logsum_ref[row, part, index : index + 1] = highest + jnp.log2(totals)
+                    chances = (weights * (1.0 / totals)).astype(jnp.bfloat16)
+                    chance_ref[row, stream * heads + head, block] = chances
+                    pieces.append(dot(chances, values[part]))
                 mixed[stream][head] = jnp.concatenate(pieces, 0).astype(jnp.bfloat16)
             for when, actions in events.items():
                 if when[1] == head:
@@ -439,17 +456,39 @@
                         for action in actions:
                             action()
         both = jnp.concatenate(mixed[0] + mixed[1], -1)
-        both = dot(unroll, both).astype(jnp.bfloat16)
-        mixed_ref[0, here] = both[:, :width]
-        mixed_ref[1, here] = both[:, width:]
+        mixed_ref[here] = dot(unroll, both).astype(jnp.bfloat16)
+        chance_copy(row).start()
+
+        @pl.when(step == 1)
+        def _():
+            for copy in far_units:
+                copy.start()
+
         return carry
 
+    def chance_copy(row):
+        return pltpu.make_async_copy(chance_ref.at[row], chance_out.at[row], sems.at[9 + row])
+
+    unit = half // 2
+    far_row = jnp.where(chip == 0, (rows - 1) * length, 0)
+    far_middle = jnp.where(chip == 0, length + half, length)
+    base = links.used
+    links.used = base + group
+    far_units = unit_copies(links, mixed_ref, mixed_pieces, [far_row + n * unit for n in range(4)], unit, base)
+    middle_units = unit_copies(links, mixed_ref, mixed_pieces, [far_middle + n * unit for n in range(2)], unit, base)
+    far_pieces = [
+        pltpu.make_async_remote_copy(
+            mixed_pieces.at[k], mixed_pieces.at[k], send_sems.at[base + k], recv_sems.at[base + k],
+            device_id={"heads": heads_here ^ k}, device_id_type=pl.DeviceIdType.MESH,
+        )
+        for k in (2, 3)
+    ]
     lax.fori_loop(0, rows, one_row, 0)
-    keep = pltpu.make_async_copy(mixed_ref.at[:, token_part(0)], mixed_pieces[0], sems.at[8])
+    for copy in middle_units:
+        copy.start()
+    keep = pltpu.make_async_copy(mixed_ref.at[token_part(0)], mixed_pieces.at[0], sems.at[8])
     keep.start()
-    sends = [
-        links.push(mixed_ref.at[:, token_part(k)], mixed_pieces[k], "heads", k) for k in (2, 3, 1)[: group - 1]
-    ]
+    sends = [links.push(mixed_ref.at[token_part(1)], mixed_pieces.at[1], "heads", 1)]
     for copy in sends:
         copy.start()
     if fast:
@@ -457,6 +496,12 @@
         down_two.step_three()
     for copy in [keep] + saves + sends + bias_copies:
         copy.wait()
+    for copy in far_units + middle_units:
+        copy.wait_send()
+    for row in range(rows):
+        chance_copy(row).wait()
+    for piece in far_pieces:
+        piece.wait_recv()
     if fast:
         for gather in gathers:
             gather.finish()
@@ -479,26 +524,28 @@
     outside = pl.BlockSpec(memory_space=pl.ANY)
     scalars = pl.BlockSpec(memory_space=pltpu.SMEM)
     bfloat, float32 = jnp.bfloat16, jnp.float32
-    weight_shape = (4, parts // 2, 2, pick, width) if fast else (4, depth, width)
+    weight_shape = (parts // 2, 2, pick, 4 * width) if fast else (depth, 4 * width)
     out_shape = [
         jax.ShapeDtypeStruct((rows, length, 4 * width), bfloat),
-        jax.ShapeDtypeStruct((rows, length, 8), float32),
         jax.ShapeDtypeStruct((rows, 8, length), float32),
         jax.ShapeDtypeStruct((rows, length, 8), float32),
         jax.ShapeDtypeStruct((group, 1, hidden), float32),
     ]
-    out_specs = [inside] * 5 + [outside] * (group + 3)
-    out_shape += [jax.ShapeDtypeStruct((2, own, width), bfloat)] * group
+    out_specs = [inside] * 4 + [outside] * 5
+    out_shape += [jax.ShapeDtypeStruct((group, own, 2 * width), bfloat)]
     out_shape += [jax.ShapeDtypeStruct((tokens, depth), bfloat)] * 2
     out_shape += [jax.ShapeDtypeStruct(weight_shape, bfloat)]
+    chance_shape = (rows, 2 * width // head_size, 2, half, half)
+    out_shape += [jax.ShapeDtypeStruct(chance_shape, bfloat)]
     scratch = [
         pltpu.VMEM((tokens, depth), bfloat),
         pltpu.VMEM((tokens, depth), bfloat),
         pltpu.VMEM(weight_shape, bfloat),
-        pltpu.VMEM((2, tokens, width), bfloat),
+        pltpu.VMEM((tokens, 2 * width), bfloat),
         pltpu.VMEM((length, width), bfloat),
         pltpu.VMEM((2, 2, half, half), float32),
-        pltpu.SemaphoreType.DMA((9,)),
+        pltpu.VMEM(chance_shape, bfloat),
+        pltpu.SemaphoreType.DMA((9 + rows,)),
         pltpu.SemaphoreType.DMA((72,)),
         pltpu.SemaphoreType.DMA((72,)),
     ]
@@ -509,7 +556,7 @@
             jax.ShapeDtypeStruct((parts // 2, 2, group // 2, 2, pick, c), bfloat) for c in (hidden, hidden, width)
         ]
         scratch += [
-            pltpu.VMEM((4, pick, width), bfloat),
+            pltpu.VMEM((pick, 4 * width), bfloat),
             pltpu.VMEM((pick, hidden), bfloat),
             pltpu.VMEM((pick, hidden), bfloat),
             pltpu.VMEM((pick, width), bfloat),
@@ -517,6 +564,7 @@
     else:
         weight_spec = outside
         attn_proj = lax.all_gather(attn_proj.astype(bfloat), "dp", axis=1, tiled=True)
+        attn_proj = jnp.swapaxes(attn_proj, 0, 1).reshape(weight_shape)
     results = pl.pallas_call(
         functools.partial(attention_forward_kernel, head_size, group, parts if fast else 1, fast),
         in_specs=[outside, outside, weight_spec] + [inside] * 4 + [scalars] + [inside] * 4,
@@ -527,40 +575,38 @@
             vmem_limit_bytes=VMEM_LIMIT, collective_id=0, has_side_effects=True
         ),
     )(
-        content, query, attn_proj, up_proj, down_proj, out_proj, up_bias[None], doc_lengths, factor_order,
-        segment_ids, table, head_bias.reshape(5, width),
+        content, query, attn_proj, up_proj, down_proj.T, out_proj, up_bias[None], doc_lengths, factor_order,
+        segment_ids, table, head_bias,
     )
-    proj, logsum, facts_row, facts_col, bias_all = results[:5]
-    mixed_pieces, results = results[5 : 5 + group], results[5 + group :]
-    content_all, query_all, weight_all = results[:3]
-    if fast:
-        wide = [full.reshape(parts, group, pick, full.shape[-1]) for full in results[3:]]
+    proj, facts_row, facts_col, bias_all, mixed_pieces = results[:5]
+    content_all, query_all, weight_all, chance_all = results[5:9]
+    if fast:
+        wide = [full.reshape(parts, group, pick, full.shape[-1]) for full in results[9:]]
     else:
         wide = [gather_all(m) for m in (up_proj.astype(bfloat), down_proj.T.astype(bfloat), out_proj.T.astype(bfloat))]
-    kept = (content_all, query_all, weight_all, (facts_row, facts_col), proj, logsum)
+    kept = (content_all, query_all, weight_all, chance_all, (facts_row, facts_col), proj)
     return kept, bias_all, mixed_pieces, wide
 
 
 def attention_backward_kernel(head_size, group, parts, fast, *refs):
-    content_hbm, query_hbm, weight_hbm, refs = *refs[:3], refs[3:]
-    upper_pieces, dresid_hbm, refs = refs[:group], refs[group], refs[group + 1 :]
-    table_ref, turned_ref, bias_ref, row_ref, col_ref, proj_ref, logsum_ref = refs[:7]
-    sources, small_ref, refs = refs[7:10], refs[10], refs[11:]
+    content_hbm, query_hbm, weight_hbm, chance_hbm, refs = *refs[:4], refs[4:]
+    upper_pieces, dresid_hbm, refs = refs[0], refs[1], refs[2:]
+    turned_ref, bias_ref, row_ref, col_ref, proj_ref = refs[:5]
+    sources, small_ref, refs = refs[5:8], refs[8], refs[9:]
     outputs, refs = refs[:9] if fast else refs[:4], refs[9:] if fast else refs[4:]
     content_grad_ref, query_grad_ref, dhead_ref = outputs[:3]
     content_all, query_all, weight_ref, upper_all, dinput_ref, dweight_ref = refs[:6]
-    relative_ref, backward_ref, mask_ref, drel_ref, dcols_ref, dkeys_ref, dvalues_ref = refs[6:13]
-    dwide_ref, near_ref, cross_ref, far_ref, dresid_ref, dhead_own, refs = *refs[13:19], refs[19:]
+    chance_ref, backward_ref, drel_ref, dcols_ref, dkeys_ref, dvalues_ref = refs[6:12]
+    dwide_ref, side_ref, cross_ref, swap_ref, dresid_ref, dhead_own, refs = *refs[12:18], refs[18:]
     sems, send_sems, recv_sems, refs = *refs[:3], refs[3:]
     rows, length = row_ref.shape[0], row_ref.shape[2]
     half = length // 2
-    depth, width = content_all.shape[1], weight_ref.shape[-1]
+    depth, width = content_all.shape[1], weight_ref.shape[-1] // 4
     heads = width // head_size
     scale = head_size ** (-0.5)
-    factor = scale * LOG2E
     heads_here, dp_here = lax.axis_index("heads"), lax.axis_index("dp")
     chip = heads_here >> 1
-    tokens = upper_pieces[0].shape[1]
+    tokens = upper_pieces.shape[1]
     links = Links(send_sems, recv_sems)
 
     def token_part(k):
@@ -570,15 +616,16 @@
         pltpu.make_async_copy(content_hbm, content_all, sems.at[0]),
         pltpu.make_async_copy(query_hbm, query_all, sems.at[1]),
         pltpu.make_async_copy(weight_hbm, weight_ref, sems.at[2]),
-        pltpu.make_async_copy(upper_pieces[0], upper_all.at[:, token_part(0)], sems.at[3]),
+        pltpu.make_async_copy(chance_hbm, chance_ref, sems.at[10]),
+        pltpu.make_async_copy(upper_pieces.at[0], upper_all.at[token_part(0)], sems.at[3]),
     ]
     for copy in copies:
         copy.start()
     dresid_copy = pltpu.make_async_copy(dresid_hbm, dresid_ref, sems.at[4])
     dresid_copy.start()
 
-    def weight(kind):
-        return weight_ref[kind].reshape(depth, width)
+    def weight(first, last):
+        return weight_ref[..., first * width : last * width].reshape(depth, (last - first) * width)
 
     barrier = pltpu.get_barrier_semaphore()
     peers = [("heads", k) for k in range(1, group)] + [("dp", k) for k in range(1, parts)]
@@ -588,18 +635,21 @@
         )
     pl.semaphore_wait(barrier, len(peers))
     upper_copies = [
-        links.push(upper_pieces[k], upper_all.at[:, token_part(0)], "heads", k) for k in range(1, group)
+        links.push(upper_pieces.at[k], upper_all.at[token_part(0)], "heads", k) for k in range(1, group)
     ]
     for copy in upper_copies:
         copy.start()
     if fast:
+        pick = sources[0].shape[3]
+        early, late, full = pl.ds(0, pick // 2), pl.ds(pick // 2, pick // 2), pl.ds(0, pick)
+        plan = ((0, early, "yx"), (0, late, "yx"), (1, early, "yx"), (1, late, "xy"), (2, full, "yx"))
         scatters = [
-            Scatter(links, sems, 5 + n, sources[n], order, refs[4 * n : 4 * n + 4])
-            for n, order in enumerate(("xy", "yx", "yx"))
+            Scatter(links, sems.at[5 + n], sources[which], part, order, refs[4 * n : 4 * n + 4])
+            for n, (which, part, order) in enumerate(plan)
         ]
-        small_got, small_more, small_mid, dweight_got, dweight_more, head_got, tile_ref, tile_got, tile_more = refs[12:]
-        for scatter in scatters:
-            scatter.begin()
+        up_one, up_two, down_one, down_two, out_one = scatters
+        small_got, small_more, small_mid, dweight_got, dweight_more, head_got, tile_ref, tile_got, tile_more = refs[20:]
+        up_one.begin()
         small_first = [links.push(small_ref, small_got.at[heads_here], "heads", k) for k in range(1, group)]
         for copy in small_first:
             copy.start()
@@ -608,17 +658,55 @@
     for copy in copies:
         copy.wait()
     upper_copies[0].wait()
-    relative_ref[...] = dot(table_ref[...], weight(3)).astype(jnp.bfloat16)
-    backward_ref[...] = dot(turned_ref[...], weight(3)).astype(jnp.bfloat16)
+    backward_ref[...] = dot(turned_ref[...], weight(3, 4)).astype(jnp.bfloat16)
     drel_ref[...] = jnp.zeros_like(drel_ref)
     dweight_ref[...] = jnp.zeros_like(dweight_ref)
     dhead_own[...] = jnp.zeros_like(dhead_own)
-
-    def after(step, place, body):
-        if fast:
-            @pl.when(step == place)
-            def _():
-                body()
+    bias_cols = [bias_ref[kind].T for kind in range(2)]
+    ones = jnp.ones((16, length), jnp.bfloat16)
+
+    def act(condition, actions):
+        @pl.when(condition)
+        def _():
+            for action in actions:
+                action()
+
+    def span(start, size):
+        return pl.ds(pl.multiple_of(start, size), size)
+
+    def sides(first, size, slot):
+        mine, other = span(first + core * size, size), span(first + (1 - core) * size, size)
+        landed = side_ref.at[:, pl.ds(slot, size)]
+        return links.push(dinput_ref.at[:, other], landed, "heads", 1), mine, landed
+
+    def add_side(side, landed=None):
+        copy, mine, place = side
+        copy.wait()
+        for n in range(2):
+            dinput_ref[n, mine] = (
+                dinput_ref[n, mine].astype(jnp.float32) + place[n].astype(jnp.float32)
+            ).astype(jnp.bfloat16)
+
+    core, unit = heads_here & 1, half // 2
+    own_first = jnp.where(chip == 0, 0, (rows - 1) * length)
+    far_first = jnp.where(chip == 0, (rows - 1) * length, 0)
+    own_middle = jnp.where(chip == 0, length, length + half)
+    far_middle = jnp.where(chip == 0, length + half, length)
+    own_side, far_side = sides(own_first, half, 0), sides(far_first, half, half)
+    own_side_two, far_side_two = sides(own_middle, unit, 2 * half), sides(far_middle, unit, 2 * half + unit)
+    across = [
+        (links.push(dinput_ref.at[:, side[1]], cross_ref.at[:, place], "heads", 2), mine[1], cross_ref.at[:, place])
+        for side, mine, place in (
+            (far_side, own_side, pl.ds(0, half)), (far_side_two, own_side_two, pl.ds(half, unit))
+        )
+    ]
+    swap_part = span(2 * half + 5 * unit * chip - half * core, unit)
+    swap_got = span(2 * half + 5 * unit * chip - half * (1 - core), unit)
+    swap = links.push(dinput_ref.at[:, swap_part], swap_ref, "heads", 1)
+
+    def far_over():
+        add_side(far_side)
+        across[0][0].start()
 
     def small_middle():
         for copy in small_first:
@@ -631,6 +719,27 @@
         for copy in small_second:
             copy.start()
 
+    events = {
+        (0, heads): [own_side[0].start],
+        (1, heads): [far_side[0].start],
+        (2, 0): [far_over, lambda: add_side(own_side)],
+    }
+    if fast:
+        for place, actions in {
+            (0, 0): [up_two.begin],
+            (0, 1): [down_two.begin],
+            (0, 2): [up_one.second, down_one.begin],
+            (0, heads): [out_one.begin],
+            (1, 0): [small_middle, up_two.second, up_one.third],
+            (1, 1): [down_two.second],
+            (1, 2): [up_two.third, down_one.second],
+            (1, heads): [out_one.second],
+            (2, 0): [down_two.third],
+            (2, 1): [down_one.third],
+            (2, 2): [out_one.third],
+        }.items():
+            events[place] = events.get(place, []) + actions
+
     def one_row(step, carry):
         row = jnp.where(step == 0, 0, rows - step)
         row = jnp.where(chip == 0, row, rows - 1 - row)
@@ -647,10 +756,9 @@
         here = pl.ds(pl.multiple_of(row * length, length), length)
         content_ref, query_ref = content_all.at[here], query_all.at[here]
         facts_row, facts_col = row_ref[row], col_ref[row]
-        write_masks(mask_ref, facts_row, facts_col, half)
         roll = roll_matrix(facts_col[:, 3:4], length)
-        upper = dot(roll, jnp.concatenate([upper_all[0, here], upper_all[1, here]], -1)).astype(jnp.bfloat16)
-        segment_col, segment_row = facts_col[:, 2:3], facts_row[2:3, :]
+        upper = dot(roll, upper_all[here]).astype(jnp.bfloat16)
+        segment_col = facts_col[:, 2:3]
         down = lax.broadcasted_iota(jnp.int32, (half, half), 0)
         along = lax.broadcasted_iota(jnp.int32, (half, half), 1)
         mirror = jnp.where(down + along == half - 1, 1.0, 0.0).astype(jnp.bfloat16)
@@ -659,34 +767,27 @@
         for head in range(heads):
             own_cols = slice(head * head_size, (head + 1) * head_size)
             cols = lambda kind: slice(kind * width + head * head_size, kind * width + (head + 1) * head_size)
-            bias = [bias_ref[kind : kind + 1, own_cols] for kind in range(5)]
+            bias = [bias_ref[kind, head : head + 1] for kind in range(5)]
             keys, values = proj_ref[row, :, cols(1)], proj_ref[row, :, cols(2)]
-            keys_twice = jnp.concatenate([keys, keys], -1)
             keys_extra = jnp.concatenate([keys, extra], -1)
-            relative = relative_ref[:, own_cols]
-            relative_twice = jnp.concatenate([relative, relative], -1)
             backward = backward_ref[:, own_cols]
+            u_col, w_col = (turned_bias[:, head : head + 1] for turned_bias in bias_cols)
             heads_sums = [jnp.zeros((1, head_size), jnp.float32) for _ in range(5)]
             for stream in range(2):
-                with_u, with_w, with_c, own, slope = query_sides(
-                    proj_ref[row, :, cols(3 * stream)], bias, segment_col, factor
-                )
+                query_now = proj_ref[row, :, cols(3 * stream)]
+                with_c = query_now.astype(jnp.float32) + bias[2]
                 index = stream * heads + head
-                own = own - logsum_ref[row, :, index : index + 1]
                 upper_now = upper[:, index * head_size : (index + 1) * head_size]
-                with_u_t, with_w_t, upper_t = with_u.T, with_w.T, upper_now.T
+                query_t, upper_t = jnp.concatenate([query_now.T, ones], 0), upper_now.T
                 dquery = []
                 for block in range(2):
                     part = slice(block * half, (block + 1) * half)
-                    scores = block_scores(
-                        with_u[part], with_w[part], keys_twice[part], relative_twice, half
-                    )
-                    scores = scores + own[part] + slope[part] * segment_row[:, part] + mask_ref[stream, block]
-                    chances = jnp.exp2(scores)
-                    dchance = dot_nt(upper_now[part], values[part])
-                    centre = jnp.sum(chances * dchance, -1, keepdims=True)
-                    dscore = (chances * (dchance - centre)).astype(jnp.bfloat16)
-                    dvalue_part = dot(upper_t[:, part], chances.astype(jnp.bfloat16))
+                    low_chances = chance_ref[row, index, block]
+                    chances = low_chances.astype(jnp.float32)
+                    weighted = chances * dot_nt(upper_now[part], values[part])
+                    centre = jnp.sum(weighted, -1, keepdims=True)
+                    dscore = (weighted - chances * centre).astype(jnp.bfloat16)
+                    dvalue_part = dot(upper_t[:, part], low_chances)
                     by_key = dot(dscore, keys_extra[part])
                     turned = dot(dscore, mirror)
                     wide = pltpu.roll(
@@ -694,10 +795,10 @@
                         0, 1, stride=1, stride_axis=0,
                     ).astype(jnp.bfloat16)
                     by_place = dot(wide, backward)
-                    dkey_part = dot(with_u_t[:, part], dscore)
-                    dkey_part = dkey_part[:head_size] + dkey_part[head_size:]
-                    drel_part = dot(with_w_t[:, part], wide)
-                    drel_ref[own_cols] += drel_part[:head_size] + drel_part[head_size:]
+                    dkey_part = dot(query_t[:, part], dscore)
+                    dkey_part = dkey_part[:head_size] + u_col * dkey_part[head_size : head_size + 1]
+                    drel_part = dot(query_t[:, part], wide)
+                    drel_ref[own_cols] += drel_part[:head_size] + w_col * drel_part[head_size : head_size + 1]
                     if stream == 0:
                         dkeys_ref[own_cols, part] = dkey_part
                         dvalues_ref[own_cols, part] = dvalue_part
@@ -715,72 +816,57 @@
                         (by_key, by_place, by_segment, seg_zero * with_c[part], seg_one * with_c[part])
                     ):
                         heads_sums[kind] = heads_sums[kind] + jnp.sum(term, 0, keepdims=True)
-                dcols_ref[:, cols(stream)] = jnp.concatenate(dquery, 0).astype(jnp.bfloat16)
+                dcols_ref[:, cols(3 * stream)] = jnp.concatenate(dquery, 0).astype(jnp.bfloat16)
             for kind in range(5):
                 dhead_own[kind : kind + 1, own_cols] += heads_sums[kind] * scale
-            if fast and head == 0:
-                after(step, 1, small_middle)
-            if fast and head == heads - 1:
-                after(step, 1, lambda: [scatter.second() for scatter in scatters[1:]])
-                after(step, 2, lambda: [scatter.third() for scatter in scatters])
-        dcols_ref[:, 2 * width : 3 * width] = (dkeys_ref[...] * (1.0 / LOG2E)).astype(jnp.bfloat16).T
-        dcols_ref[:, 3 * width :] = dvalues_ref[...].astype(jnp.bfloat16).T
+            for when, actions in events.items():
+                if when[1] == head:
+                    act(step == when[0], actions)
+        dcols_ref[:, width : 2 * width] = (dkeys_ref[...] * scale).astype(jnp.bfloat16).T
+        dcols_ref[:, 2 * width : 3 * width] = dvalues_ref[...].astype(jnp.bfloat16).T
         unroll = unroll_matrix(facts_row[3:4, :], length)
         joined = dot(unroll, dcols_ref[...]).astype(jnp.bfloat16)
         joined_t = joined.T
         content, query = content_ref[...], query_ref[...]
-        dweight_ref[0] += dot(joined_t[:width], content) + dot(joined_t[width : 2 * width], query)
-        dweight_ref[1] += dot(joined_t[2 * width : 3 * width], content)
-        dweight_ref[2] += dot(joined_t[3 * width :], content)
-        dinput_ref[0, here] = (
-            dot_nt(joined[:, :width], weight(0))
-            + dot_nt(joined[:, 2 * width : 3 * width], weight(1))
-            + dot_nt(joined[:, 3 * width :], weight(2))
-        ).astype(jnp.bfloat16)
-        dinput_ref[1, here] = dot_nt(joined[:, width : 2 * width], weight(0)).astype(jnp.bfloat16)
-        if fast:
-            after(step, 1, scatters[0].second)
+        dweight_ref[: 3 * width] += dot(joined_t[: 3 * width], content)
+        dweight_ref[:width] += dot(joined_t[3 * width :], query)
+        dinput_ref[0, here] = dot_nt(joined[:, : 3 * width], weight(0, 3)).astype(jnp.bfloat16)
+        dinput_ref[1, here] = dot_nt(joined[:, 3 * width :], weight(0, 1)).astype(jnp.bfloat16)
+        for when, actions in events.items():
+            if when[1] == heads:
+                act(step == when[0], actions)
 
     lax.fori_loop(0, rows, one_row, 0)
-    drel = drel_ref[...] * (1.0 / LOG2E)
+    for side in (far_side_two, own_side_two):
+        side[0].start()
+    drel = drel_ref[...] * scale
     high = drel.astype(jnp.bfloat16)
     low = (drel - high.astype(jnp.float32)).astype(jnp.bfloat16)
-    dweight_ref[3] = dot(high, turned_ref[...]) + dot(low, turned_ref[...])
-    cross = [
-        links.push(dinput_ref.at[n, token_part(3)], cross_ref.at[n], "heads", 1) for n in range(2)
-    ]
-    near = [links.push(dinput_ref.at[n, token_part(1)], near_ref.at[n], "heads", 1) for n in range(2)]
-    far = [links.push(cross_ref.at[n], far_ref.at[n], "heads", 2) for n in range(2)]
-    for copy in cross + near:
-        copy.start()
-    for kind in range(4):
-        turned = dweight_ref[kind].astype(jnp.bfloat16).T
-        dwide_ref[kind] = turned.reshape(dwide_ref.shape[1:])
+    dweight_ref[3 * width :] = dot(high, turned_ref[...]) + dot(low, turned_ref[...])
+    dwide_ref[...] = dweight_ref[...].astype(jnp.bfloat16).T.reshape(dwide_ref.shape)
     if fast:
         place_y, place_z = dp_here & 1, dp_here >> 1
-        dweight_first = links.push(dwide_ref.at[:, :, 1 - place_y], dweight_got, "dp", 1)
+        dweight_first = links.push(dwide_ref.at[:, 1 - place_y], dweight_got, "dp", 1)
         dweight_first.start()
         head_copies = [links.push(dhead_own, head_got.at[dp_here], "dp", k) for k in range(1, parts)]
         for copy in head_copies:
             copy.start()
         head_got[dp_here] = dhead_own[...]
-    for n in range(2):
-        cross[n].wait()
-        both = cross_ref[n].astype(jnp.float32) + dinput_ref[n, token_part(2)].astype(jnp.float32)
-        cross_ref[n] = both.astype(jnp.bfloat16)
-        far[n].start()
+    add_side(far_side_two)
+    across[1][0].start()
+    add_side(own_side_two)
     if fast:
         dweight_first.wait()
-        dweight_second = []
-        for kind in range(4):
-            dweight_got[kind] = (
-                dweight_got[kind].astype(jnp.float32) + dwide_ref[kind, :, place_y].astype(jnp.float32)
-            ).astype(jnp.bfloat16)
-        for m in range(1, 4):
-            dweight_second.append(
-                links.push(dweight_got.at[:, place_z ^ m], dweight_more.at[m - 1], "dp", 2 * m)
-            )
-            dweight_second[-1].start()
+        add_planes(dweight_got, lambda z: dwide_ref[z, place_y], dweight_got)
+        dweight_second = [
+            links.push(dweight_got.at[place_z ^ m], dweight_more.at[m - 1], "dp", 2 * m) for m in range(1, 4)
+        ]
+        for copy in dweight_second:
+            copy.start()
+    for side in across:
+        add_side(side)
+    swap.start()
+    if fast:
         up_share, down_share, out_share, proj_share, small_sum, norm_ref = outputs[3:]
         squares = jnp.zeros((1, 1), jnp.float32)
         for copy in small_second:
@@ -797,17 +883,17 @@
             total = total + head_got[k]
         dhead_ref[...] = total
         squares = squares + square_sum(total) / parts
-        for scatter, share in zip(scatters, (up_share, down_share, out_share)):
-            share[...] = scatter.last()
-            squares = squares + square_sum(share[...])
+        for (which, part, _), scatter in zip(plan, scatters):
+            total = scatter.last()
+            (up_share, down_share, out_share)[which][part] = total
+            squares = squares + square_sum(total)
         for copy in dweight_second:
             copy.wait()
-        for kind in range(4):
-            total = dweight_got[kind, place_z].astype(jnp.float32)
-            for m in range(1, 4):
-                total = total + dweight_more[m - 1, kind].astype(jnp.float32)
-            proj_share[kind] = total
-            squares = squares + square_sum(total)
+        total = dweight_got[place_z].astype(jnp.float32)
+        for m in range(1, 4):
+            total = total + dweight_more[m - 1].astype(jnp.float32)
+        proj_share[...] = total
+        squares = squares + square_sum(total)
         tile_ref[...] = jnp.broadcast_to(squares, tile_ref.shape)
         tile_got[heads_here] = tile_ref[...]
         tile_first = [links.push(tile_ref, tile_got.at[heads_here], "heads", k) for k in range(1, group)]
@@ -828,15 +914,10 @@
         for copy in tile_second:
             copy.start()
     dresid_copy.wait()
+    swap.wait()
+    dinput_ref[:, swap_got] = swap_ref[...]
     for n, place in enumerate((content_grad_ref, query_grad_ref)):
-        near[n].wait()
-        far[n].wait()
-        place[...] = (
-            dresid_ref[n]
-            + dinput_ref[n, token_part(0)].astype(jnp.float32)
-            + near_ref[n].astype(jnp.float32)
-            + far_ref[n].astype(jnp.float32)
-        )
+        place[...] = dresid_ref[n] + dinput_ref[n, token_part(0)].astype(jnp.float32)
     if fast:
         for copy in tile_second:
             copy.wait()
@@ -847,15 +928,15 @@
 
 
 def attention_backward(
-    kept, tables, head_bias, upper_pieces, dresid, gradients, small
+    kept, table, head_bias, upper, dresid, gradients, small
 ):
-    content_all, query_all, weight_all, facts, proj, logsum = kept
+    content_all, query_all, weight_all, chance_all, facts, proj = kept
     rows, length = facts[0].shape[0], facts[0].shape[2]
-    group = len(upper_pieces)
-    fast = weight_all.ndim == 5
+    group = upper.shape[0]
+    fast = weight_all.ndim == 4
     tokens, depth = content_all.shape
     own = tokens // group
-    pick, width = weight_all.shape[-2:]
+    pick, width = weight_all.shape[-2], weight_all.shape[-1] // 4
     parts = depth // pick
     head_size = head_bias.shape[-1]
     half = length // 2
@@ -867,54 +948,54 @@
         jax.ShapeDtypeStruct((own, depth), float32),
         jax.ShapeDtypeStruct((8, width), float32),
     ]
-    wide_shape = (4, parts // 2, 2, pick, width) if fast else (4, pick, width)
+    wide_shape = weight_all.shape
     scratch = [
         pltpu.VMEM((tokens, depth), bfloat),
         pltpu.VMEM((tokens, depth), bfloat),
         pltpu.VMEM(weight_all.shape, bfloat),
-        pltpu.VMEM((2, tokens, width), bfloat),
+        pltpu.VMEM((tokens, 2 * width), bfloat),
         pltpu.VMEM((2, tokens, depth), bfloat),
-        pltpu.VMEM((4, width, depth), float32),
+        pltpu.VMEM((4 * width, depth), float32),
+        pltpu.VMEM(chance_all.shape, bfloat),
         pltpu.VMEM((length, width), bfloat),
-        pltpu.VMEM((length, width), bfloat),
-        pltpu.VMEM((2, 2, half, half), float32),
         pltpu.VMEM((width, length), float32),
         pltpu.VMEM((length, 4 * width), bfloat),
         pltpu.VMEM((width, length), float32),
         pltpu.VMEM((width, length), float32),
         pltpu.VMEM(wide_shape, bfloat),
+        pltpu.VMEM((2, 2 * own, depth), bfloat),
         pltpu.VMEM((2, own, depth), bfloat),
-        pltpu.VMEM((2, own, depth), bfloat),
-        pltpu.VMEM((2, own, depth), bfloat),
+        pltpu.VMEM((2, half // 2, depth), bfloat),
         pltpu.VMEM((2, own, depth), float32),
         pltpu.VMEM((8, width), float32),
-        pltpu.SemaphoreType.DMA((8,)),
-        pltpu.SemaphoreType.DMA((64,)),
-        pltpu.SemaphoreType.DMA((64,)),
+        pltpu.SemaphoreType.DMA((11,)),
+        pltpu.SemaphoreType.DMA((80,)),
+        pltpu.SemaphoreType.DMA((80,)),
     ]
     if fast:
         planes = parts // 2
         columns = [gradient.shape[-1] for gradient in gradients]
         out_shape += [jax.ShapeDtypeStruct((pick, c), float32) for c in columns]
         out_shape += [
-            jax.ShapeDtypeStruct((4, pick, width), float32),
+            jax.ShapeDtypeStruct((pick, 4 * width), float32),
             jax.ShapeDtypeStruct(small.shape, float32),
             jax.ShapeDtypeStruct((8, 128), float32),
         ]
         gradients = [g.reshape(planes, 2, group // 2, pick, g.shape[-1]) for g in gradients]
-        for c in columns:
+        sizes = [(pick // 2, columns[0])] * 2 + [(pick // 2, columns[1])] * 2 + [(pick, columns[2])]
+        for size in sizes:
             scratch += [
-                pltpu.VMEM((planes, 2, pick, c), bfloat),
-                pltpu.VMEM((planes, 2, pick, c), bfloat),
-                pltpu.VMEM((planes, pick, c), bfloat),
-                pltpu.VMEM((planes - 1, pick, c), bfloat),
+                pltpu.VMEM((planes, 2) + size, bfloat),
+                pltpu.VMEM((planes, 2) + size, bfloat),
+                pltpu.VMEM((planes,) + size, bfloat),
+                pltpu.VMEM((planes - 1,) + size, bfloat),
             ]
         scratch += [
             pltpu.VMEM((group,) + small.shape, float32),
             pltpu.VMEM((parts,) + small.shape, float32),
             pltpu.VMEM(small.shape, float32),
-            pltpu.VMEM((4, planes, pick, width), bfloat),
-            pltpu.VMEM((planes - 1, 4, pick, width), bfloat),
+            pltpu.VMEM((planes, pick, 4 * width), bfloat),
+            pltpu.VMEM((planes - 1, pick, 4 * width), bfloat),
             pltpu.VMEM((parts, 8, width), float32),
             pltpu.VMEM((8, 128), float32),
             pltpu.VMEM((group, 8, 128), float32),
@@ -924,7 +1005,7 @@
         out_shape += [jax.ShapeDtypeStruct(wide_shape, bfloat)]
     return pl.pallas_call(
         functools.partial(attention_backward_kernel, head_size, group, parts, fast),
-        in_specs=[outside] * (group + 4) + [inside] * 7 + [outside] * 3 + [inside],
+        in_specs=[outside] * 6 + [inside] * 5 + [outside] * 3 + [inside],
         out_specs=[inside] * len(out_shape),
         out_shape=out_shape,
         scratch_shapes=scratch,
@@ -932,8 +1013,8 @@
             vmem_limit_bytes=VMEM_LIMIT, collective_id=2, has_side_effects=True
         ),
     )(
-        content_all, query_all, weight_all, *upper_pieces, dresid, *tables,
-        head_bias.reshape(5, width), *facts, proj, logsum, *gradients, small,
+        content_all, query_all, weight_all, chance_all, upper, dresid, table,
+        head_bias, *facts, proj, *gradients, small,
     )
 
 
@@ -955,11 +1036,11 @@
 
 
 def feed_kernel(group, *refs):
-    mixed_pieces, refs = refs[:group], refs[group:]
+    mixed_ref, refs = refs[0], refs[1:]
     bias_ref, refs = refs[0], refs[1:]
     content_ref, query_ref, dcontent_ref, dquery_ref, norm_ref, up_hbm, down_hbm, out_hbm = refs[:8]
     content_out, query_out, dresid_ref, refs = refs[8], refs[9], refs[10], refs[11:]
-    dmixed_pieces, refs = refs[:group], refs[group:]
+    dmixed_ref, refs = refs[0], refs[1:]
     dup_hbm, ddown_hbm, dout_ref, dsmall_ref, refs = refs[0], refs[1], refs[2], refs[3], refs[4:]
     up_ref, down_ref, out_ref, hidden_ref, slope_ref = refs[:5]
     low_ref, low_t_ref, normed_ref, total_ref, up_got, down_got, out_got, out_sent = refs[5:13]
@@ -987,12 +1068,16 @@
         load.wait()
     hidden = up_ref.shape[-1]
 
+    def mixed_piece(k):
+        both = mixed_ref[k]
+        return jnp.concatenate([both[:, : both.shape[1] // 2], both[:, both.shape[1] // 2 :]], 0)
+
     def out_block(k):
         return out_ref[here ^ k].reshape(depth, out_ref.shape[-1])
 
     total = jnp.concatenate([content_ref[...], query_ref[...]], 0).astype(jnp.float32)
     for k in range(group):
-        total = total + dot_nt(mixed_pieces[k][...].reshape(tokens, -1), out_block(k))
+        total = total + dot_nt(mixed_piece(k), out_block(k))
     normed, inverse_one = norm_parts(total)
     normed_ref[...] = normed
     middle = normed * gain_one + bias_one
@@ -1101,16 +1186,15 @@
     ]
     for chip in range(chips):
         k = 2 * chip + 1
-        mixed = mixed_pieces[k][...].reshape(tokens, -1)
+        mixed = mixed_piece(k)
         out_sent[chip] = dot(dlow_t, mixed).astype(jnp.bfloat16).reshape(out_sent.shape[1:])
         out_copies[chip].start()
     for k in range(group):
-        dmixed_pieces[k][...] = (
-            dot(dlow, out_block(k)).astype(jnp.bfloat16).reshape(dmixed_pieces[k].shape)
-        )
+        dmixed = dot(dlow, out_block(k)).astype(jnp.bfloat16)
+        dmixed_ref[k] = jnp.concatenate([dmixed[:own], dmixed[own:]], -1)
     for chip in range(chips):
         k = 2 * chip
-        mixed = mixed_pieces[k][...].reshape(tokens, -1)
+        mixed = mixed_piece(k)
         dout = dot(dlow_t, mixed)
         out_copies[chip].wait_recv()
         dout = dout + out_got[chip].astype(jnp.float32).reshape(dout.shape)
@@ -1125,8 +1209,8 @@
             copy.wait()
 
 
-def feed_layer(mixed_pieces, bias_all, content, query, dcontent, dquery, norm_param, up, down, out):
-    group = len(mixed_pieces)
+def feed_layer(mixed, bias_all, content, query, dcontent, dquery, norm_param, up, down, out):
+    group = mixed.shape[0]
     own, depth = content.shape
     parts, _, pick, hidden = up.shape
     width = out.shape[-1]
@@ -1135,15 +1219,15 @@
     tokens = 2 * own
     results = pl.pallas_call(
         functools.partial(feed_kernel, group),
-        in_specs=[inside] * (group + 6) + [outside] * 3,
-        out_specs=[inside, inside, outside] + [inside] * group + [outside, outside, inside, inside],
+        in_specs=[inside] * 7 + [outside] * 3,
+        out_specs=[inside, inside, outside, inside, outside, outside, inside, inside],
         out_shape=[
             jax.ShapeDtypeStruct((own, depth), jnp.bfloat16),
             jax.ShapeDtypeStruct((own, depth), jnp.bfloat16),
             jax.ShapeDtypeStruct((tokens, depth), jnp.float32),
         ]
-        + [jax.ShapeDtypeStruct((2, own, width), jnp.bfloat16)] * group
         + [
+            jax.ShapeDtypeStruct((group, own, 2 * width), jnp.bfloat16),
             jax.ShapeDtypeStruct((parts, group // 2, pick, hidden), jnp.bfloat16),
             jax.ShapeDtypeStruct((parts, group // 2, pick, hidden), jnp.bfloat16),
             jax.ShapeDtypeStruct((parts, group // 2, pick, width), jnp.bfloat16),
@@ -1170,8 +1254,8 @@
         compiler_params=pltpu.CompilerParams(
             vmem_limit_bytes=VMEM_LIMIT, collective_id=1, has_side_effects=True
         ),
-    )(*mixed_pieces, bias_all, content, query, dcontent, dquery, norm_param, up, down, out)
-    return results[0], results[1], results[2].reshape(2, own, depth), results[3 : 3 + group], results[3 + group :]
+    )(mixed, bias_all, content, query, dcontent, dquery, norm_param, up, down, out)
+    return results[0], results[1], results[2].reshape(2, own, depth), results[3], results[4:]
 
 
 def exchange(value, axis, mask):
@@ -1190,8 +1274,8 @@
     return lax.axis_size("dp") <= 8 and pick % 16 == 0
 
 
-def reduce_projection(pieces):
-    return lax.psum_scatter(pieces[0], "dp", scatter_dimension=1, tiled=True).astype(jnp.float32)
+def reduce_projection(full):
+    return lax.psum_scatter(full, "dp", scatter_dimension=0, tiled=True).astype(jnp.float32)
 
 
 def gather_all(own):
@@ -1211,17 +1295,82 @@
     return lax.psum_scatter(mine, "dp", scatter_dimension=0, tiled=True)
 
 
-def adam_step(master, first, second, gradient, factor, decayed):
+def adam_parts(master, first, second, gradient, factor, decayed):
     clipped = gradient * factor
     new_first = BETA_ONE * first + (1.0 - BETA_ONE) * clipped
     new_second = BETA_TWO * second + (1.0 - BETA_TWO) * clipped * clipped
-    first_hat = new_first / (1.0 - BETA_ONE**STEP)
-    second_hat = new_second / (1.0 - BETA_TWO**STEP)
+    first_hat = new_first * (1.0 / (1.0 - BETA_ONE**STEP))
+    second_hat = new_second * (1.0 / (1.0 - BETA_TWO**STEP))
     update = first_hat / (jnp.sqrt(second_hat) + ADAM_EPSILON)
     if decayed:
         update = update + WEIGHT_DECAY * master
-        return (new_first, new_second, master - MATRIX_RATE * update)
-    return (new_first, new_second, master - VECTOR_RATE * update)
+        return new_first, new_second, master - MATRIX_RATE * update
+    return new_first, new_second, master - VECTOR_RATE * update
+
+
+def update_kernel(group, *refs):
+    kept, refs = refs[:4], refs[4:]
+    up_share, down_share, out_share, proj_share, dhead_ref, small_ref, norm_ref, refs = *refs[:7], refs[7:]
+    weights, refs = refs[:21], refs[21:]
+    placed, refs = refs[:4], refs[4:]
+    results, grad_norm, stages, sems = refs[:28], refs[28], refs[29:33], refs[33]
+    loads = [pltpu.make_async_copy(a, b, sems.at[n]) for n, (a, b) in enumerate(zip(kept, stages))]
+    stores = [pltpu.make_async_copy(a, b, sems.at[4 + n]) for n, (a, b) in enumerate(zip(stages, placed))]
+    for copy in loads:
+        copy.start()
+    norm = norm_ref[0:1, 0:1]
+    grad_norm[...] = norm
+    factor = CLIP_NORM / jnp.maximum(norm, CLIP_NORM)
+
+    def put(index, gradient, decayed, place=lambda ref: ref[...], store=None):
+        values = adam_parts(*(place(ref) for ref in weights[3 * index : 3 * index + 3]), gradient, factor, decayed)
+        for ref, value in zip(results[4 * index : 4 * index + 4], (gradient,) + values):
+            if store is None:
+                ref[...] = value
+            else:
+                store(ref, value)
+
+    width = proj_share.shape[1] // 4
+    for kind in range(4):
+        def store(ref, value, kind=kind):
+            ref[kind] = value
+
+        put(0, proj_share[:, kind * width : (kind + 1) * width], True, lambda ref, kind=kind: ref[kind], store)
+    for load, store in zip(loads, stores):
+        load.wait()
+        store.start()
+    put(1, out_share[...].T, True)
+    put(2, up_share[...], True)
+    put(3, down_share[...], True)
+    heads, size = weights[12].shape[1:]
+    for head in range(heads):
+        def store(ref, value, head=head):
+            ref[:, head, :] = value
+
+        put(4, dhead_ref[:5, head * size : (head + 1) * size], False, lambda ref, head=head: ref[:, head, :], store)
+    put(5, small_ref[pl.ds(lax.axis_index("heads"), 1)], False)
+    put(6, small_ref[group : group + 5], False)
+    for store in stores:
+        store.wait()
+
+
+def update_layer(kept, shares, dhead, small_sum, norm_tile, weights):
+    inside = pl.BlockSpec(memory_space=pltpu.VMEM)
+    outside = pl.BlockSpec(memory_space=pl.ANY)
+    up_share, down_share, out_share, proj_share = shares
+    out_shape = [jax.ShapeDtypeStruct(a.shape, a.dtype) for a in kept]
+    for index in range(7):
+        out_shape += [jax.ShapeDtypeStruct(weights[3 * index].shape, jnp.float32)] * 4
+    out_shape.append(jax.ShapeDtypeStruct((1, 1), jnp.float32))
+    results = pl.pallas_call(
+        functools.partial(update_kernel, lax.axis_size("heads")),
+        in_specs=[outside] * 4 + [inside] * 28,
+        out_specs=[outside] * 4 + [inside] * 29,
+        out_shape=out_shape,
+        scratch_shapes=[pltpu.VMEM(a.shape, a.dtype) for a in kept] + [pltpu.SemaphoreType.DMA((8,))],
+        compiler_params=pltpu.CompilerParams(vmem_limit_bytes=VMEM_LIMIT),
+    )(*kept, up_share, down_share, out_share, proj_share, dhead, small_sum, norm_tile, *weights)
+    return results[:4], results[4:32], results[32]
 
 
 def local(
@@ -1267,83 +1416,43 @@
         up_full, down_full, out_full,
     )
     backward = attention_backward(
-        kept, tables, head_bias, dmixed_pieces, dresid, (dup, ddown, dout), dsmall
+        kept, tables[1], head_bias, dmixed_pieces, dresid, (dup, ddown, dout), dsmall
     )
-    heads_count, head_index = lax.axis_size("heads"), lax.axis_index("heads")
+    input_grad = backward[:2]
     if by_pieces(attn_proj.shape[1]):
-        input_grad, dhead = backward[:2], backward[2]
+        dhead = backward[2]
         up_share, down_share, out_share, proj_share, small_sum, norm_tile = backward[3:]
-        grad_norm = norm_tile[0, 0]
     else:
-        input_grad, dhead = backward[:2], total_over(backward[2], "dp")
-        proj_share = reduce_projection([backward[3]])
+        dp_count, heads_count = lax.axis_size("dp"), lax.axis_size("heads")
+        dhead = total_over(backward[2], "dp")
+        proj_share = reduce_projection(backward[3])
         up_share, down_share, out_share = scatter_all(dup), scatter_all(ddown), scatter_all(dout)
         small_sum = total_over(total_over(dsmall, "heads"), "dp")
         squares = sum(jnp.sum(share * share) for share in (up_share, down_share, out_share, proj_share))
-        squares = squares + jnp.sum(dhead * dhead) / lax.axis_size("dp")
-        squares = squares + jnp.sum(small_sum * small_sum) / (lax.axis_size("dp") * heads_count)
-        grad_norm = jnp.sqrt(total_over(total_over(squares.reshape(1, 1), "heads"), "dp"))[0, 0]
-    down_share, out_share = down_share.T, out_share.T
-    head_grad = dhead[:5].reshape(head_bias.shape)
-    bias_sum, norm_sum = small_sum[:heads_count], small_sum[heads_count : heads_count + 5]
-    bias_grad = lax.dynamic_slice_in_dim(bias_sum, head_index, 1, 0)[0]
-    factor = CLIP_NORM / jnp.maximum(grad_norm, CLIP_NORM)
-    attn_first, attn_second, attn_new = adam_step(
-        attn_proj, attn_proj_first, attn_proj_second, proj_share, factor, True
+        squares = squares + jnp.sum(dhead * dhead) / dp_count
+        squares = squares + jnp.sum(small_sum * small_sum) / (dp_count * heads_count)
+        norm = jnp.sqrt(total_over(total_over(squares.reshape(1, 1), "heads"), "dp"))
+        norm_tile = jnp.broadcast_to(norm, (8, 128))
+    moments = (
+        (attn_proj, attn_proj_first, attn_proj_second),
+        (out_proj, out_proj_first, out_proj_second),
+        (up_proj, up_proj_first, up_proj_second),
+        (down_proj.T, down_proj_first.T, down_proj_second.T),
+        (head_bias, head_bias_first, head_bias_second),
+        (up_bias[None], up_bias_first[None], up_bias_second[None]),
+        (norm_param, norm_param_first, norm_param_second),
     )
-    out_first, out_second, out_new = adam_step(
-        out_proj, out_proj_first, out_proj_second, out_share, factor, True
+    placed, updated, grad_norm = update_layer(
+        (content_out, query_out) + tuple(input_grad),
+        (up_share, down_share, out_share, proj_share),
+        dhead, small_sum, norm_tile, [array for group in moments for array in group],
     )
-    up_first, up_second, up_new = adam_step(
-        up_proj, up_proj_first, up_proj_second, up_share, factor, True
-    )
-    down_first, down_second, down_new = adam_step(
-        down_proj, down_proj_first, down_proj_second, down_share, factor, True
-    )
-    head_first, head_second, head_new = adam_step(
-        head_bias, head_bias_first, head_bias_second, head_grad, factor, False
-    )
-    bias_first, bias_second, bias_new = adam_step(
-        up_bias, up_bias_first, up_bias_second, bias_grad, factor, False
-    )
-    norm_first, norm_second, norm_new = adam_step(
-        norm_param, norm_param_first, norm_param_second, norm_sum, factor, False
-    )
-    return (
-        content_out,
-        query_out,
-        input_grad[0],
-        input_grad[1],
-        grad_norm,
-        proj_share,
-        attn_first,
-        attn_second,
-        attn_new,
-        out_share,
-        out_first,
-        out_second,
-        out_new,
-        up_share,
-        up_first,
-        up_second,
-        up_new,
-        down_share,
-        down_first,
-        down_second,
-        down_new,
-        head_grad,
-        head_first,
-        head_second,
-        head_new,
-        bias_grad,
-        bias_first,
-        bias_second,
-        bias_new,
-        norm_sum,
-        norm_first,
-        norm_second,
-        norm_new,
-    )
+    updated = list(updated)
+    for index in range(12, 16):
+        updated[index] = updated[index].T
+    for index in range(20, 24):
+        updated[index] = updated[index].reshape(-1)
+    return (*placed, grad_norm[0, 0], *updated)
 
 
 def solution(mesh):

time: 333 us -> 276 us (0.83); the launches traced: 335 us -> 273 us
  Pallas kernels: 307 us -> 264 us
  local copies, waits for them, and re-layouts: 17.8 us -> 2.44 us
    pallas_call x1, Pallas kernels: 120 us -> 95.3 us  [attention_forward(): pl.pallas_call(functools.partial(attention_forward_kernel, head_size, gro...]
    pallas_call x1, Pallas kernels: 142 us -> 118 us  [attention_backward(): pl.pallas_call(functools.partial(attention_backward_kernel, head_size, gr...]
    unnamed x71 -> x4, local copies, waits for them, and re-layouts: 12.3 us -> 0.01 us
    sub x7 -> x0, other arithmetic: 8.32 us -> none  [the longest x4 5.6 us: adam_step(): return (new_first, new_second, master - MATRIX_RATE * update)]
    pallas_call x0 -> x1, Pallas kernels: none -> 7.49 us  [update_layer(): pl.pallas_call(functools.partial(update_kernel, lax.axis_size('heads')),...]
    pallas_call x0 -> x4, other arithmetic: none -> 5.13 us  [update_layer(): pl.pallas_call(functools.partial(update_kernel, lax.axis_size('heads')),...]
where the time goes in v5:
time: 276 us; the launch traced here: 273 us
  Pallas kernels  264 us (96%)
  other arithmetic  5.13 us (2%)
    pallas_call x1, Pallas kernels, attention_backward(): pl.pallas_call(functools.partial(attention_backward_kernel, head_size, gr...  118 us
    pallas_call x1, Pallas kernels, attention_forward(): pl.pallas_call(functools.partial(attention_forward_kernel, head_size, gro...  95.3 us
    pallas_call x1, Pallas kernels, feed_layer(): pl.pallas_call(functools.partial(feed_kernel, group), in_specs=[inside] *...  43.9 us
    pallas_call x1, Pallas kernels, update_layer(): pl.pallas_call(functools.partial(update_kernel, lax.axis_size('heads')),...  7.49 us

profile of v5, /device:TPU:0, one launch (start us, length us, event | category | flops | bytes accessed | tf_op | source)
XLA Modules:
  0.0 272.9 jit_solution(4730725373902919506)
XLA Ops:
  0.7 1.3 broadcast_in_dim.10.refs_6_.refs_26_
  1.9 95.3 %shard_map.541 = (bf16[3,512,768]{2,1,0:T(8,128)(2,1)}, f32[3,8,512]{2,1,0:T(8,128)}, f32[3,512,8]{2,1,0:T(8,128)}, f32[4,1,768]{2,1,0:T(1,128)}, bf16[4,384,384...) custom-call(bf16[384,768]{1,0:T(8,128)(2,1)} %refs_2_.3, ...), custom_call_target="tpu_custom_call" | custom-call | tf_op jit(solution)/shard_map/pallas_call | solution.py:568
  97.3 43.9 %shard_map.542 = (bf16[384,768]{1,0:T(8,128)(2,1)}, bf16[384,768]{1,0:T(8,128)(2,1)}, f32[768,768]{1,0:T(8,128)}, bf16[4,384,384]{2,1,0:T(8,128)(2,1)}, bf16[8,2...) custom-call(bf16[4,384,384]{2,1,0:T(8,128)(2,1)} %get-tuple-element., ...), custom_call_target="tpu_custom_call" | custom-call | tf_op jit(solution)/shard_map/pallas_call | solution.py:1220
  141.2 0.0 copy-start
  141.2 0.0 copy-start.1
  141.2 117.7 %shard_map.543 = (f32[384,768]{1,0:T(8,128)}, f32[384,768]{1,0:T(8,128)}, f32[8,192]{1,0:T(8,128)}, f32[96,768]{1,0:T(8,128)}, f32[96,768]{1,0:T(8,128)}, /*inde...) custom-call(bf16[1536,768]{1,0:T(8,128)(2,1)} %get-tuple-element.102.refs_0_, ...), custom_call_target="tpu_custom_call" | custom-call | tf_op jit(solution)/shard_map/pallas_call | solution.py:1006
  258.9 0.0 copy-done
  258.9 0.6 broadcast_in_dim.11.refs_27_
  259.5 0.0 copy-done.1
  259.5 0.6 broadcast_in_dim.12.refs_28_
  260.1 7.5 %shard_map.544 = (bf16[384,768]{1,0:T(8,128)(2,1)}, bf16[384,768]{1,0:T(8,128)(2,1)}, f32[384,768]{1,0:T(8,128)}, f32[384,768]{1,0:T(8,128)}, f32[4,96,192]{2,1,...) custom-call(bf16[384,768]{1,0:T(8,128)(2,1)} %get-tuple-element.100., ...), custom_call_target="tpu_custom_call" | custom-call | tf_op jit(solution)/shard_map/pallas_call | solution.py:1365
  267.6 1.3 reduce
  268.8 1.3 reduce.1
  270.1 1.3 reduce.2
  271.4 1.3 reduce.3
Async XLA Ops:
  141.2 117.7 %copy-start = (f32[768]{0:T(1024)S(1)}, f32[768]{0:T(1024)}, u32[]{:S(2)}) copy-start(f32[768]{0:T(1024)} %param.53) | copy-start | bytes 9220
  141.2 118.3 %copy-start.1 = (f32[768]{0:T(1024)S(1)}, f32[768]{0:T(1024)}, u32[]{:S(2)}) copy-start(f32[768]{0:T(1024)} %param.54) | copy-start | bytes 9220

commit v6 on v5

--- a/solution.py
+++ b/solution.py
@@ -650,6 +650,7 @@
         up_one, up_two, down_one, down_two, out_one = scatters
         small_got, small_more, small_mid, dweight_got, dweight_more, head_got, tile_ref, tile_got, tile_more = refs[20:]
         up_one.begin()
+        out_one.begin()
         small_first = [links.push(small_ref, small_got.at[heads_here], "heads", k) for k in range(1, group)]
         for copy in small_first:
             copy.start()
@@ -726,17 +727,15 @@
     }
     if fast:
         for place, actions in {
-            (0, 0): [up_two.begin],
             (0, 1): [down_two.begin],
-            (0, 2): [up_one.second, down_one.begin],
-            (0, heads): [out_one.begin],
-            (1, 0): [small_middle, up_two.second, up_one.third],
-            (1, 1): [down_two.second],
-            (1, 2): [up_two.third, down_one.second],
-            (1, heads): [out_one.second],
+            (0, 2): [up_two.begin],
+            (0, heads): [up_one.second, out_one.second],
+            (1, 0): [small_middle],
+            (1, 1): [down_two.second, up_one.third],
+            (1, 2): [up_two.second, down_one.begin, out_one.third],
             (2, 0): [down_two.third],
-            (2, 1): [down_one.third],
-            (2, 2): [out_one.third],
+            (2, 1): [up_two.third],
+            (2, 2): [down_one.second],
         }.items():
             events[place] = events.get(place, []) + actions
 
@@ -856,6 +855,7 @@
     across[1][0].start()
     add_side(own_side_two)
     if fast:
+        down_one.third()
         dweight_first.wait()
         add_planes(dweight_got, lambda z: dwide_ref[z, place_y], dweight_got)
         dweight_second = [
@@ -1348,7 +1348,13 @@
             ref[:, head, :] = value
 
         put(4, dhead_ref[:5, head * size : (head + 1) * size], False, lambda ref, head=head: ref[:, head, :], store)
-    put(5, small_ref[pl.ds(lax.axis_index("heads"), 1)], False)
+    def as_row(ref):
+        return ref[...].reshape(1, ref.shape[0])
+
+    def from_row(ref, value):
+        ref[...] = value.reshape(ref.shape)
+
+    put(5, small_ref[pl.ds(lax.axis_index("heads"), 1)], False, as_row, from_row)
     put(6, small_ref[group : group + 5], False)
     for store in stores:
         store.wait()
@@ -1439,7 +1445,7 @@
         (up_proj, up_proj_first, up_proj_second),
         (down_proj.T, down_proj_first.T, down_proj_second.T),
         (head_bias, head_bias_first, head_bias_second),
-        (up_bias[None], up_bias_first[None], up_bias_second[None]),
+        (up_bias, up_bias_first, up_bias_second),
         (norm_param, norm_param_first, norm_param_second),
     )
     placed, updated, grad_norm = update_layer(
@@ -1450,8 +1456,6 @@
     updated = list(updated)
     for index in range(12, 16):
         updated[index] = updated[index].T
-    for index in range(20, 24):
-        updated[index] = updated[index].reshape(-1)
     return (*placed, grad_norm[0, 0], *updated)
 
 

time: 276 us -> 264 us (0.957)
  Pallas kernels: 264 us -> 258 us
  other arithmetic: 5.13 us -> 0 us
    pallas_call x1, Pallas kernels: 118 us -> 112 us  [attention_backward(): pl.pallas_call(functools.partial(attention_backward_kernel, head_size, gr...]
    pallas_call x4 -> x0, other arithmetic: 5.13 us -> none  [update_layer(): pl.pallas_call(functools.partial(update_kernel, lax.axis_size('heads')),...]
where the time goes in v6:
time: 264 us; the launch traced here: 261 us
  Pallas kernels  258 us (98%)
    pallas_call x1, Pallas kernels, attention_backward(): pl.pallas_call(functools.partial(attention_backward_kernel, head_size, gr...  112 us
    pallas_call x1, Pallas kernels, attention_forward(): pl.pallas_call(functools.partial(attention_forward_kernel, head_size, gro...  95.3 us
    pallas_call x1, Pallas kernels, feed_layer(): pl.pallas_call(functools.partial(feed_kernel, group), in_specs=[inside] *...  43.9 us
    pallas_call x1, Pallas kernels, update_layer(): pl.pallas_call(functools.partial(update_kernel, lax.axis_size('heads')),...  7.66 us

profile of v6, /device:TPU:0, one launch (start us, length us, event | category | flops | bytes accessed | tf_op | source)
XLA Modules:
  0.0 260.7 jit_solution(18405693633877575974)
XLA Ops:
  0.7 1.3 broadcast_in_dim.3.refs_6_
  1.9 95.3 %shard_map.541 = (bf16[3,512,768]{2,1,0:T(8,128)(2,1)}, f32[3,8,512]{2,1,0:T(8,128)}, f32[3,512,8]{2,1,0:T(8,128)}, f32[4,1,768]{2,1,0:T(1,128)}, bf16[4,384,384...) custom-call(bf16[384,768]{1,0:T(8,128)(2,1)} %refs_2_.3, ...), custom_call_target="tpu_custom_call" | custom-call | tf_op jit(solution)/shard_map/pallas_call | solution.py:568
  97.3 43.9 %shard_map.542 = (bf16[384,768]{1,0:T(8,128)(2,1)}, bf16[384,768]{1,0:T(8,128)(2,1)}, f32[768,768]{1,0:T(8,128)}, bf16[4,384,384]{2,1,0:T(8,128)(2,1)}, bf16[8,2...) custom-call(bf16[4,384,384]{2,1,0:T(8,128)(2,1)} %get-tuple-element., ...), custom_call_target="tpu_custom_call" | custom-call | tf_op jit(solution)/shard_map/pallas_call | solution.py:1220
  141.1 111.6 %shard_map.543 = (f32[384,768]{1,0:T(8,128)}, f32[384,768]{1,0:T(8,128)}, f32[8,192]{1,0:T(8,128)}, f32[96,768]{1,0:T(8,128)}, f32[96,768]{1,0:T(8,128)}, /*inde...) custom-call(bf16[1536,768]{1,0:T(8,128)(2,1)} %get-tuple-element.102.refs_0_, ...), custom_call_target="tpu_custom_call" | custom-call | tf_op jit(solution)/shard_map/pallas_call | solution.py:1006
  252.8 7.7 %shard_map.544 = (bf16[384,768]{1,0:T(8,128)(2,1)}, bf16[384,768]{1,0:T(8,128)(2,1)}, f32[384,768]{1,0:T(8,128)}, f32[384,768]{1,0:T(8,128)}, f32[4,96,192]{2,1,...) custom-call(bf16[384,768]{1,0:T(8,128)(2,1)} %get-tuple-element.100., ...), custom_call_target="tpu_custom_call" | custom-call | tf_op jit(solution)/shard_map/pallas_call | solution.py:1371

commit v7 on v6

--- a/solution.py
+++ b/solution.py
@@ -616,13 +616,20 @@
         pltpu.make_async_copy(content_hbm, content_all, sems.at[0]),
         pltpu.make_async_copy(query_hbm, query_all, sems.at[1]),
         pltpu.make_async_copy(weight_hbm, weight_ref, sems.at[2]),
-        pltpu.make_async_copy(chance_hbm, chance_ref, sems.at[10]),
         pltpu.make_async_copy(upper_pieces.at[0], upper_all.at[token_part(0)], sems.at[3]),
     ]
     for copy in copies:
         copy.start()
+    def row_at(step):
+        row = jnp.where(step == 0, 0, rows - step)
+        return jnp.where(chip == 0, row, rows - 1 - row)
+
+    def chance_copy(row):
+        return pltpu.make_async_copy(chance_hbm.at[row], chance_ref.at[row], sems.at[10 + row])
+
+    for step in range(rows):
+        chance_copy(row_at(step)).start()
     dresid_copy = pltpu.make_async_copy(dresid_hbm, dresid_ref, sems.at[4])
-    dresid_copy.start()
 
     def weight(first, last):
         return weight_ref[..., first * width : last * width].reshape(depth, (last - first) * width)
@@ -740,11 +747,12 @@
             events[place] = events.get(place, []) + actions
 
     def one_row(step, carry):
-        row = jnp.where(step == 0, 0, rows - step)
-        row = jnp.where(chip == 0, row, rows - 1 - row)
+        row = row_at(step)
+        chance_copy(row).wait()
 
         @pl.when(step == 1)
         def _():
+            dresid_copy.start()
             for copy in upper_copies[1:]:
                 copy.wait()
 
@@ -968,7 +976,7 @@
         pltpu.VMEM((2, half // 2, depth), bfloat),
         pltpu.VMEM((2, own, depth), float32),
         pltpu.VMEM((8, width), float32),
-        pltpu.SemaphoreType.DMA((11,)),
+        pltpu.SemaphoreType.DMA((10 + rows,)),
         pltpu.SemaphoreType.DMA((80,)),
         pltpu.SemaphoreType.DMA((80,)),
     ]
@@ -1084,10 +1092,10 @@
     low_ref[...] = middle.astype(jnp.bfloat16)
     low_t_ref[...] = low_ref[...].T
     total_ref[...] = middle + bias_out
-    for load in loads[group:]:
-        load.wait()
 
     def forward(j, carry):
+        pltpu.make_async_copy(up_hbm.at[:, j], up_ref.at[j], sems.at[group + j]).wait()
+        pltpu.make_async_copy(down_hbm.at[:, j], down_ref.at[j], sems.at[2 * group + j]).wait()
         for part in (slice(0, own), slice(own, tokens)):
             before = dot(low_ref[part], up_ref[j].reshape(depth, hidden)) + bias_ref[j]
             square = before * before

time: 264 us -> 264 us (level)
  no operation moved by 1% of the time
where the time goes in v7:
time: 264 us; the launch traced here: 260 us
  Pallas kernels  258 us (98%)
    pallas_call x1, Pallas kernels, attention_backward(): pl.pallas_call(functools.partial(attention_backward_kernel, head_size, gr...  112 us
    pallas_call x1, Pallas kernels, attention_forward(): pl.pallas_call(functools.partial(attention_forward_kernel, head_size, gro...  95.3 us
    pallas_call x1, Pallas kernels, feed_layer(): pl.pallas_call(functools.partial(feed_kernel, group), in_specs=[inside] *...  43.3 us
    pallas_call x1, Pallas kernels, update_layer(): pl.pallas_call(functools.partial(update_kernel, lax.axis_size('heads')),...  7.66 us

profile of v7, /device:TPU:0, one launch (start us, length us, event | category | flops | bytes accessed | tf_op | source)
XLA Modules:
  0.0 260.2 jit_solution(16835367163217760171)
XLA Ops:
  0.7 1.3 broadcast_in_dim.3.refs_6_
  1.9 95.3 %shard_map.541 = (bf16[3,512,768]{2,1,0:T(8,128)(2,1)}, f32[3,8,512]{2,1,0:T(8,128)}, f32[3,512,8]{2,1,0:T(8,128)}, f32[4,1,768]{2,1,0:T(1,128)}, bf16[4,384,384...) custom-call(bf16[384,768]{1,0:T(8,128)(2,1)} %refs_2_.3, ...), custom_call_target="tpu_custom_call" | custom-call | tf_op jit(solution)/shard_map/pallas_call | solution.py:568
  97.3 43.3 %shard_map.542 = (bf16[384,768]{1,0:T(8,128)(2,1)}, bf16[384,768]{1,0:T(8,128)(2,1)}, f32[768,768]{1,0:T(8,128)}, bf16[4,384,384]{2,1,0:T(8,128)(2,1)}, bf16[8,2...) custom-call(bf16[4,384,384]{2,1,0:T(8,128)(2,1)} %get-tuple-element., ...), custom_call_target="tpu_custom_call" | custom-call | tf_op jit(solution)/shard_map/pallas_call | solution.py:1228
  140.6 111.7 %shard_map.543 = (f32[384,768]{1,0:T(8,128)}, f32[384,768]{1,0:T(8,128)}, f32[8,192]{1,0:T(8,128)}, f32[96,768]{1,0:T(8,128)}, f32[96,768]{1,0:T(8,128)}, /*inde...) custom-call(bf16[1536,768]{1,0:T(8,128)(2,1)} %get-tuple-element.102.refs_0_, ...), custom_call_target="tpu_custom_call" | custom-call | tf_op jit(solution)/shard_map/pallas_call | solution.py:1014
  252.3 7.7 %shard_map.544 = (bf16[384,768]{1,0:T(8,128)(2,1)}, bf16[384,768]{1,0:T(8,128)(2,1)}, f32[384,768]{1,0:T(8,128)}, f32[384,768]{1,0:T(8,128)}, f32[4,96,192]{2,1,...) custom-call(bf16[384,768]{1,0:T(8,128)(2,1)} %get-tuple-element.100., ...), custom_call_target="tpu_custom_call" | custom-call | tf_op jit(solution)/shard_map/pallas_call | solution.py:1379
